TPU v7x, 32 devices: a whole 2x2x4 slice. The times are simulated.
32 devices in a mesh: shot: 2 (over y), gx: 4 (over z), gy: 4 (over x, core).
Axes of the slice: x: 2, y: 2, z: 4, core: 2. Of those that a mesh axis runs over, the one named last changes fastest.
Arguments:
- vel_coef: float32 [128, 128, 128], P('gx', 'gy'), may hold values from 0.03 to 0.2
- src_prev: float32 [2, 128, 128, 128], P('shot', 'gx', 'gy'), may hold values from -6 to 6
- src_cur: float32 [2, 128, 128, 128], P('shot', 'gx', 'gy'), may hold values from -6 to 6
- rcv_prev: float32 [2, 128, 128, 128], P('shot', 'gx', 'gy'), may hold values from -6 to 6
- rcv_cur: float32 [2, 128, 128, 128], P('shot', 'gx', 'gy'), may hold values from -6 to 6
- src_pos: int32 [2], P('shot'), may hold values from 0 to 2097151
- src_amp: float32 [2, 3], P('shot'), may hold values from -24 to 24
- rcv_pos: int32 [2, 512], P('shot'), may hold values from 0 to 2097151
- rcv_data: float32 [2, 3, 512], P('shot'), may hold values from -6 to 6
- aperture: int32 [2, 8], P('shot'), may hold values from 0 to 15, as said below
- owner: int32 [16, 16], replicated, may hold values from 0 to 15, as said below
Outputs:
- src_next: float32 [2, 128, 128, 128], P('shot', 'gx', 'gy')
- rcv_next: float32 [2, 128, 128, 128], P('shot', 'gx', 'gy')
- gathers: float32 [16, 16, 16, 2, 32, 128], P(('gx', 'gy'), 'shot')
Inputs may be any that keep to these rules, and one draw needn't show every extreme that they name: `aperture`: each row lists 8 different tiles. `owner`: each row and each column holds every tile number once.
All inputs are finite; a program needn't handle non-finite values.
Results may differ from a plain program's by a relative error of at most 0.0003.
Values sent between devices are 32-bit elements; how exact they have to be, the bound alone decides.
No kernel may reach another device: no remote copies, remote signals or barrier semaphores. Data moves between devices by JAX's collectives and lax.ppermute only.
A program may use at most 64 MiB of HBM per device.

v0:
```python
import jax
import jax.numpy as jnp
from jax import lax
from jax.sharding import PartitionSpec as P

OFFS = 16
STEPS = 3
HALF = 8


LAP_CENTER = -2.5
LAP_NEAR = 4.0 / 3.0
LAP_FAR = -1.0 / 12.0


def padded(cells, sides, width):
    for axis, dim in sides:
        count = lax.axis_size(axis)
        ends = count - 1
        head = lax.slice_in_dim(cells, 0, width, axis=dim)
        tail = lax.slice_in_dim(cells, cells.shape[dim] - width, cells.shape[dim], axis=dim)
        cells = jnp.concatenate(
            [
                lax.ppermute(tail, axis, [(i, (i + 1) % count) for i in range(ends)]),
                cells,
                lax.ppermute(head, axis, [((i + 1) % count, i) for i in range(ends)]),
            ],
            axis=dim,
        )
    return cells


def laplacian(widened):
    centre = widened[..., 2:-2, 2:-2, :]
    summed = 3.0 * LAP_CENTER * centre
    summed = summed + LAP_NEAR * (widened[..., 3:-1, 2:-2, :] + widened[..., 1:-3, 2:-2, :])
    summed = summed + LAP_FAR * (widened[..., 4:, 2:-2, :] + widened[..., :-4, 2:-2, :])
    summed = summed + LAP_NEAR * (widened[..., 2:-2, 3:-1, :] + widened[..., 2:-2, 1:-3, :])
    summed = summed + LAP_FAR * (widened[..., 2:-2, 4:, :] + widened[..., 2:-2, :-4, :])
    depth_pad = jnp.pad(centre, [(0, 0)] * (centre.ndim - 1) + [(2, 2)])
    summed = summed + LAP_NEAR * (depth_pad[..., 3:-1] + depth_pad[..., 1:-3])
    summed = summed + LAP_FAR * (depth_pad[..., 4:] + depth_pad[..., :-4])
    return summed


def inject(field_in, positions, values, anchor_x, anchor_y, grid_y, depth_cells):
    ext_x, ext_y = (field_in.shape[0], field_in.shape[1])
    plane_cells = grid_y * depth_cells
    local_x = positions // plane_cells - anchor_x
    local_y = positions // depth_cells % grid_y - anchor_y
    local_z = positions % depth_cells
    inside = (local_x >= 0) & (local_x < ext_x) & (local_y >= 0) & (local_y < ext_y)
    flat_index = jnp.where(
        inside, (local_x * ext_y + local_y) * depth_cells + local_z, ext_x * ext_y * depth_cells
    )
    flat_field = field_in.reshape(-1).at[flat_index].add(values, mode="drop")
    return flat_field.reshape(field_in.shape)


def body(
    vel_coef,
    src_prev,
    src_cur,
    rcv_prev,
    rcv_cur,
    src_pos,
    src_amp,
    rcv_pos,
    rcv_data,
    aperture,
    owner,
):
    width_x, width_y, depth_cells = vel_coef.shape
    tile_count = lax.axis_size("gx") * lax.axis_size("gy")
    grid_y = width_y * lax.axis_size("gy")
    start_x = lax.axis_index("gx") * width_x
    start_y = lax.axis_index("gy") * width_y
    tile_id = lax.axis_index(("gx", "gy"))
    snapshots = []
    previous = jnp.concatenate([src_prev, rcv_prev], 0)
    current = jnp.concatenate([src_cur, rcv_cur], 0)
    for step_index in range(STEPS):
        widened = padded(current, (("gx", 1), ("gy", 2)), 2)
        updated = 2.0 * current - previous + vel_coef * laplacian(widened)
        source_field = inject(
            updated[0], src_pos, src_amp[:, step_index], start_x, start_y, grid_y, depth_cells
        )
        receiver_field = inject(
            updated[1], rcv_pos[0], rcv_data[0, step_index], start_x, start_y, grid_y, depth_cells
        )
        updated = jnp.stack([source_field, receiver_field])
        previous, current = (current, updated)
        snapshots.append(padded(current, (("gx", 1),), HALF))
    in_aperture = jnp.any(aperture[0] == tile_id)

    def correlate():
        offset_rows = []
        for offset_index in range(OFFS):
            lead_start = 2 * HALF - offset_index
            summed = None
            for snapshot in snapshots:
                product_term = (
                    snapshot[0, lead_start : lead_start + width_x]
                    * snapshot[1, offset_index : offset_index + width_x]
                )
                summed = product_term if summed is None else summed + product_term
            offset_rows.append(summed)
        return jnp.stack(offset_rows)

    def nothing_here():
        return jnp.zeros((OFFS, width_x, width_y, depth_cells), jnp.float32)

    partial_image = lax.cond(in_aperture, correlate, nothing_here)
    strip_rows = width_x // tile_count
    strips = partial_image.reshape(OFFS, tile_count, strip_rows, width_y, depth_cells)
    owner_row = lax.dynamic_index_in_dim(owner, tile_id, 0, keepdims=False)
    tile_numbers = jnp.arange(tile_count, dtype=jnp.int32)
    matches = owner_row[:, None] == tile_numbers[None, :]
    strip_for = jnp.sum(jnp.where(matches, tile_numbers[:, None], 0), axis=0)
    outgoing = jnp.take(strips, strip_for, axis=1)
    reduced = lax.psum_scatter(outgoing, "shot", scatter_dimension=0, tiled=True)
    arrived = lax.all_to_all(reduced, ("gx", "gy"), split_axis=1, concat_axis=1, tiled=True)
    return (current[0:1], current[1:2], arrived[None])


def solution(mesh):
    return jax.shard_map(
        body,
        mesh=mesh,
        in_specs=(
            P("gx", "gy", None),
            P("shot", "gx", "gy", None),
            P("shot", "gx", "gy", None),
            P("shot", "gx", "gy", None),
            P("shot", "gx", "gy", None),
            P("shot"),
            P("shot", None),
            P("shot", None),
            P("shot", None, None),
            P("shot", None),
            P(),
        ),
        out_specs=(
            P("shot", "gx", "gy", None),
            P("shot", "gx", "gy", None),
            P(("gx", "gy"), "shot", None, None, None, None),
        ),
        check_vma=False,
    )
```

profile of v0, /device:TPU:11, one launch (start us, length us, event | category | flops | bytes accessed | tf_op | source)
XLA Modules:
  0.0 346.4 jit_solution(3418797452451878014)
XLA Ops:
  11.5 3.2 collective-permute-start.1
  18.2 3.1 collective-permute-start.2
  26.7 2.1 fusion.63
  28.8 3.5 %scatter_fusion = f32[131072]{0:T(1024)S(1)} fusion(f32[131072]{0:T(1024)S(1)} %bitcast.81, s32[512]{0:T(512)S(1)} %bitcast.143, f32[512]{0:T(512)S(1)} %bitcast.148), kind=kCustom, calls=%fused_computation.1 | custom fusion | flops 512 | bytes 8192 | tf_op jit(solution)/shard_map/scatter-add | solution.py:56
  34.5 3.2 collective-permute-start.5
  38.6 3.2 collective-permute-start.12
  43.9 5.6 %collective-permute-start.6 = (f32[2,36,2,128]{3,2,1,0:T(2,128)S(1)}, f32[2,36,2,128]{3,2,1,0:T(2,128)S(1)}, u32[]{:S(2)}, u32[]{:S(2)}) collective-permute-start(f32[2,36,2,128]{3,2,1,0:T(2,128)S(1)} %get-tuple-element.100), channel_id=1, source_target_pairs={{1,0},{2,1},{3,2},{5,4},{6,5},{7,6},{9,8},{10,9},{11,10},{13,12},{... | collective-permute-start | bytes 221192 | tf_op jit(solution)/shard_map/ppermute | solution.py:26
  56.5 3.5 %scatter_fusion.1 = f32[131072]{0:T(1024)S(1)} fusion(f32[131072]{0:T(1024)S(1)} %bitcast.90, s32[512]{0:T(512)S(1)} %bitcast.144, f32[512]{0:T(512)S(1)} %bitcast.147), kind=kCustom, calls=%fused_computation.2 | custom fusion | flops 512 | bytes 8192 | tf_op jit(solution)/shard_map/scatter-add | solution.py:56
  62.0 3.4 collective-permute-start.9
  66.2 3.2 collective-permute-start.14
  69.5 5.3 %collective-permute-start.10 = (f32[2,36,2,128]{3,2,1,0:T(2,128)S(1)}, f32[2,36,2,128]{3,2,1,0:T(2,128)S(1)}, u32[]{:S(2)}, u32[]{:S(2)}) collective-permute-start(f32[2,36,2,128]{3,2,1,0:T(2,128)S(1)} %get-tuple-element.96), channel_id=1, source_target_pairs={{1,0},{2,1},{3,2},{5,4},{6,5},{7,6},{9,8},{10,9},{11,10},{13,12},{... | collective-permute-start | bytes 221192 | tf_op jit(solution)/shard_map/ppermute | solution.py:26
  76.4 2.8 collective-permute-start.15
  80.9 3.5 %scatter_fusion.2 = f32[131072]{0:T(1024)S(1)} fusion(f32[131072]{0:T(1024)S(1)} %bitcast.115, s32[512]{0:T(512)S(1)} %bitcast.145, f32[512]{0:T(512)S(1)} %bitcast.146), kind=kCustom, calls=%fused_computation.3 | custom fusion | flops 512 | bytes 8192 | tf_op jit(solution)/shard_map/scatter-add | solution.py:56
  86.7 2.5 collective-permute-start.16
  89.2 2.8 collective-permute-start.17
  95.0 2.2 collective-permute-done.17
  97.4 16.4 %conditional.1 = (f32[16,16,2,32,128]{4,3,2,1,0:T(8,128)}) conditional(s32[]{:T(128)} %convert_element_type.7, () %tuple.28, (f32[2,48,32,128]{3,2,1,0:T(8,128)S(1)}, f32[2,48,32,128]{3,2,1,0:T(8,128)S(1)}, f32[2,48,32,128]{3,2,1,0:T(8,128)S(1)}, f32[131072]{0:T(1024)S(1)}, f32[131072]{0:T(1024)S(1)}, /*index=5*/f32[131072]{0:T(1024)S(1)}, ...), branch_computations={%region_5.6_spmd, %region_6.7_spmd} | conditional | flops 10485760 | bytes 75497480 | solution.py:113
  113.8 7.7 %gather_fusion = f32[16,16,2,32,128]{4,3,2,1,0:T(8,128)} fusion(f32[16,16,2,32,128]{4,3,2,1,0:T(8,128)} %get-tuple-element.134, s32[1024]{0:T(1024)S(1)} %pad_clamp_fusion), kind=kCustom, calls=%fused_computation | custom fusion | bytes 16777280 | tf_op jit(solution)/shard_map/jit(_take)/gather | solution.py:120
  121.6 4.5 %select_bitcast_fusion = f32[16,16,2,32,128]{4,3,2,0,1:T(8,128)S(1)} fusion(f32[16,16,2,32,128]{4,3,2,1,0:T(8,128)} %gather_fusion, pred[16]{0:T(512)(128)(4,1)S(1)} %compare_and_fusion), kind=kLoop, calls=%fused_computation.37 | loop fusion | flops 2097152 | bytes 16777232 | tf_op jit(solution)/shard_map/jit(_take)/select_n | solution.py:120
  128.0 8.1 %copy.23 = f32[2,8,1024,128]{3,1,2,0:T(8,128)} copy(f32[2,8,1024,128]{3,2,1,0:T(8,128)S(1)} %bitcast.120) | data formatting | bytes 16777216
  136.1 99.6 %reduce-scatter.5.cloned.1.call-done = f32[8,131072]{1,0:T(8,128)} async-done(((f32[16,131072]{1,0:T(8,128)}), f32[8,131072]{1,0:T(8,128)}) %reduce-scatter.5.cloned.1.call-update) | async-done | bytes 4194320
  235.8 2.9 copy.18
  238.7 98.4 %all_to_all.5 = f32[8,16,2,32,128]{4,3,2,0,1:T(8,128)S(1)} all-to-all(f32[8,16,2,32,128]{4,3,2,0,1:T(8,128)S(1)} %copy.18), channel_id=1, replica_groups=mesh['shot'=2,'gx'=4,'gy'=4] {'gx','gy'}, dimensions={1} | all-to-all | bytes 8388608 | tf_op jit(solution)/shard_map/all_to_all | solution.py:122
  337.1 2.5 copy.16
  (109 shorter events, 52.7 us)
Async XLA Ops:
  7.2 8.4 %copy-start.10 = (s32[1,8]{1,0:T(1,128)S(1)}, s32[1,8]{1,0:T(1,128)}, u32[]{:S(2)}) copy-start(s32[1,8]{1,0:T(1,128)} %param.28) | copy-start | bytes 100
  7.2 9.7 %copy-start.9 = (s32[1,512]{1,0:T(1,128)S(1)}, s32[1,512]{1,0:T(1,128)}, u32[]{:S(2)}) copy-start(s32[1,512]{1,0:T(1,128)} %param.26) | copy-start | bytes 6148
  7.2 10.2 %copy-start.8 = (f32[1,3]{1,0:T(1,128)S(1)}, f32[1,3]{1,0:T(1,128)}, u32[]{:S(2)}) copy-start(f32[1,3]{1,0:T(1,128)} %param.25) | copy-start | bytes 40
  7.2 228.5 %reduce-scatter.5.cloned.1.call-start = ((), (), s32[]{:S(2)}) async-start(), calls=%async_computation.2 | async-start | bytes 12582912
  9.4 8.7 %collective-permute-start = (f32[2,2,32,128]{3,2,1,0:T(8,128)S(1)}, f32[2,2,32,128]{3,2,1,0:T(8,128)S(1)}, u32[]{:S(2)}, u32[]{:S(2)}) collective-permute-start(f32[2,2,32,128]{3,2,1,0:T(8,128)S(1)} %get-tuple-element.126), channel_id=1, source_target_pairs={{4,0},{8,4},{12,8},{5,1},{9,5},{13,9},{6,2},{10,6},{14,10},{7,3},{... | collective-permute-start | bytes 196616 | tf_op jit(solution)/shard_map/ppermute | solution.py:26
  11.5 6.6 %collective-permute-start.1 = (f32[2,2,32,128]{3,2,1,0:T(8,128)S(1)}, f32[2,2,32,128]{3,2,1,0:T(8,128)S(1)}, u32[]{:S(2)}, u32[]{:S(2)}) collective-permute-start(f32[2,2,32,128]{3,2,1,0:T(8,128)S(1)} %get-tuple-element.127), channel_id=1, source_target_pairs={{0,4},{4,8},{8,12},{1,5},{5,9},{9,13},{2,6},{6,10},{10,14},{3,7},{... | collective-permute-start | bytes 196616 | tf_op jit(solution)/shard_map/ppermute | solution.py:24
  18.2 4.5 %collective-permute-start.2 = (f32[2,36,2,128]{3,2,1,0:T(2,128)S(1)}, f32[2,36,2,128]{3,2,1,0:T(2,128)S(1)}, u32[]{:S(2)}, u32[]{:S(2)}) collective-permute-start(f32[2,36,2,128]{3,2,1,0:T(2,128)S(1)} %get-tuple-element.104), channel_id=1, source_target_pairs={{1,0},{2,1},{3,2},{5,4},{6,5},{7,6},{9,8},{10,9},{11,10},{13,12},{... | collective-permute-start | bytes 221192 | tf_op jit(solution)/shard_map/ppermute | solution.py:26
  21.3 3.2 collective-permute-start.3
  32.4 11.4 %collective-permute-start.4 = (f32[2,2,32,128]{3,2,1,0:T(8,128)S(1)}, f32[2,2,32,128]{3,2,1,0:T(8,128)S(1)}, u32[]{:S(2)}, u32[]{:S(2)}) collective-permute-start(f32[2,2,32,128]{3,2,1,0:T(8,128)S(1)} %get-tuple-element.123), channel_id=1, source_target_pairs={{4,0},{8,4},{12,8},{5,1},{9,5},{13,9},{6,2},{10,6},{14,10},{7,3},{... | collective-permute-start | bytes 196616 | tf_op jit(solution)/shard_map/ppermute | solution.py:26
  34.5 9.3 %collective-permute-start.5 = (f32[2,2,32,128]{3,2,1,0:T(8,128)S(1)}, f32[2,2,32,128]{3,2,1,0:T(8,128)S(1)}, u32[]{:S(2)}, u32[]{:S(2)}) collective-permute-start(f32[2,2,32,128]{3,2,1,0:T(8,128)S(1)} %get-tuple-element.122), channel_id=1, source_target_pairs={{0,4},{4,8},{8,12},{1,5},{5,9},{9,13},{2,6},{6,10},{10,14},{3,7},{... | collective-permute-start | bytes 196616 | tf_op jit(solution)/shard_map/ppermute | solution.py:24
  38.6 50.6 %collective-permute-start.12 = (f32[2,8,32,128]{3,2,1,0:T(8,128)}, f32[2,8,32,128]{3,2,1,0:T(8,128)S(1)}, u32[]{:S(2)}, u32[]{:S(2)}) collective-permute-start(f32[2,8,32,128]{3,2,1,0:T(8,128)} %get-tuple-element.110), channel_id=1, source_target_pairs={{0,4},{4,8},{8,12},{1,5},{5,9},{9,13},{2,6},{6,10},{10,14},{3,7},{... | collective-permute-start | bytes 786440 | tf_op jit(solution)/shard_map/ppermute | solution.py:24
  41.8 50.2 %collective-permute-start.13 = (f32[2,8,32,128]{3,2,1,0:T(8,128)}, f32[2,8,32,128]{3,2,1,0:T(8,128)}, u32[]{:S(2)}, u32[]{:S(2)}) collective-permute-start(f32[2,8,32,128]{3,2,1,0:T(8,128)} %get-tuple-element.111), channel_id=1, source_target_pairs={{4,0},{8,4},{12,8},{5,1},{9,5},{13,9},{6,2},{10,6},{14,10},{7,3},{... | collective-permute-start | bytes 786440 | tf_op jit(solution)/shard_map/ppermute | solution.py:26
  43.9 7.1 %collective-permute-start.6 = (f32[2,36,2,128]{3,2,1,0:T(2,128)S(1)}, f32[2,36,2,128]{3,2,1,0:T(2,128)S(1)}, u32[]{:S(2)}, u32[]{:S(2)}) collective-permute-start(f32[2,36,2,128]{3,2,1,0:T(2,128)S(1)} %get-tuple-element.100), channel_id=1, source_target_pairs={{1,0},{2,1},{3,2},{5,4},{6,5},{7,6},{9,8},{10,9},{11,10},{13,12},{... | collective-permute-start | bytes 221192 | tf_op jit(solution)/shard_map/ppermute | solution.py:26
  49.5 3.2 collective-permute-start.7
  60.1 9.3 %collective-permute-start.8 = (f32[2,2,32,128]{3,2,1,0:T(8,128)S(1)}, f32[2,2,32,128]{3,2,1,0:T(8,128)S(1)}, u32[]{:S(2)}, u32[]{:S(2)}) collective-permute-start(f32[2,2,32,128]{3,2,1,0:T(8,128)S(1)} %get-tuple-element.117), channel_id=1, source_target_pairs={{4,0},{8,4},{12,8},{5,1},{9,5},{13,9},{6,2},{10,6},{14,10},{7,3},{... | collective-permute-start | bytes 196616 | tf_op jit(solution)/shard_map/ppermute | solution.py:26
  62.0 7.4 %collective-permute-start.9 = (f32[2,2,32,128]{3,2,1,0:T(8,128)S(1)}, f32[2,2,32,128]{3,2,1,0:T(8,128)S(1)}, u32[]{:S(2)}, u32[]{:S(2)}) collective-permute-start(f32[2,2,32,128]{3,2,1,0:T(8,128)S(1)} %get-tuple-element.116), channel_id=1, source_target_pairs={{0,4},{4,8},{8,12},{1,5},{5,9},{9,13},{2,6},{6,10},{10,14},{3,7},{... | collective-permute-start | bytes 196616 | tf_op jit(solution)/shard_map/ppermute | solution.py:24
  66.2 26.8 %collective-permute-start.14 = (f32[2,8,32,128]{3,2,1,0:T(8,128)}, f32[2,8,32,128]{3,2,1,0:T(8,128)}, u32[]{:S(2)}, u32[]{:S(2)}) collective-permute-start(f32[2,8,32,128]{3,2,1,0:T(8,128)} %get-tuple-element.108), channel_id=1, source_target_pairs={{0,4},{4,8},{8,12},{1,5},{5,9},{9,13},{2,6},{6,10},{10,14},{3,7},{... | collective-permute-start | bytes 786440 | tf_op jit(solution)/shard_map/ppermute | solution.py:24
  69.5 6.9 %collective-permute-start.10 = (f32[2,36,2,128]{3,2,1,0:T(2,128)S(1)}, f32[2,36,2,128]{3,2,1,0:T(2,128)S(1)}, u32[]{:S(2)}, u32[]{:S(2)}) collective-permute-start(f32[2,36,2,128]{3,2,1,0:T(2,128)S(1)} %get-tuple-element.96), channel_id=1, source_target_pairs={{1,0},{2,1},{3,2},{5,4},{6,5},{7,6},{9,8},{10,9},{11,10},{13,12},{... | collective-permute-start | bytes 221192 | tf_op jit(solution)/shard_map/ppermute | solution.py:26
  74.8 4.4 %collective-permute-start.11 = (f32[2,36,2,128]{3,2,1,0:T(2,128)S(1)}, f32[2,36,2,128]{3,2,1,0:T(2,128)S(1)}, u32[]{:S(2)}, u32[]{:S(2)}) collective-permute-start(f32[2,36,2,128]{3,2,1,0:T(2,128)S(1)} %get-tuple-element.97), channel_id=1, source_target_pairs={{0,1},{1,2},{2,3},{4,5},{5,6},{6,7},{8,9},{9,10},{10,11},{12,13},{... | collective-permute-start | bytes 221192 | tf_op jit(solution)/shard_map/ppermute | solution.py:24
  76.4 16.7 %collective-permute-start.15 = (f32[2,8,32,128]{3,2,1,0:T(8,128)}, f32[2,8,32,128]{3,2,1,0:T(8,128)}, u32[]{:S(2)}, u32[]{:S(2)}) collective-permute-start(f32[2,8,32,128]{3,2,1,0:T(8,128)} %get-tuple-element.109), channel_id=1, source_target_pairs={{4,0},{8,4},{12,8},{5,1},{9,5},{13,9},{6,2},{10,6},{14,10},{7,3},{... | collective-permute-start | bytes 786440 | tf_op jit(solution)/shard_map/ppermute | solution.py:26
  84.5 12.8 %copy-start.2 = (f32[131072]{0:T(1024)}, f32[131072]{0:T(1024)S(1)}, u32[]{:S(2)}) copy-start(f32[131072]{0:T(1024)S(1)} %scatter_fusion.2) | copy-start | bytes 1572868
  86.6 10.7 %copy-start.3 = (f32[131072]{0:T(1024)}, f32[131072]{0:T(1024)S(1)}, u32[]{:S(2)}) copy-start(f32[131072]{0:T(1024)S(1)} %fusion.65) | copy-start | bytes 1572868
  86.7 8.3 %collective-permute-start.16 = (f32[2,8,32,128]{3,2,1,0:T(8,128)S(1)}, f32[2,8,32,128]{3,2,1,0:T(8,128)S(1)}, u32[]{:S(2)}, u32[]{:S(2)}) collective-permute-start(f32[2,8,32,128]{3,2,1,0:T(8,128)S(1)} %get-tuple-element.106), channel_id=1, source_target_pairs={{0,4},{4,8},{8,12},{1,5},{5,9},{9,13},{2,6},{6,10},{10,14},{3,7},{... | collective-permute-start | bytes 786440 | tf_op jit(solution)/shard_map/ppermute | solution.py:24
  89.2 8.0 %collective-permute-start.17 = (f32[2,8,32,128]{3,2,1,0:T(8,128)S(1)}, f32[2,8,32,128]{3,2,1,0:T(8,128)S(1)}, u32[]{:S(2)}, u32[]{:S(2)}) collective-permute-start(f32[2,8,32,128]{3,2,1,0:T(8,128)S(1)} %get-tuple-element.107), channel_id=1, source_target_pairs={{4,0},{8,4},{12,8},{5,1},{9,5},{13,9},{6,2},{10,6},{14,10},{7,3},{... | collective-permute-start | bytes 786440 | tf_op jit(solution)/shard_map/ppermute | solution.py:26
  (6 other events, 24.8 us)
Sparse Core Ops, SparseCore 0:
  136.3 99.4 reduce-scatter.4
where the time goes:
time: 349 us; the launch traced here: 346 us
  waiting for transfers between devices  106 us (30%)
  blocking collectives  98.4 us (28%)
  starting transfers between devices  50.3 us (14%)
  local copies, waits for them, and re-layouts  39.9 us (11%)
  other arithmetic  35.2 us (10%)
  between operations  16.5 us (5%)
    unnamed x2, waiting for transfers between devices  99.6 us
    all_to_all x1, blocking collectives, body(): lax.all_to_all(reduced, ('gx', 'gy'), split_axis=1, concat_axis=1, tiled=...  98.4 us
    ppermute x9, starting transfers between devices, padded(): lax.ppermute(head, axis, [((i + 1) % count, i) for i in range(ends)])  27.7 us
    ppermute x9, starting transfers between devices, padded(): lax.ppermute(tail, axis, [(i, (i + 1) % count) for i in range(ends)])  22.5 us
    scatter-add x6, other arithmetic, inject(): flat_field = field_in.reshape(-1).at[flat_index].add(values, mode='drop')  17 us
    unnamed x27, local copies, waits for them, and re-layouts  16.6 us
    cond x15, local copies, waits for them, and re-layouts  12.8 us
    gather x1, local copies, waits for them, and re-layouts, body(): outgoing = jnp.take(strips, strip_for, axis=1)  7.74 us
  transfers between devices with their start and end apart: 19, of which 5 were waited for; matrix products, arithmetic and copies ran while one was open for 6% of the time, Pallas kernels for 0%

commit v1 on v0

v1 whole, which is shorter than its diff:
```python
import functools

import jax
import jax.numpy as jnp
from jax import lax
from jax.experimental import pallas as pl
from jax.experimental.pallas import tpu as pltpu
from jax.sharding import PartitionSpec as P

OFFS = 16
STEPS = 3
HALF = 8
PAD = 8
VALID = (6, 4, 2)
CORNER = 6

LAP_CENTER = -2.5
LAP_NEAR = 4.0 / 3.0
LAP_FAR = -1.0 / 12.0

ANY = pl.BlockSpec(memory_space=pl.ANY)
SMEM = pl.BlockSpec(memory_space=pltpu.SMEM)
VMEM = pl.BlockSpec(memory_space=pltpu.VMEM)


def swap_pairs(count):
    first = [(i, i ^ 1) for i in range(count) if (i ^ 1) < count]
    second = []
    for i in range(1, count - 1, 2):
        second += [(i, i + 1), (i + 1, i)]
    return first, second


def largest_block(count, limit):
    return max(n for n in range(1, limit + 1) if count % n == 0)


def run_copies(copies):
    for copy in copies:
        copy.start()
    for copy in copies:
        copy.wait()


def is_upper(axis, swap):
    return lax.rem(lax.axis_index(axis) + swap, 2) == 0


def pick(condition, upper, lower, multiple=1):
    return pl.multiple_of(jnp.where(condition, upper, lower), multiple)


def pack_kernel(vel, src_prev, src_cur, rcv_prev, rcv_cur, x0, x1, y0, y1, sems):
    width_x, width_y, depth = vel.shape
    fields = (src_cur.at[0], rcv_cur.at[0], src_prev.at[0], rcv_prev.at[0], vel)
    copies = []

    def add(src, dst):
        copies.append(pltpu.make_async_copy(src, dst, sems.at[len(copies)]))

    for swap, out in enumerate((y0, y1)):
        start = pick(is_upper("gy", swap), width_y - PAD, 0, PAD)
        for n, field in enumerate(fields):
            add(field.at[:, pl.ds(start, PAD)], out.at[n])
    for swap, out in enumerate((x0, x1)):
        row = 0
        for n, field in enumerate(fields):
            rows = HALF if n < 2 else VALID[0]
            start = pick(is_upper("gx", swap), width_x - rows, 0)
            add(field.at[pl.ds(start, rows)], out.at[pl.ds(row, rows)])
            row += rows
    run_copies(copies)


def corner_kernel(y0, y1, late, c0, c1, sems):
    width_x = y0.shape[1]
    copies = []
    for swap, out in enumerate((c0, c1)):
        start = pick(is_upper("gx", swap), width_x - CORNER, 0)
        for n, halo in enumerate((y0, y1)):
            copies.append(
                pltpu.make_async_copy(halo.at[:, pl.ds(start, CORNER)], out.at[n], sems.at[len(copies)])
            )
    run_copies(copies)


def locate(position, width_x, width_y, depth):
    grid_y = width_y * lax.axis_size("gy")
    x = lax.div(position, grid_y * depth) - lax.axis_index("gx") * width_x
    y = lax.rem(lax.div(position, depth), grid_y) - lax.axis_index("gy") * width_y
    reach = VALID[0]
    inside = (x >= -reach) & (x < width_x + reach) & (y >= -PAD // 2) & (y < width_y + PAD // 2)
    return x, y, lax.rem(position, depth), inside


def spread_kernel(width_x, width_y, positions, values, out):
    rows, depth = out.shape[1], out.shape[2]
    receivers = positions.shape[1]
    x, y, depths, inside = locate(positions[...], width_x, width_y, depth)
    cell_row = jnp.where(inside, (x + VALID[0]) * (width_y + PAD) + y + PAD // 2, -1)
    lanes = lax.broadcasted_iota(jnp.int32, (depth, receivers), 0)
    rest = jnp.concatenate(
        [
            jnp.where(lanes == depths, values[:, t * receivers : (t + 1) * receivers], 0.0)
            for t in range(STEPS)
        ],
        axis=0,
    )
    parts = []
    for _ in range(3):
        parts.append(rest.astype(jnp.bfloat16))
        rest = rest - parts[-1].astype(jnp.float32)
    index = lax.broadcasted_iota(jnp.int32, (rows, receivers), 0)
    hot = jnp.where(index == cell_row, 1.0, 0.0).astype(jnp.bfloat16)
    total = lax.dot_general(
        hot, jnp.concatenate(parts, axis=0), (((1,), (1,)), ((), ())), preferred_element_type=jnp.float32
    )
    for t in range(STEPS):
        high, middle, low = (
            total[:, (n * STEPS + t) * depth : (n * STEPS + t + 1) * depth] for n in range(3)
        )
        out[t] = high + (middle + low)


def depth_matrix(depth):
    row = lax.broadcasted_iota(jnp.int32, (depth, depth), 0)
    col = lax.broadcasted_iota(jnp.int32, (depth, depth), 1)
    apart = jnp.abs(row - col)
    return jnp.where(apart == 1, 16.0, jnp.where(apart == 2, -1.0, 0.0)).astype(jnp.bfloat16)


def depth_neighbours(here, matrix):
    rest = here.reshape(-1, here.shape[-1])
    total = None
    for _ in range(3):
        part = rest.astype(jnp.bfloat16)
        rest = rest - part.astype(jnp.float32)
        term = jnp.dot(part, matrix, preferred_element_type=jnp.float32)
        total = term if total is None else total + term
    return total.reshape(here.shape)


def advance(cur, prev, vel, out, inject, rows, cols, matrix):
    first, count = rows
    col, width = cols
    block = largest_block(count, 22)

    def one(step, carry):
        x = first + step * block
        at = lambda ref, dx, dy: ref[pl.ds(x + dx, block), pl.ds(col + dy, width), :]
        here = at(cur, 0, 0)
        near = at(cur, 1, 0) + at(cur, -1, 0) + at(cur, 0, 1) + at(cur, 0, -1)
        far = at(cur, 2, 0) + at(cur, -2, 0) + at(cur, 0, 2) + at(cur, 0, -2)
        lap = (3.0 * LAP_CENTER) * here + LAP_NEAR * near + LAP_FAR * far
        lap = lap + (1.0 / 12.0) * depth_neighbours(here, matrix)
        new = 2.0 * here - at(prev, 0, 0) + at(vel, 0, 0) * lap
        if inject is not None:
            new = new + inject[pl.ds(x - (PAD - VALID[0]), block), pl.ds(col - PAD // 2, width), :]
        out[pl.ds(x, block), pl.ds(col, width), :] = new
        return carry

    lax.fori_loop(0, count // block, one, 0)


def chunk_shift(i, r):
    shots = lax.axis_size("shot")
    held = OFFS // shots
    keeper = lax.rem(lax.axis_index("shot") + r, shots)
    return HALF - (keeper * held + jnp.where(2 * keeper < shots, held - 1 - i, i))


def read_tables(owner, aperture, strip_for):
    tile = lax.axis_index(("gx", "gy"))
    for k in range(owner.shape[0]):
        strip_for[owner[tile, k]] = k
    active = aperture[0, 0] == tile
    for k in range(1, aperture.shape[1]):
        active = active | (aperture[0, k] == tile)
    return active


def correlate(lead, lag, strip_for, keep, tiles, strip_rows, cols, outs, slot, i):
    shifts = [chunk_shift(i, r) for r in range(len(outs))]

    def one(tile, carry):
        for u in range(strip_rows):
            x = HALF + strip_for[tile] * strip_rows + u
            for r, out in enumerate(outs):
                shift = shifts[r]
                total = None
                for t in range(STEPS):
                    term = lead(t, x + shift, cols) * lag(t, x - shift, cols)
                    total = term if total is None else total + term
                out[tile, slot, u] = jnp.where(keep, total, 0.0)
        return carry

    lax.fori_loop(0, tiles, one, 0)


def front_kernel(
    early, shots, tiles, owner, aperture, src_pos, amps,
    vel, src_prev, src_cur, rcv_prev, rcv_cur, x0, x1, y0, y1, c0, c1, inject_hbm, *rest
):
    count = shots if early else 0
    outs = rest[:count]
    src_next, rcv_next, snaps, edge0, edge1 = rest[count : count + 5]
    ext, s1, s2, s3, inject, strip_for, in_sems, out_sems = rest[count + 5 :]
    width_x, width_y, depth = vel.shape
    inner_y = pl.ds(PAD, width_y)
    copies = []

    def add(src, dst):
        copies.append(pltpu.make_async_copy(src, dst, in_sems.at[len(copies)]))

    for n, field in enumerate((src_cur.at[0], rcv_cur.at[0], src_prev.at[0], rcv_prev.at[0], vel)):
        add(field, ext.at[n, pl.ds(PAD, width_x), inner_y])
    for swap, halo in enumerate((y0, y1)):
        col = pick(is_upper("gy", swap), PAD + width_y, 0, PAD)
        add(halo, ext.at[:, pl.ds(PAD, width_x), pl.ds(col, PAD)])
    for swap, halo in enumerate((x0, x1)):
        row = 0
        for n in range(5):
            rows = HALF if n < 2 else VALID[0]
            start = pick(is_upper("gx", swap), PAD + width_x, PAD - rows)
            add(halo.at[pl.ds(row, rows)], ext.at[n, pl.ds(start, rows), inner_y])
            row += rows
    for swap, corner in enumerate((c0, c1)):
        start = pick(is_upper("gx", swap), PAD + width_x, PAD - CORNER)
        for n in range(2):
            col = pick(is_upper("gy", n), PAD + width_y, 0, PAD)
            add(corner.at[n], ext.at[:, pl.ds(start, CORNER), pl.ds(col, PAD)])
    add(inject_hbm, inject)
    for copy in copies:
        copy.start()
    for copy in copies[:-1]:
        copy.wait()

    lane = lax.broadcasted_iota(jnp.int32, (1, depth), 1)
    matrix = depth_matrix(depth)
    fields = [(ext.at[0], ext.at[1])] + [(s.at[0], s.at[1]) for s in (s1, s2, s3)]
    before = (ext.at[2], ext.at[3])
    src_x, src_y, src_z, src_here = locate(src_pos[0], width_x, width_y, depth)
    src_x = jnp.where(src_here, src_x + PAD, PAD)
    src_y = jnp.where(src_here, src_y + PAD, PAD)
    keep = read_tables(owner, aperture, strip_for)
    sends = []

    def send(src, dst):
        copy = pltpu.make_async_copy(src, dst, out_sems.at[len(sends)])
        copy.start()
        sends.append(copy)

    for f in range(2):
        if f == 1:
            copies[-1].wait()
        for t in range(STEPS):
            reach = VALID[t]
            rows = (PAD - reach, width_x + 2 * reach)
            cols = (PAD, width_y) if t == STEPS - 1 else (PAD // 2, width_y + PAD)
            prev = before[f] if t == 0 else fields[t - 1][f]
            out = fields[t + 1][f]
            advance(
                fields[t][f], prev, ext.at[4], out, inject.at[t] if f == 1 else None, rows, cols, matrix
            )
            if f == 0:

                @pl.when(src_here)
                def _():
                    row = out[src_x, pl.ds(src_y, 1), :]
                    out[src_x, pl.ds(src_y, 1), :] = row + jnp.where(lane == src_z, amps[0, t], 0.0)

            send(out.at[pl.ds(PAD - reach, width_x + 2 * reach), inner_y],
                 snaps.at[t, f, pl.ds(PAD - reach, width_x + 2 * reach)])
            if t == STEPS - 1:
                send(out.at[pl.ds(PAD, width_x), inner_y], (src_next, rcv_next)[f].at[0])
    row = 0
    for t in range(STEPS):
        rows = HALF - VALID[t]
        for f in range(2):
            for swap, edge in enumerate((edge0, edge1)):
                start = pick(is_upper("gx", swap), PAD + width_x - HALF, PAD + VALID[t])
                send(fields[t + 1][f].at[pl.ds(start, rows), inner_y], edge.at[pl.ds(row, rows)])
            row += rows
    strip_rows = width_x // tiles
    for i in range(early):
        correlate(
            lambda t, x, c: fields[t + 1][0][x, c, :],
            lambda t, x, c: fields[t + 1][1][x, c, :],
            strip_for, keep, tiles, strip_rows, inner_y, outs, i, i,
        )
    for copy in sends:
        copy.wait()


def rest_kernel(groups, shots, tiles, owner, aperture, snaps, edge0, edge1, *rest):
    outs = rest[: len(groups) * shots]
    held, strip_for, sems = rest[len(groups) * shots :]
    width_x = held.shape[2] - 2 * HALF
    copies = []

    def add(src, dst):
        copies.append(pltpu.make_async_copy(src, dst, sems.at[len(copies)]))

    row = 0
    for t in range(STEPS):
        reach = VALID[t]
        rows = HALF - reach
        for f in range(2):
            span = pl.ds(HALF - reach, width_x + 2 * reach)
            add(snaps.at[t, f, span], held.at[t, f, span])
            for swap, edge in enumerate((edge0, edge1)):
                start = pick(is_upper("gx", swap), HALF + width_x + reach, 0)
                add(edge.at[pl.ds(row, rows)], held.at[t, f, pl.ds(start, rows)])
            row += rows
    keep = read_tables(owner, aperture, strip_for)
    run_copies(copies)
    for g, group in enumerate(groups):
        for slot, i in enumerate(group):
            correlate(
                lambda t, x, c: held[t, 0, x],
                lambda t, x, c: held[t, 1, x],
                strip_for, keep, tiles, width_x // tiles, None,
                outs[g * shots : (g + 1) * shots], slot, i,
            )


def sum_kernel(*refs):
    total = refs[0][...]
    for part in refs[1:-1]:
        total = total + part[...]
    refs[-1][...] = total


def body(
    vel_coef, src_prev, src_cur, rcv_prev, rcv_cur, src_pos, src_amp, rcv_pos, rcv_data, aperture, owner
):
    f32 = jnp.float32
    width_x, width_y, depth = vel_coef.shape
    n_gx, n_gy, shots = lax.axis_size("gx"), lax.axis_size("gy"), lax.axis_size("shot")
    tiles = n_gx * n_gy
    strip_rows = width_x // tiles
    shot = lax.axis_index("shot")
    swaps_x, swaps_y = swap_pairs(n_gx), swap_pairs(n_gy)

    held = OFFS // shots
    chunk_offset = [
        [o * held + (held - 1 - i if 2 * o < shots else i) for o in range(shots)] for i in range(held)
    ]
    early = 0
    while early < held and all(abs(HALF - h) <= VALID[-1] for h in chunk_offset[early]):
        early += 1
    ext_x, ext_y = width_x + 2 * VALID[0], width_y + PAD

    big = pltpu.CompilerParams(vmem_limit_bytes=60 * 1024 * 1024)
    x_rows = 2 * HALF + 3 * VALID[0]
    args = (vel_coef, src_prev, src_cur, rcv_prev, rcv_cur)

    x_part = jax.ShapeDtypeStruct((x_rows, width_y, depth), f32)
    y_part = jax.ShapeDtypeStruct((5, width_x, PAD, depth), f32)
    sends = pl.pallas_call(
        pack_kernel,
        out_shape=(x_part, x_part, y_part, y_part),
        in_specs=[ANY] * 5,
        out_specs=(VMEM,) * 4,
        scratch_shapes=[pltpu.SemaphoreType.DMA((20,))],
        compiler_params=big,
        name="pack_halos",
    )(*args)
    halos = [lax.ppermute(sends[n], "gx", swaps_x[n]) for n in range(2)]
    halos += [lax.ppermute(sends[2 + n], "gy", swaps_y[n]) for n in range(2)]

    receivers = rcv_pos.shape[1]
    inject = pl.pallas_call(
        functools.partial(spread_kernel, width_x, width_y),
        out_shape=jax.ShapeDtypeStruct((STEPS, ext_x * ext_y, depth), f32),
        in_specs=[VMEM] * 2,
        out_specs=VMEM,
        compiler_params=big,
        cost_estimate=pl.CostEstimate(
            flops=6 * ext_x * ext_y * receivers * depth * STEPS, bytes_accessed=4 * STEPS * ext_x * ext_y * depth,
            transcendentals=0),
        name="spread_receivers",
    )(rcv_pos, rcv_data.reshape(1, STEPS * receivers))
    inject = inject.reshape(STEPS, ext_x, ext_y, depth)

    corner = jax.ShapeDtypeStruct((2, 5, CORNER, PAD, depth), f32)
    corners = pl.pallas_call(
        corner_kernel,
        out_shape=(corner, corner),
        in_specs=[ANY] * 3,
        out_specs=(VMEM, VMEM),
        scratch_shapes=[pltpu.SemaphoreType.DMA((4,))],
        compiler_params=big,
        name="pack_corners",
    )(halos[2], halos[3], inject)
    halos += [lax.ppermute(corners[n], "gx", swaps_x[n]) for n in range(2)]

    def piece(group):
        return jax.ShapeDtypeStruct((tiles, len(group), strip_rows, width_y, depth), f32)

    groups = ([tuple(range(early))] if early else []) + [
        tuple(range(i, min(i + 3, held))) for i in range(early, held, 3)
    ]
    ahead, later = (groups[:1], groups[1:]) if early else ([], groups)
    field = jax.ShapeDtypeStruct(src_cur.shape, f32)
    edge_rows = 2 * sum(HALF - v for v in VALID)
    edge = jax.ShapeDtypeStruct((edge_rows, width_y, depth), f32)
    snap_shape = (STEPS, 2, width_x + 2 * HALF, width_y, depth)
    span = (width_x + 2 * PAD, width_y + 2 * PAD, depth)
    step_ops = 60 * width_x * width_y * depth * STEPS
    result = pl.pallas_call(
        functools.partial(front_kernel, early, shots, tiles),
        out_shape=tuple(piece(g) for g in ahead) * shots
        + (field, field, jax.ShapeDtypeStruct(snap_shape, f32), edge, edge),
        in_specs=[SMEM] * 4 + [ANY] * 12,
        out_specs=(VMEM,) * (len(ahead) * shots) + (ANY,) * 5,
        scratch_shapes=[
            pltpu.VMEM((5,) + span, f32),
            pltpu.VMEM((2,) + span, f32),
            pltpu.VMEM((2,) + span, f32),
            pltpu.VMEM((2,) + span, f32),
            pltpu.VMEM((STEPS, ext_x, ext_y, depth), f32),
            pltpu.SMEM((tiles,), jnp.int32),
            pltpu.SemaphoreType.DMA((22,)),
            pltpu.SemaphoreType.DMA((20,)),
        ],
        compiler_params=big,
        cost_estimate=pl.CostEstimate(flops=step_ops, bytes_accessed=12 * 2**20, transcendentals=0),
        name="three_steps",
    )(owner, aperture, src_pos, src_amp, *args, *halos, inject)
    pieces = list(result[: len(ahead) * shots])
    src_next, rcv_next, snaps, *edges = result[len(ahead) * shots :]
    edges = [lax.ppermute(edges[n], "gx", swaps_x[n]) for n in range(2)]
    if later:
        pieces += pl.pallas_call(
            functools.partial(rest_kernel, later, shots, tiles),
            out_shape=tuple(piece(g) for g in later for _ in range(shots)),
            in_specs=[SMEM] * 2 + [ANY] * 3,
            out_specs=(VMEM,) * (len(later) * shots),
            scratch_shapes=[
                pltpu.VMEM(snap_shape, f32), pltpu.SMEM((tiles,), jnp.int32), pltpu.SemaphoreType.DMA((18,))],
            compiler_params=big,
            cost_estimate=pl.CostEstimate(
                flops=5 * OFFS * width_x * width_y * depth, bytes_accessed=12 * 2**20, transcendentals=0),
            name="other_offsets",
        )(owner, aperture, snaps, *edges)

    gathers = jnp.zeros((1, held, tiles, strip_rows, width_y, depth), f32)
    for g, group in enumerate(groups):
        going = pieces[g * shots + 1 : (g + 1) * shots]
        if g >= 2:
            going, coming = lax.optimization_barrier((going, coming))
        coming = [
            lax.ppermute(cells, "shot", [(s, (s + r + 1) % shots) for s in range(shots)])
            for r, cells in enumerate(going)
        ]
        parts = [pieces[g * shots]] + coming
        shape = parts[0].shape
        spec = pl.BlockSpec((4,) + shape[1:], lambda n: (n, 0, 0, 0, 0))
        total = pl.pallas_call(
            sum_kernel,
            grid=(tiles // 4,),
            out_shape=jax.ShapeDtypeStruct(shape, f32),
            in_specs=[spec] * shots,
            out_specs=spec,
            compiler_params=pltpu.CompilerParams(vmem_limit_bytes=16 * 1024 * 1024),
            cost_estimate=pl.CostEstimate(flops=2**37, bytes_accessed=2**28, transcendentals=0),
            name="sum_shots",
        )(*parts)
        arrived = lax.all_to_all(total, ("gx", "gy"), split_axis=0, concat_axis=0, tiled=True)
        for slot, i in enumerate(group):
            where = jnp.where(2 * shot < shots, held - 1 - i, i)
            gathers = lax.dynamic_update_slice(gathers, arrived[None, None, :, slot], (0, where, 0, 0, 0, 0))
    return src_next, rcv_next, gathers


def solution(mesh):
    return jax.shard_map(
        body,
        mesh=mesh,
        in_specs=(
            P("gx", "gy", None),
            P("shot", "gx", "gy", None),
            P("shot", "gx", "gy", None),
            P("shot", "gx", "gy", None),
            P("shot", "gx", "gy", None),
            P("shot"),
            P("shot", None),
            P("shot", None),
            P("shot", None, None),
            P("shot", None),
            P(),
        ),
        out_specs=(
            P("shot", "gx", "gy", None),
            P("shot", "gx", "gy", None),
            P(("gx", "gy"), "shot", None, None, None, None),
        ),
        check_vma=False,
    )
```

time: 349 us -> 192 us (0.55)
  blocking collectives: 98.4 us -> 0 us
  Pallas kernels: 0 us -> 37 us
  other arithmetic: 35.2 us -> 0 us
  local copies, waits for them, and re-layouts: 39.9 us -> 19.9 us
  between operations: 16.5 us -> 1.42 us
  waiting for transfers between devices: 106 us -> 93.7 us
  starting transfers between devices: 50.3 us -> 38.6 us
    unnamed x2 -> x0, waiting for transfers between devices: 99.6 us -> none
    all_to_all x1 -> x0, blocking collectives: 98.4 us -> none  [body(): lax.all_to_all(reduced, ('gx', 'gy'), split_axis=1, concat_axis=1, tiled=...]
    ppermute x18 -> x11, waiting for transfers between devices: 6.32 us -> 50.6 us  [the longest x3 38.8 us: body(): lax.ppermute(cells, 'shot', [(s, (s + r + 1) % shots) for s in range(shot...]
    all_to_all x0 -> x3, waiting for transfers between devices: none -> 43.1 us  [body(): lax.all_to_all(total, ('gx', 'gy'), split_axis=0, concat_axis=0, tiled=True)]
    ppermute x18 -> x11, starting transfers between devices: 50.2 us -> 12.8 us  [the longest x2 4.55 us: body(): halos = [lax.ppermute(sends[n], 'gx', swaps_x[n]) for n in range(2)]]
    pallas_call x0 -> x8, Pallas kernels: none -> 37 us  [the longest x1 11.5 us: body(): pl.pallas_call(functools.partial(front_kernel, early, shots, tiles), out_...]
    all_to_all x0 -> x3, starting transfers between devices: none -> 25.7 us  [body(): lax.all_to_all(total, ('gx', 'gy'), split_axis=0, concat_axis=0, tiled=True)]
    scatter-add x6 -> x0, other arithmetic: 17 us -> none  [inject(): flat_field = field_in.reshape(-1).at[flat_index].add(values, mode='drop')]
  transfers between devices with their start and end apart: 19 -> 14, of which waited for: 5 -> 11; matrix products, arithmetic and copies ran while one was open for 6% -> 5% of each run, Pallas kernels for 0% -> 12%
where the time goes in v1:
time: 192 us; the launch traced here: 191 us
  waiting for transfers between devices  93.7 us (49%)
  starting transfers between devices  38.6 us (20%)
  Pallas kernels  37 us (19%)
  local copies, waits for them, and re-layouts  19.9 us (10%)
    all_to_all x3, waiting for transfers between devices, body(): lax.all_to_all(total, ('gx', 'gy'), split_axis=0, concat_axis=0, tiled=True)  43.1 us
    ppermute x3, waiting for transfers between devices, body(): lax.ppermute(cells, 'shot', [(s, (s + r + 1) % shots) for s in range(shot...  38.8 us
    all_to_all x3, starting transfers between devices, body(): lax.all_to_all(total, ('gx', 'gy'), split_axis=0, concat_axis=0, tiled=True)  25.7 us
    pallas_call x1, Pallas kernels, body(): pl.pallas_call(functools.partial(front_kernel, early, shots, tiles), out_...  11.5 us
    dynamic_update_slice x8, local copies, waits for them, and re-layouts, body(): lax.dynamic_update_slice(gathers, arrived[None, None, :, slot], (0, where...  8.79 us
    pallas_call x1, Pallas kernels, body(): pl.pallas_call(functools.partial(rest_kernel, later, shots, tiles), out_s...  8.61 us
    unnamed x30, local copies, waits for them, and re-layouts  8.55 us
    pallas_call x3, Pallas kernels, body(): pl.pallas_call(sum_kernel, grid=(tiles // 4,), out_shape=jax.ShapeDtypeSt...  6.86 us
  transfers between devices with their start and end apart: 14, of which 11 were waited for; matrix products, arithmetic and copies ran while one was open for 5% of the time, Pallas kernels for 12%

profile of v1, /device:TPU:11, one launch (start us, length us, event | category | flops | bytes accessed | tf_op | source)
XLA Modules:
  0.0 190.6 jit_solution(6675923713420417607)
XLA Ops:
  0.6 3.4 %pack_halos.1 = (f32[34,32,128]{2,1,0:T(8,128)}, f32[34,32,128]{2,1,0:T(8,128)}, f32[5,32,8,128]{3,2,1,0:T(8,128)}, f32[5,32,8,128]{3,2,1,0:T(8,128)}) custom-call(f32[32,32,128]{2,1,0:T(8,128)} %vel.3, f32[1,32,32,128]{3,2,1,0:T(8,128)} %src_prev.3, f32[1,32,32,128]{3,2,1,0:T(8,128)} %src_cur.3, f32[1,32,32,128]{3,2,1,0:T(8,128)} %rcv_prev.3, ...), custom_call_target="tpu_custom_call" | custom-call | tf_op jit(solution)/shard_map/pack_halos/pallas_call | solution.py:360
  5.7 4.3 %collective-permute-start.1 = (f32[34,32,128]{2,1,0:T(8,128)}, f32[34,32,128]{2,1,0:T(8,128)S(1)}, u32[]{:S(2)}, u32[]{:S(2)}) collective-permute-start(f32[34,32,128]{2,1,0:T(8,128)} %get-tuple-element.22), channel_id=1, source_target_pairs={{4,8},{8,4},{5,9},{9,5},{6,10},{10,6},{7,11},{11,7},{20,24},{24,20... | collective-permute-start | bytes 1671176 | tf_op jit(solution)/shard_map/ppermute | solution.py:369
  10.0 4.8 %spread_receivers.1 = f32[3,1760,128]{2,1,0:T(8,128)} custom-call(s32[1,512]{1,0:T(1,128)} %positions.1, f32[1,1536]{1,0:T(1,128)} %bitcast.36), custom_call_target="tpu_custom_call" | custom-call | flops 2076180480 | bytes 2703360 | tf_op jit(solution)/shard_map/spread_receivers/pallas_call | solution.py:373
  15.9 1.9 pack_corners.1
  17.9 1.9 %collective-permute-start.5 = (f32[2,5,6,8,128]{4,3,2,1,0:T(8,128)}, f32[2,5,6,8,128]{4,3,2,1,0:T(8,128)S(1)}, u32[]{:S(2)}, u32[]{:S(2)}) collective-permute-start(f32[2,5,6,8,128]{4,3,2,1,0:T(8,128)} %get-tuple-element.26), channel_id=1, source_target_pairs={{4,8},{8,4},{5,9},{9,5},{6,10},{10,6},{7,11},{11,7},{20,24},{24,20... | collective-permute-start | bytes 737288 | tf_op jit(solution)/shard_map/ppermute | solution.py:396
  21.0 2.4 %collective-permute-done.4.c0 = f32[2,5,6,8,128]{4,3,2,1,0:T(8,128)S(1)} collective-permute-done((f32[2,5,6,8,128]{4,3,2,1,0:T(8,128)}, f32[2,5,6,8,128]{4,3,2,1,0:T(8,128)S(1)}, u32[]{:S(2)}, u32[]{:S(2)}) %collective-permute-start.4) | collective-permute-done | bytes 245792 | tf_op jit(solution)/shard_map/ppermute | solution.py:396
  23.4 2.6 %collective-permute-done.5.c1 = f32[2,5,6,8,128]{4,3,2,1,0:T(8,128)S(1)} collective-permute-done((f32[2,5,6,8,128]{4,3,2,1,0:T(8,128)}, f32[2,5,6,8,128]{4,3,2,1,0:T(8,128)S(1)}, u32[]{:S(2)}, u32[]{:S(2)}) %collective-permute-start.5) | collective-permute-done | bytes 245792 | tf_op jit(solution)/shard_map/ppermute | solution.py:396
  26.7 11.5 %three_steps.1 = (f32[16,2,2,32,128]{4,3,2,1,0:T(8,128)}, f32[16,2,2,32,128]{4,3,2,1,0:T(8,128)}, f32[1,32,32,128]{3,2,1,0:T(8,128)}, f32[1,32,32,128]{3,2,1,0:T...) custom-call(s32[16,16]{1,0:T(8,128)} %owner.3, s32[1,8]{1,0:T(1,128)} %aperture.3, ...), custom_call_target="tpu_custom_call" | custom-call | flops 23592960 | bytes 12582912 | tf_op jit(solution)/shard_map/three_steps/pallas_call | solution.py:411
  39.5 3.1 %collective-permute-start.8 = (f32[24,32,128]{2,1,0:T(8,128)}, f32[24,32,128]{2,1,0:T(8,128)S(1)}, u32[]{:S(2)}, u32[]{:S(2)}) collective-permute-start(f32[24,32,128]{2,1,0:T(8,128)} %get-tuple-element.33), channel_id=1, source_target_pairs={{4,8},{8,4},{5,9},{9,5},{6,10},{10,6},{7,11},{11,7},{20,24},{24,20... | collective-permute-start | bytes 1179656 | tf_op jit(solution)/shard_map/ppermute | solution.py:433
  42.6 4.4 %collective-permute-done.7.edge0 = f32[24,32,128]{2,1,0:T(8,128)S(1)} collective-permute-done((f32[24,32,128]{2,1,0:T(8,128)}, f32[24,32,128]{2,1,0:T(8,128)S(1)}, u32[]{:S(2)}, u32[]{:S(2)}) %collective-permute-start.7) | collective-permute-done | bytes 393248 | tf_op jit(solution)/shard_map/ppermute | solution.py:433
  47.0 1.9 collective-permute-done.8.edge1
  49.6 8.6 %other_offsets.1 = (f32[16,3,2,32,128]{4,3,2,1,0:T(8,128)}, f32[16,3,2,32,128]{4,3,2,1,0:T(8,128)}, f32[16,3,2,32,128]{4,3,2,1,0:T(8,128)}, f32[16,3,2,32,128]{4,3,2,1,0:T(8,128)}) custom-call(s32[16,16]{1,0:T(8,128)} %owner.3, s32[1,8]{1,0:T(1,128)} %aperture.3, f32[3,2,48,32,128]{4,3,2,1,0:T(8,128)} %get-tuple-element.31.snaps, f32[24,32,128]{2,1,0:T(8,128)} %copy-done.11, ...), custom_call_target="tpu_custom_call" | custom-call | flops 10485760 | bytes 12582912 | tf_op jit(solution)/shard_map/other_offsets/pallas_call | solution.py:435
  65.0 11.6 %all-to-all-start = ((f32[16,2,2,32,128]{4,3,2,1,0:T(8,128)}), f32[16,2,2,32,128]{4,3,2,1,0:T(8,128)}, u32[]{:S(2)}, u32[]{:S(2)}) async-start(f32[16,2,2,32,128]{4,3,2,1,0:T(8,128)} %sum_shots.3), calls=%async_computation | async-start | bytes 2097152 | tf_op jit(solution)/shard_map/all_to_all | solution.py:470
  76.6 18.4 %collective-permute-done.9.refs_1_ = f32[16,3,2,32,128]{4,3,2,1,0:T(8,128)S(1)} collective-permute-done((f32[16,3,2,32,128]{4,3,2,1,0:T(8,128)}, f32[16,3,2,32,128]{4,3,2,1,0:T(8,128)S(1)}, u32[]{:S(2)}, u32[]{:S(2)}) %collective-permute-start.9) | collective-permute-done | bytes 1572896 | tf_op jit(solution)/shard_map/ppermute | solution.py:454
  99.6 2.1 %all-to-all-done = f32[16,2,2,32,128]{4,3,2,1,0:T(8,128)} async-done(((f32[16,2,2,32,128]{4,3,2,1,0:T(8,128)}), f32[16,2,2,32,128]{4,3,2,1,0:T(8,128)}, u32[]{:S(2)}, u32[]{:S(2)}) %all-to-all-start) | async-done | bytes 1048608 | tf_op jit(solution)/shard_map/all_to_all | solution.py:470
  101.6 9.2 %all-to-all-start.1 = ((f32[16,3,2,32,128]{4,3,2,1,0:T(8,128)}), f32[16,3,2,32,128]{4,3,2,1,0:T(8,128)S(1)}, u32[]{:S(2)}, u32[]{:S(2)}) async-start(f32[16,3,2,32,128]{4,3,2,1,0:T(8,128)} %sum_shots.4), calls=%async_computation.1 | async-start | bytes 3145728 | tf_op jit(solution)/shard_map/all_to_all | solution.py:470
  110.8 18.9 %collective-permute-done.10.refs_1_ = f32[16,3,2,32,128]{4,3,2,1,0:T(8,128)} collective-permute-done((f32[16,3,2,32,128]{4,3,2,1,0:T(8,128)}, f32[16,3,2,32,128]{4,3,2,1,0:T(8,128)}, u32[]{:S(2)}, u32[]{:S(2)}) %collective-permute-start.10) | collective-permute-done | bytes 1572896 | tf_op jit(solution)/shard_map/ppermute | solution.py:454
  129.7 3.6 %sum_shots.5 = f32[16,3,2,32,128]{4,3,2,1,0:T(8,128)} custom-call(f32[16,3,2,32,128]{4,3,2,1,0:T(8,128)S(1)} %copy-done, f32[16,3,2,32,128]{4,3,2,1,0:T(8,128)} %collective-permute-done.10.refs_1_), custom_call_target="tpu_custom_call" | custom-call | flops 137438953472 | bytes 268435456 | tf_op jit(solution)/shard_map/sum_shots/pallas_call | solution.py:460
  133.3 13.7 %all-to-all-done.1 = f32[16,3,2,32,128]{4,3,2,1,0:T(8,128)S(1)} async-done(((f32[16,3,2,32,128]{4,3,2,1,0:T(8,128)}), f32[16,3,2,32,128]{4,3,2,1,0:T(8,128)S(1)}, u32[]{:S(2)}, u32[]{:S(2)}) %all-to-all-start.1) | async-done | bytes 1572896 | tf_op jit(solution)/shard_map/all_to_all | solution.py:470
  147.0 4.9 %all-to-all-start.2 = ((f32[16,3,2,32,128]{4,3,2,1,0:T(8,128)}), f32[16,3,2,32,128]{4,3,2,1,0:T(8,128)S(1)}, u32[]{:S(2)}, u32[]{:S(2)}) async-start(f32[16,3,2,32,128]{4,3,2,1,0:T(8,128)} %sum_shots.5), calls=%async_computation.2 | async-start | bytes 3145728 | tf_op jit(solution)/shard_map/all_to_all | solution.py:470
  151.9 2.5 %broadcast_in_dim.3 = f32[1,8,16,2,32,128]{5,4,3,2,1,0:T(8,128)} broadcast(f32[]{:T(128)} %constant.11.clone.1), dimensions={} | broadcast | bytes 4194308 | tf_op jit(solution)/shard_map/broadcast_in_dim | solution.py:448
  154.5 1.9 fusion.7
  156.4 1.9 fusion.6
  160.8 27.4 %all-to-all-done.2 = f32[16,3,2,32,128]{4,3,2,1,0:T(8,128)S(1)} async-done(((f32[16,3,2,32,128]{4,3,2,1,0:T(8,128)}), f32[16,3,2,32,128]{4,3,2,1,0:T(8,128)S(1)}, u32[]{:S(2)}, u32[]{:S(2)}) %all-to-all-start.2) | async-done | bytes 1572896 | tf_op jit(solution)/shard_map/all_to_all | solution.py:470
  (51 shorter events, 22.4 us)
Async XLA Ops:
  4.0 10.8 %collective-permute-start.2 = (f32[5,32,8,128]{3,2,1,0:T(8,128)}, f32[5,32,8,128]{3,2,1,0:T(8,128)S(1)}, u32[]{:S(2)}, u32[]{:S(2)}) collective-permute-start(f32[5,32,8,128]{3,2,1,0:T(8,128)} %get-tuple-element.23), channel_id=1, source_target_pairs={{0,1},{1,0},{2,3},{3,2},{4,5},{5,4},{6,7},{7,6},{8,9},{9,8},{10,11... | collective-permute-start | bytes 1966088 | tf_op jit(solution)/shard_map/ppermute | solution.py:370
  4.7 10.1 %collective-permute-start.3 = (f32[5,32,8,128]{3,2,1,0:T(8,128)}, f32[5,32,8,128]{3,2,1,0:T(8,128)S(1)}, u32[]{:S(2)}, u32[]{:S(2)}) collective-permute-start(f32[5,32,8,128]{3,2,1,0:T(8,128)} %get-tuple-element.24), channel_id=1, source_target_pairs={{1,2},{2,1},{5,6},{6,5},{9,10},{10,9},{13,14},{14,13},{17,18},{18,... | collective-permute-start | bytes 1966088 | tf_op jit(solution)/shard_map/ppermute | solution.py:370
  5.4 15.0 %collective-permute-start = (f32[34,32,128]{2,1,0:T(8,128)}, f32[34,32,128]{2,1,0:T(8,128)S(1)}, u32[]{:S(2)}, u32[]{:S(2)}) collective-permute-start(f32[34,32,128]{2,1,0:T(8,128)} %get-tuple-element.21), channel_id=1, source_target_pairs={{0,4},{4,0},{8,12},{12,8},{1,5},{5,1},{9,13},{13,9},{2,6},{6,2},{1... | collective-permute-start | bytes 1671176 | tf_op jit(solution)/shard_map/ppermute | solution.py:369
  5.7 15.3 %collective-permute-start.1 = (f32[34,32,128]{2,1,0:T(8,128)}, f32[34,32,128]{2,1,0:T(8,128)S(1)}, u32[]{:S(2)}, u32[]{:S(2)}) collective-permute-start(f32[34,32,128]{2,1,0:T(8,128)} %get-tuple-element.22), channel_id=1, source_target_pairs={{4,8},{8,4},{5,9},{9,5},{6,10},{10,6},{7,11},{11,7},{20,24},{24,20... | collective-permute-start | bytes 1671176 | tf_op jit(solution)/shard_map/ppermute | solution.py:369
  17.8 5.6 %collective-permute-start.4 = (f32[2,5,6,8,128]{4,3,2,1,0:T(8,128)}, f32[2,5,6,8,128]{4,3,2,1,0:T(8,128)S(1)}, u32[]{:S(2)}, u32[]{:S(2)}) collective-permute-start(f32[2,5,6,8,128]{4,3,2,1,0:T(8,128)} %get-tuple-element.25), channel_id=1, source_target_pairs={{0,4},{4,0},{8,12},{12,8},{1,5},{5,1},{9,13},{13,9},{2,6},{6,2},{1... | collective-permute-start | bytes 737288 | tf_op jit(solution)/shard_map/ppermute | solution.py:396
  17.9 8.1 %collective-permute-start.5 = (f32[2,5,6,8,128]{4,3,2,1,0:T(8,128)}, f32[2,5,6,8,128]{4,3,2,1,0:T(8,128)S(1)}, u32[]{:S(2)}, u32[]{:S(2)}) collective-permute-start(f32[2,5,6,8,128]{4,3,2,1,0:T(8,128)} %get-tuple-element.26), channel_id=1, source_target_pairs={{4,8},{8,4},{5,9},{9,5},{6,10},{10,6},{7,11},{11,7},{20,24},{24,20... | collective-permute-start | bytes 737288 | tf_op jit(solution)/shard_map/ppermute | solution.py:396
  20.5 5.5 %copy-start.9 = (f32[34,32,128]{2,1,0:T(8,128)}, f32[34,32,128]{2,1,0:T(8,128)S(1)}, u32[]{:S(2)}) copy-start(f32[34,32,128]{2,1,0:T(8,128)S(1)} %collective-permute-done.x0) | copy-start | bytes 1671172
  21.0 5.0 %copy-start.10 = (f32[34,32,128]{2,1,0:T(8,128)}, f32[34,32,128]{2,1,0:T(8,128)S(1)}, u32[]{:S(2)}) copy-start(f32[34,32,128]{2,1,0:T(8,128)S(1)} %collective-permute-done.1.x1) | copy-start | bytes 1671172
  23.4 2.6 %copy-start.13 = (f32[2,5,6,8,128]{4,3,2,1,0:T(8,128)}, f32[2,5,6,8,128]{4,3,2,1,0:T(8,128)S(1)}, u32[]{:S(2)}) copy-start(f32[2,5,6,8,128]{4,3,2,1,0:T(8,128)S(1)} %collective-permute-done.4.c0) | copy-start | bytes 737284
  38.2 21.8 %collective-permute-start.6 = (f32[16,2,2,32,128]{4,3,2,1,0:T(8,128)}, f32[16,2,2,32,128]{4,3,2,1,0:T(8,128)S(1)}, u32[]{:S(2)}, u32[]{:S(2)}) collective-permute-start(f32[16,2,2,32,128]{4,3,2,1,0:T(8,128)} %get-tuple-element.30), channel_id=1, source_target_pairs={{0,16},{16,0},{1,17},{17,1},{2,18},{18,2},{3,19},{19,3},{4,20},{20... | collective-permute-start | bytes 3145736 | tf_op jit(solution)/shard_map/ppermute | solution.py:454
  39.5 7.4 %collective-permute-start.7 = (f32[24,32,128]{2,1,0:T(8,128)}, f32[24,32,128]{2,1,0:T(8,128)S(1)}, u32[]{:S(2)}, u32[]{:S(2)}) collective-permute-start(f32[24,32,128]{2,1,0:T(8,128)} %get-tuple-element.32), channel_id=1, source_target_pairs={{0,4},{4,0},{8,12},{12,8},{1,5},{5,1},{9,13},{13,9},{2,6},{6,2},{1... | collective-permute-start | bytes 1179656 | tf_op jit(solution)/shard_map/ppermute | solution.py:433
  39.5 9.3 %collective-permute-start.8 = (f32[24,32,128]{2,1,0:T(8,128)}, f32[24,32,128]{2,1,0:T(8,128)S(1)}, u32[]{:S(2)}, u32[]{:S(2)}) collective-permute-start(f32[24,32,128]{2,1,0:T(8,128)} %get-tuple-element.33), channel_id=1, source_target_pairs={{4,8},{8,4},{5,9},{9,5},{6,10},{10,6},{7,11},{11,7},{20,24},{24,20... | collective-permute-start | bytes 1179656 | tf_op jit(solution)/shard_map/ppermute | solution.py:433
  47.0 1.9 copy-start.11
  58.2 36.9 %collective-permute-start.9 = (f32[16,3,2,32,128]{4,3,2,1,0:T(8,128)}, f32[16,3,2,32,128]{4,3,2,1,0:T(8,128)S(1)}, u32[]{:S(2)}, u32[]{:S(2)}) collective-permute-start(f32[16,3,2,32,128]{4,3,2,1,0:T(8,128)} %get-tuple-element.35), channel_id=1, source_target_pairs={{0,16},{16,0},{1,17},{17,1},{2,18},{18,2},{3,19},{19,3},{4,20},{20... | collective-permute-start | bytes 4718600 | tf_op jit(solution)/shard_map/ppermute | solution.py:454
  61.0 1.2 copy-start.4
  62.2 1.2 copy-start.6
  63.5 33.0 %copy-start.1 = (f32[16,3,2,32,128]{4,3,2,1,0:T(8,128)S(1)}, f32[16,3,2,32,128]{4,3,2,1,0:T(8,128)}, u32[]{:S(2)}) copy-start(f32[16,3,2,32,128]{4,3,2,1,0:T(8,128)} %get-tuple-element.34.refs_0_) | copy-start | bytes 4718596
  65.0 36.6 %all-to-all-start = ((f32[16,2,2,32,128]{4,3,2,1,0:T(8,128)}), f32[16,2,2,32,128]{4,3,2,1,0:T(8,128)}, u32[]{:S(2)}, u32[]{:S(2)}) async-start(f32[16,2,2,32,128]{4,3,2,1,0:T(8,128)} %sum_shots.3), calls=%async_computation | async-start | bytes 2097152 | tf_op jit(solution)/shard_map/all_to_all | solution.py:470
  95.1 1.1 copy-start.2
  96.2 33.5 %collective-permute-start.10 = (f32[16,3,2,32,128]{4,3,2,1,0:T(8,128)}, f32[16,3,2,32,128]{4,3,2,1,0:T(8,128)}, u32[]{:S(2)}, u32[]{:S(2)}) collective-permute-start(f32[16,3,2,32,128]{4,3,2,1,0:T(8,128)} %get-tuple-element.38), channel_id=1, source_target_pairs={{0,16},{16,0},{1,17},{17,1},{2,18},{18,2},{3,19},{19,3},{4,20},{20... | collective-permute-start | bytes 4718600 | tf_op jit(solution)/shard_map/ppermute | solution.py:454
  96.4 1.4 copy-start.3
  97.9 31.9 %copy-start = (f32[16,3,2,32,128]{4,3,2,1,0:T(8,128)S(1)}, f32[16,3,2,32,128]{4,3,2,1,0:T(8,128)}, u32[]{:S(2)}) copy-start(f32[16,3,2,32,128]{4,3,2,1,0:T(8,128)} %get-tuple-element.36.refs_0_) | copy-start | bytes 4718596
  101.6 45.4 %all-to-all-start.1 = ((f32[16,3,2,32,128]{4,3,2,1,0:T(8,128)}), f32[16,3,2,32,128]{4,3,2,1,0:T(8,128)S(1)}, u32[]{:S(2)}, u32[]{:S(2)}) async-start(f32[16,3,2,32,128]{4,3,2,1,0:T(8,128)} %sum_shots.4), calls=%async_computation.1 | async-start | bytes 3145728 | tf_op jit(solution)/shard_map/all_to_all | solution.py:470
  147.0 41.1 %all-to-all-start.2 = ((f32[16,3,2,32,128]{4,3,2,1,0:T(8,128)}), f32[16,3,2,32,128]{4,3,2,1,0:T(8,128)S(1)}, u32[]{:S(2)}, u32[]{:S(2)}) async-start(f32[16,3,2,32,128]{4,3,2,1,0:T(8,128)} %sum_shots.5), calls=%async_computation.2 | async-start | bytes 3145728 | tf_op jit(solution)/shard_map/all_to_all | solution.py:470
  (5 other events, 4.4 us)

commit v2 on v1

v2 whole, which is shorter than its diff:
```python
import functools

import jax
import jax.numpy as jnp
from jax import lax
from jax.experimental import pallas as pl
from jax.experimental.pallas import tpu as pltpu
from jax.sharding import PartitionSpec as P

OFFS = 16
STEPS = 3
HALF = 8
PAD = 8
VALID = (6, 4, 2)
CORNER = 6

LAP_CENTER = -2.5
LAP_NEAR = 4.0 / 3.0
LAP_FAR = -1.0 / 12.0

ANY = pl.BlockSpec(memory_space=pl.ANY)
SMEM = pl.BlockSpec(memory_space=pltpu.SMEM)
VMEM = pl.BlockSpec(memory_space=pltpu.VMEM)


def swap_pairs(count):
    first = [(i, i ^ 1) for i in range(count) if (i ^ 1) < count]
    second = []
    for i in range(1, count - 1, 2):
        second += [(i, i + 1), (i + 1, i)]
    return first, second


def largest_block(count, limit):
    return max(n for n in range(1, limit + 1) if count % n == 0)


def run_copies(copies):
    for copy in copies:
        copy.start()
    for copy in copies:
        copy.wait()


def is_upper(axis, swap):
    return lax.rem(lax.axis_index(axis) + swap, 2) == 0


def pick(condition, upper, lower, multiple=1):
    return pl.multiple_of(jnp.where(condition, upper, lower), multiple)


def pack_kernel(vel, src_prev, src_cur, rcv_prev, rcv_cur, x0, x1, y0, y1, *scratch):
    *buffers, sems, out_sems = scratch
    width_x, width_y, depth = vel.shape
    fields = (src_cur.at[0], rcv_cur.at[0], src_prev.at[0], rcv_prev.at[0], vel)
    jobs = []
    count = 0
    for swap in range(2):
        start = pick(is_upper("gy", swap), width_y - PAD, 0, PAD)
        copies = []
        for n, field in enumerate(fields):
            copies.append(
                pltpu.make_async_copy(field.at[:, pl.ds(start, PAD)], buffers[2 + swap].at[n], sems.at[count])
            )
            count += 1
        jobs.append((copies, buffers[2 + swap], (y0, y1)[swap]))
    for swap in range(2):
        row = 0
        copies = []
        for n, field in enumerate(fields):
            rows = HALF if n < 2 else VALID[0]
            start = pick(is_upper("gx", swap), width_x - rows, 0)
            copies.append(
                pltpu.make_async_copy(
                    field.at[pl.ds(start, rows)], buffers[swap].at[pl.ds(row, rows)], sems.at[count])
            )
            row += rows
            count += 1
        jobs.append((copies, buffers[swap], (x0, x1)[swap]))
    for copies, _, _ in jobs:
        for copy in copies:
            copy.start()
    sends = []
    for n, (copies, buffer, out) in enumerate(jobs):
        for copy in copies:
            copy.wait()
        sends.append(pltpu.make_async_copy(buffer, out, out_sems.at[n]))
        sends[-1].start()
    for copy in sends:
        copy.wait()


def corner_kernel(y0, y1, late, c0, c1, sems):
    width_x = y0.shape[1]
    copies = []
    for swap, out in enumerate((c0, c1)):
        start = pick(is_upper("gx", swap), width_x - CORNER, 0)
        for n, halo in enumerate((y0, y1)):
            copies.append(
                pltpu.make_async_copy(halo.at[:, pl.ds(start, CORNER)], out.at[n], sems.at[len(copies)])
            )
    run_copies(copies)


def locate(position, width_x, width_y, depth):
    grid_y = width_y * lax.axis_size("gy")
    x = lax.div(position, grid_y * depth) - lax.axis_index("gx") * width_x
    y = lax.rem(lax.div(position, depth), grid_y) - lax.axis_index("gy") * width_y
    reach = VALID[0]
    inside = (x >= -reach) & (x < width_x + reach) & (y >= -PAD // 2) & (y < width_y + PAD // 2)
    return x, y, lax.rem(position, depth), inside


def spread_kernel(width_x, width_y, positions, values, out):
    rows, depth = out.shape[1], out.shape[2]
    receivers = positions.shape[1]
    x, y, depths, inside = locate(positions[...], width_x, width_y, depth)
    cell_row = jnp.where(inside, (x + VALID[0]) * (width_y + PAD) + y + PAD // 2, -1)
    lanes = lax.broadcasted_iota(jnp.int32, (depth, receivers), 0)
    rest = jnp.concatenate(
        [
            jnp.where(lanes == depths, values[:, t * receivers : (t + 1) * receivers], 0.0)
            for t in range(STEPS)
        ],
        axis=0,
    )
    parts = []
    for _ in range(3):
        parts.append(rest.astype(jnp.bfloat16))
        rest = rest - parts[-1].astype(jnp.float32)
    index = lax.broadcasted_iota(jnp.int32, (rows, receivers), 0)
    hot = jnp.where(index == cell_row, 1.0, 0.0).astype(jnp.bfloat16)
    total = lax.dot_general(
        hot, jnp.concatenate(parts, axis=0), (((1,), (1,)), ((), ())), preferred_element_type=jnp.float32
    )
    for t in range(STEPS):
        high, middle, low = (
            total[:, (n * STEPS + t) * depth : (n * STEPS + t + 1) * depth] for n in range(3)
        )
        out[t] = high + (middle + low)


def depth_matrix(depth):
    row = lax.broadcasted_iota(jnp.int32, (depth, depth), 0)
    col = lax.broadcasted_iota(jnp.int32, (depth, depth), 1)
    apart = jnp.abs(row - col)
    return jnp.where(apart == 1, 16.0, jnp.where(apart == 2, -1.0, 0.0)).astype(jnp.bfloat16)


def depth_neighbours(here, matrix):
    rest = here.reshape(-1, here.shape[-1])
    total = None
    for _ in range(3):
        part = rest.astype(jnp.bfloat16)
        rest = rest - part.astype(jnp.float32)
        term = jnp.dot(part, matrix, preferred_element_type=jnp.float32)
        total = term if total is None else total + term
    return total.reshape(here.shape)


def advance(cur, prev, vel, out, inject, rows, cols, matrix):
    first, count = rows
    col, width = cols
    block = largest_block(count, 28)

    def one(step, carry):
        x = first + step * block
        at = lambda ref, dx, dy: ref[pl.ds(x + dx, block), pl.ds(col + dy, width), :]
        here = at(cur, 0, 0)
        near = at(cur, 1, 0) + at(cur, -1, 0) + at(cur, 0, 1) + at(cur, 0, -1)
        far = at(cur, 2, 0) + at(cur, -2, 0) + at(cur, 0, 2) + at(cur, 0, -2)
        lap = (3.0 * LAP_CENTER) * here + LAP_NEAR * near + LAP_FAR * far
        lap = lap + (1.0 / 12.0) * depth_neighbours(here, matrix)
        new = 2.0 * here - at(prev, 0, 0) + at(vel, 0, 0) * lap
        if inject is not None:
            new = new + inject[pl.ds(x - (PAD - VALID[0]), block), pl.ds(col - PAD // 2, width), :]
        out[pl.ds(x, block), pl.ds(col, width), :] = new
        return carry

    if count == block:
        one(0, 0)
    else:
        lax.fori_loop(0, count // block, one, 0)


def chunk_shift(i, r):
    shots = lax.axis_size("shot")
    held = OFFS // shots
    keeper = lax.rem(lax.axis_index("shot") + r, shots)
    return HALF - (keeper * held + jnp.where(2 * keeper < shots, held - 1 - i, i))


def is_active(aperture):
    tile = lax.axis_index(("gx", "gy"))
    active = aperture[0, 0] == tile
    for k in range(1, aperture.shape[1]):
        active = active | (aperture[0, k] == tile)
    return active


def correlate(lead, lag, strips, keep, strip_rows, outs, slot, i):
    shifts = [chunk_shift(i, r) for r in range(len(outs))]
    place, count = strips

    def one(n, carry):
        for u in range(strip_rows):
            x = HALF + place(n) * strip_rows + u
            for r, out in enumerate(outs):
                total = None
                for t in range(STEPS):
                    term = lead(t, x + shifts[r]) * lag(t, x - shifts[r])
                    total = term if total is None else total + term
                out[n, slot, u] = jnp.where(keep, total, 0.0)
        return carry

    lax.fori_loop(0, count, one, 0)


def inner_rows(t, width_x):
    return PAD + 2 * (t + 1), width_x - 4 * (t + 1)


def outer_rows(t, width_x):
    first, count = inner_rows(t, width_x)
    return (PAD - VALID[t], first + VALID[t] - PAD), (first + count, PAD + width_x + VALID[t] - first - count)


def rims(width_x):
    return (PAD + 2, PAD), (width_x - 2, PAD)


class Sources:
    def __init__(self, src_pos, amps, shape):
        width_x, width_y, depth = shape
        x, y, z, here = locate(src_pos[0], width_x, width_y, depth)
        self.row, self.col, self.here, self.amps = x + PAD, y + PAD, here, amps
        self.lane = lax.broadcasted_iota(jnp.int32, (1, depth), 1)
        self.depth = z

    def add(self, out, t, rows):
        first, count = rows

        @pl.when(self.here & (self.row >= first) & (self.row < first + count))
        def _():
            cells = out[self.row, pl.ds(self.col, 1), :]
            out[self.row, pl.ds(self.col, 1), :] = cells + jnp.where(self.lane == self.depth, self.amps[0, t], 0.0)


def column_window(t, width_y):
    return (PAD, width_y) if t == STEPS - 1 else (PAD // 2, width_y + PAD)


def inner_kernel(
    early, shots, owner, aperture, src_pos, amps,
    vel, src_prev, src_cur, rcv_prev, rcv_cur, y0, y1, inject_from, *rest
):
    count = shots if early else 0
    outs, (s1, s2, s3, ext, inject, sems) = rest[:count], rest[count:]
    width_x, width_y, depth = vel.shape
    inner_y = pl.ds(PAD, width_y)
    copies = []

    def add(src, dst):
        copies.append(pltpu.make_async_copy(src, dst, sems.at[len(copies)]))

    for swap, halo in enumerate((y0, y1)):
        col = pick(is_upper("gy", swap), PAD + width_y, 0, PAD)
        add(halo, ext.at[:, pl.ds(PAD, width_x), pl.ds(col, PAD)])
    for n, field in ((0, src_cur.at[0]), (2, src_prev.at[0]), (4, vel), (1, rcv_cur.at[0]), (3, rcv_prev.at[0])):
        add(field, ext.at[n, pl.ds(PAD, width_x), inner_y])
    used = pl.ds(PAD, width_x - 4)
    add(inject_from.at[:, used], inject.at[:, used])
    for copy in copies:
        copy.start()
    keep = is_active(aperture)
    matrix = depth_matrix(depth)
    source = Sources(src_pos, amps, vel.shape)
    for f in range(2):
        for copy in copies[5:] if f else copies[:5]:
            copy.wait()
        fields = [ext.at[f], s1.at[f], s2.at[f], s3.at[f]]
        for t in range(STEPS):
            prev = ext.at[2 + f] if t == 0 else fields[t - 1]
            rows = inner_rows(t, width_x)
            advance(
                fields[t], prev, ext.at[4], fields[t + 1], inject.at[t] if f == 1 else None,
                rows, column_window(t, width_y), matrix,
            )
            if f == 0:
                source.add(fields[t + 1], t, rows)
    steps = (s1, s2, s3)
    strip_rows = width_x // owner.shape[0]
    for i in range(early):
        correlate(
            lambda t, x: steps[t][0, x, inner_y, :], lambda t, x: steps[t][1, x, inner_y, :],
            strip_map(0, width_x, strip_rows), keep, strip_rows, outs, i, i,
        )


def outer_kernel(
    early, shots, owner, aperture, src_pos, amps,
    vel, src_prev, src_cur, rcv_prev, rcv_cur, x0, x1, y0, y1, c0, c1, inject_from, i1, i2, i3, *rest
):
    count = shots if early else 0
    outs, (s1, s2, s3, edge0, edge1, ext, inject, sems, out_sems) = rest[:count], rest[count:]
    width_x, width_y, depth = vel.shape
    inner_y = pl.ds(PAD, width_y)
    copies = []

    def add(src, dst):
        copies.append(pltpu.make_async_copy(src, dst, sems.at[len(copies)]))

    for swap, halo in enumerate((y0, y1)):
        col = pick(is_upper("gy", swap), PAD + width_y, 0, PAD)
        for first in (0, width_x - PAD):
            add(halo.at[:, pl.ds(first, PAD)], ext.at[:, pl.ds(PAD + first, PAD), pl.ds(col, PAD)])
    for swap, corner in enumerate((c0, c1)):
        start = pick(is_upper("gx", swap), PAD + width_x, PAD - CORNER)
        for n in range(2):
            col = pick(is_upper("gy", n), PAD + width_y, 0, PAD)
            add(corner.at[n], ext.at[:, pl.ds(start, CORNER), pl.ds(col, PAD)])
    row = 0
    fields = (src_cur.at[0], rcv_cur.at[0], src_prev.at[0], rcv_prev.at[0], vel)
    for n in range(5):
        rows = HALF if n < 2 else VALID[0]
        for swap, halo in enumerate((x0, x1)):
            start = pick(is_upper("gx", swap), PAD + width_x, PAD - rows)
            add(halo.at[pl.ds(row, rows)], ext.at[n, pl.ds(start, rows), inner_y])
        for first in (0, width_x - PAD):
            add(fields[n].at[pl.ds(first, PAD)], ext.at[n, pl.ds(PAD + first, PAD), inner_y])
        row += rows
    for first, rows in rims(width_x):
        for inner, step in ((i1, s1), (i2, s2), (i3, s3)):
            add(inner.at[:, pl.ds(first, rows)], step.at[:, pl.ds(first, rows)])
    for first in (0, inject.shape[1] - 12):
        used = pl.ds(first, 12)
        add(inject_from.at[:, used], inject.at[:, used])
    for copy in copies:
        copy.start()
    keep = is_active(aperture)
    matrix = depth_matrix(depth)
    source = Sources(src_pos, amps, vel.shape)
    for copy in copies:
        copy.wait()
    chain = [[ext.at[f], s1.at[f], s2.at[f], s3.at[f]] for f in range(2)]
    for t in range(STEPS):
        for f, fields in enumerate(chain):
            prev = ext.at[2 + f] if t == 0 else fields[t - 1]
            for rows in outer_rows(t, width_x):
                advance(
                    fields[t], prev, ext.at[4], fields[t + 1], inject.at[t] if f == 1 else None,
                    rows, column_window(t, width_y), matrix,
                )
        for rows in outer_rows(t, width_x):
            source.add(chain[0][t + 1], t, rows)
    steps = (s1, s2, s3)
    sends = []
    row = 0
    for t in range(STEPS):
        rows = HALF - VALID[t]
        for f in range(2):
            for swap, edge in enumerate((edge0, edge1)):
                start = pick(is_upper("gx", swap), PAD + width_x - HALF, PAD + VALID[t])
                sends.append(
                    pltpu.make_async_copy(
                        steps[t].at[f, pl.ds(start, rows), inner_y], edge.at[pl.ds(row, rows)],
                        out_sems.at[len(sends)],
                    )
                )
                sends[-1].start()
            row += rows
    strip_rows = width_x // owner.shape[0]
    for i in range(early):
        correlate(
            lambda t, x: steps[t][0, x, inner_y, :], lambda t, x: steps[t][1, x, inner_y, :],
            strip_map(1, width_x, strip_rows), keep, strip_rows, outs, i, i,
        )
    for copy in sends:
        copy.wait()


def strip_map(part, width_x, strip_rows):
    side = HALF // strip_rows
    middle = (width_x - 2 * HALF) // strip_rows
    if part == 0:
        return lambda n: n + side, middle
    return lambda n: n + jnp.where(n < side, 0, middle), 2 * side


def rest_kernel(part, groups, shots, owner, aperture, i1, i2, i3, o1, o2, o3, *rest):
    edges, rest = rest[: 3 * part], rest[3 * part :]
    count = len(groups) * shots
    results, rest = rest[:count], rest[count:]
    last, rest = rest[: 2 - 2 * part], rest[2 - 2 * part :]
    outs, (held, sems, out_sems) = (results[0], *rest[: count - 1]), rest[count - 1 :]
    width_x = held.shape[2] - 2 * HALF
    inner_y = pl.ds(PAD, held.shape[3])
    copies = []

    def add(src, dst):
        copies.append(pltpu.make_async_copy(src, dst, sems.at[len(copies)]))

    (low, rim), (high, _) = rims(width_x)
    row = 0
    for t, (inner, outer) in enumerate(((i1, o1), (i2, o2), (i3, o3))):
        reach = VALID[t] if part else 0
        rows = HALF - VALID[t]
        middle = pl.ds(low + rim, high - low - rim)
        spans = (pl.ds(PAD - reach, low + rim - PAD + reach), pl.ds(high, PAD + width_x + reach - high))
        add(inner.at[:, middle, inner_y], held.at[t, :, middle])
        for span in spans:
            add(outer.at[:, span, inner_y], held.at[t, :, span])
        for f in range(2 * part):
            for swap, edge in enumerate(edges[:2]):
                start = pick(is_upper("gx", swap), HALF + width_x + reach, 0)
                add(edge.at[pl.ds(row, rows)], held.at[t, f, pl.ds(start, rows)])
            row += rows
    keep = is_active(aperture)
    run_copies(copies)
    sends = []

    def send(src, dst):
        sends.append(pltpu.make_async_copy(src, dst, out_sems.at[len(sends)]))
        sends[-1].start()

    strip_rows = width_x // owner.shape[0]
    for g, group in enumerate(groups):
        for slot, i in enumerate(group):
            places = slice(g * shots, (g + 1) * shots)
            correlate(
                lambda t, x: held[t, 0, x], lambda t, x: held[t, 1, x],
                strip_map(part, width_x, strip_rows), keep, strip_rows, outs[places], slot, i,
            )
            for out, result in zip(outs[places], results[places]):
                if out is not result:
                    send(out.at[:, slot], result.at[:, slot])
    for f, out in enumerate(last):
        send(held.at[STEPS - 1, f, pl.ds(HALF, width_x)], out.at[0])
    for copy in sends:
        copy.wait()


def sum_kernel(part, shots, owner, *refs):
    parts = refs[:shots]
    total, cells, sems = refs[shots + part :]
    tiles = owner.shape[0]
    tile = lax.axis_index(("gx", "gy"))
    strip, count = strip_map(part, parts[0].shape[2] * tiles, parts[0].shape[2])
    copies = []
    for n in range(count):
        one = parts[0][n]
        for other in parts[1:]:
            one = one + other[n]
        cells[n] = one
        copies.append(pltpu.make_async_copy(cells.at[n], total.at[owner[tile, strip(n)]], sems.at[n]))
        copies[-1].start()
    for copy in copies:
        copy.wait()


def place_kernel(group, held, old, piece, out, sems):
    shots = lax.axis_size("shot")
    copies = []
    for slot, i in enumerate(group):
        where = jnp.where(2 * lax.axis_index("shot") < shots, held - 1 - i, i)
        copies.append(pltpu.make_async_copy(piece.at[:, slot], out.at[0, where], sems.at[slot]))
    run_copies(copies)


def body(
    vel_coef, src_prev, src_cur, rcv_prev, rcv_cur, src_pos, src_amp, rcv_pos, rcv_data, aperture, owner
):
    f32 = jnp.float32
    width_x, width_y, depth = vel_coef.shape
    n_gx, n_gy, shots = lax.axis_size("gx"), lax.axis_size("gy"), lax.axis_size("shot")
    tiles = n_gx * n_gy
    strip_rows = width_x // tiles
    shot = lax.axis_index("shot")
    swaps_x, swaps_y = swap_pairs(n_gx), swap_pairs(n_gy)

    held = OFFS // shots
    chunk_offset = [
        [o * held + (held - 1 - i if 2 * o < shots else i) for o in range(shots)] for i in range(held)
    ]
    early = 0
    while early < held and all(abs(HALF - h) <= VALID[-1] for h in chunk_offset[early]):
        early += 1
    ext_x, ext_y = width_x + 2 * VALID[0], width_y + PAD

    small = pltpu.CompilerParams(vmem_limit_bytes=16 * 1024 * 1024)
    big = pltpu.CompilerParams(vmem_limit_bytes=24 * 1024 * 1024)
    x_rows = 2 * HALF + 3 * VALID[0]
    args = (vel_coef, src_prev, src_cur, rcv_prev, rcv_cur)

    x_part = jax.ShapeDtypeStruct((x_rows, width_y, depth), f32)
    y_part = jax.ShapeDtypeStruct((5, width_x, PAD, depth), f32)
    sends = pl.pallas_call(
        pack_kernel,
        out_shape=(x_part, x_part, y_part, y_part),
        in_specs=[ANY] * 5,
        out_specs=(ANY,) * 4,
        scratch_shapes=[pltpu.VMEM(part.shape, f32) for part in (x_part, x_part, y_part, y_part)]
        + [pltpu.SemaphoreType.DMA((20,)), pltpu.SemaphoreType.DMA((4,))],
        compiler_params=pltpu.CompilerParams(vmem_limit_bytes=60 * 1024 * 1024),
        name="pack_halos",
    )(*args)
    halos = [lax.ppermute(sends[n], "gx", swaps_x[n]) for n in range(2)]
    halos += [lax.ppermute(sends[2 + n], "gy", swaps_y[n]) for n in range(2)]

    receivers = rcv_pos.shape[1]
    inject = pl.pallas_call(
        functools.partial(spread_kernel, width_x, width_y),
        out_shape=jax.ShapeDtypeStruct((STEPS, ext_x * ext_y, depth), f32),
        in_specs=[VMEM] * 2,
        out_specs=VMEM,
        compiler_params=big,
        cost_estimate=pl.CostEstimate(
            flops=6 * ext_x * ext_y * receivers * depth * STEPS, bytes_accessed=4 * STEPS * ext_x * ext_y * depth,
            transcendentals=0),
        name="spread_receivers",
    )(rcv_pos, rcv_data.reshape(1, STEPS * receivers))
    inject = inject.reshape(STEPS, ext_x, ext_y, depth)

    corner = jax.ShapeDtypeStruct((2, 5, CORNER, PAD, depth), f32)
    corners = pl.pallas_call(
        corner_kernel,
        out_shape=(corner, corner),
        in_specs=[ANY] * 3,
        out_specs=(VMEM, VMEM),
        scratch_shapes=[pltpu.SemaphoreType.DMA((4,))],
        compiler_params=big,
        name="pack_corners",
    )(halos[2], halos[3], inject)
    halos += [lax.ppermute(corners[n], "gx", swaps_x[n]) for n in range(2)]

    def piece(strips, group):
        return jax.ShapeDtypeStruct((strips, len(group), strip_rows, width_y, depth), f32)

    first = tuple(range(early))
    groups = [tuple(range(i, min(i + 3, held))) for i in range(early, held, 3)]
    edge_rows = 2 * sum(HALF - v for v in VALID)
    edge = jax.ShapeDtypeStruct((edge_rows, width_y, depth), f32)
    span = (width_x + 2 * PAD, width_y + 2 * PAD, depth)
    step = jax.ShapeDtypeStruct((2,) + span, f32)
    step_ops = 30 * width_x * width_y * depth * STEPS
    tables = (owner, aperture)
    middle = (width_x - 2 * HALF) // strip_rows
    inner = pl.pallas_call(
        functools.partial(inner_kernel, early, shots),
        out_shape=(piece(middle, first),) * (shots if early else 0) + (step,) * 3,
        in_specs=[SMEM] * 4 + [ANY] * 8,
        out_specs=(VMEM,) * ((shots if early else 0) + 3),
        scratch_shapes=[
            pltpu.VMEM((5,) + span, f32),
            pltpu.VMEM((STEPS, ext_x, ext_y, depth), f32),
            pltpu.SemaphoreType.DMA((8,)),
        ],
        compiler_params=big,
        cost_estimate=pl.CostEstimate(flops=step_ops, bytes_accessed=12 * 2**20, transcendentals=0),
        name="inner_steps",
    )(*tables, src_pos, src_amp, *args, *halos[2:4], inject)
    inner_pieces, inner = inner[:-3], inner[-3:]
    outer = pl.pallas_call(
        functools.partial(outer_kernel, early, shots),
        out_shape=(piece(tiles - middle, first),) * (shots if early else 0) + (step,) * 3 + (edge, edge),
        in_specs=[SMEM] * 4 + [ANY] * 15,
        out_specs=(VMEM,) * ((shots if early else 0) + 3) + (VMEM,) * 2,
        scratch_shapes=[
            pltpu.VMEM((5,) + span, f32),
            pltpu.VMEM((STEPS, ext_x, ext_y, depth), f32),
            pltpu.SemaphoreType.DMA((40,)),
            pltpu.SemaphoreType.DMA((12,)),
        ],
        compiler_params=big,
        cost_estimate=pl.CostEstimate(flops=step_ops, bytes_accessed=12 * 2**20, transcendentals=0),
        name="outer_steps",
    )(*tables, src_pos, src_amp, *args, *halos, inject, *inner)
    outer_pieces, outer, edges = outer[:-5], outer[-5:-2], outer[-2:]
    edges = [lax.ppermute(edges[n], "gx", swaps_x[n]) for n in range(2)]
    field = jax.ShapeDtypeStruct(src_cur.shape, f32)

    def others(part, *operands):
        strips = middle if part == 0 else tiles - middle
        shapes = [piece(strips, g).shape for g in groups for _ in range(shots)]
        result = pl.pallas_call(
            functools.partial(rest_kernel, part, groups, shots),
            out_shape=(jax.ShapeDtypeStruct(shapes[0], f32),)
            + tuple(pltpu.HBM(shape, f32) for shape in shapes[1:])
            + (field,) * (2 - 2 * part),
            in_specs=[SMEM] * 2 + [ANY] * len(operands),
            out_specs=(VMEM,) + (ANY,) * (len(shapes) + 1 - 2 * part),
            scratch_shapes=[pltpu.VMEM(shape, f32) for shape in shapes[1:]]
            + [
                pltpu.VMEM((STEPS, 2, width_x + 2 * HALF, width_y, depth), f32),
                pltpu.SemaphoreType.DMA((21,)),
                pltpu.SemaphoreType.DMA((2 + held * shots,)),
            ],
            compiler_params=big,
            cost_estimate=pl.CostEstimate(
                flops=5 * OFFS * width_x * width_y * depth, bytes_accessed=12 * 2**20, transcendentals=0),
            name=("far_strips", "near_strips")[part],
        )(*tables, *operands)
        return result[: len(shapes)], result[len(shapes) :]

    def swapped(cells):
        return [
            lax.ppermute(one, "shot", [(s, (s + r + 1) % shots) for s in range(shots)])
            for r, one in enumerate(cells)
        ]

    long_cost = pl.CostEstimate(flops=2**37, bytes_accessed=2**28, transcendentals=0)

    def summed(kept, coming, group):
        total = []
        for part in range(2):
            cells = list(kept[part]) + list(coming[part])
            total = [
                pl.pallas_call(
                    functools.partial(sum_kernel, part, shots),
                    out_shape=piece(tiles, group),
                    in_specs=[SMEM] + [VMEM] * shots + [ANY] * part,
                    out_specs=ANY,
                    scratch_shapes=[
                        pltpu.VMEM(cells[0].shape, f32), pltpu.SemaphoreType.DMA((cells[0].shape[0],))],
                    input_output_aliases={1 + shots: 0} if part else {},
                    compiler_params=small,
                    cost_estimate=pl.CostEstimate(flops=(2**20, 2**34)[part], bytes_accessed=2**20, transcendentals=0),
                    name=("sum_far", "sum_near")[part],
                )(owner, *cells, *total)
            ]
        return total[0]

    totals = []
    coming = []
    if early:
        both = (inner_pieces, outer_pieces)
        coming = [swapped(cells[1:]) for cells in both]
        totals.append(summed([cells[:1] for cells in both], coming, first))
    far, (src_next, rcv_next) = others(0, *inner, *outer)
    near, _ = others(1, *inner, *outer, *edges, totals[0] if early else edges[0])
    for g, group in enumerate(groups):
        both = [cells[g * shots : (g + 1) * shots] for cells in (far, near)]
        going = [cells[1:] for cells in both]
        if coming:
            if g == 0 and early:
                (going[0], coming) = lax.optimization_barrier((going[0], coming))
            else:
                (going, coming) = lax.optimization_barrier((going, coming))
        coming = [swapped(cells) for cells in going]
        totals.append(summed([cells[:1] for cells in both], coming, group))
    gathers = jnp.zeros((1, held, tiles, strip_rows, width_y, depth), f32)
    chunks = ([first] if early else []) + groups
    for n, (group, total) in enumerate(zip(chunks, totals)):
        arrived = lax.all_to_all(total, ("gx", "gy"), split_axis=0, concat_axis=0, tiled=True)
        if n < len(chunks) - 1:
            for slot, i in enumerate(group):
                where = jnp.where(2 * shot < shots, held - 1 - i, i)
                gathers = lax.dynamic_update_slice(gathers, arrived[None, None, :, slot], (0, where, 0, 0, 0, 0))
            continue
        gathers = pl.pallas_call(
            functools.partial(place_kernel, group, held),
            out_shape=jax.ShapeDtypeStruct(gathers.shape, f32),
            in_specs=[ANY, VMEM],
            out_specs=ANY,
            scratch_shapes=[pltpu.SemaphoreType.DMA((len(group),))],
            input_output_aliases={0: 0},
            compiler_params=small,
            name="place_strips",
        )(gathers, arrived)
    return src_next, rcv_next, gathers


def solution(mesh):
    return jax.shard_map(
        body,
        mesh=mesh,
        in_specs=(
            P("gx", "gy", None),
            P("shot", "gx", "gy", None),
            P("shot", "gx", "gy", None),
            P("shot", "gx", "gy", None),
            P("shot", "gx", "gy", None),
            P("shot"),
            P("shot", None),
            P("shot", None),
            P("shot", None, None),
            P("shot", None),
            P(),
        ),
        out_specs=(
            P("shot", "gx", "gy", None),
            P("shot", "gx", "gy", None),
            P(("gx", "gy"), "shot", None, None, None, None),
        ),
        check_vma=False,
    )
```

time: 192 us -> 173 us (0.901)
  local copies, waits for them, and re-layouts: 19.9 us -> 10.2 us
  waiting for transfers between devices: 93.7 us -> 89.2 us
  starting transfers between devices: 38.6 us -> 36.3 us
    ppermute x3 -> x6, waiting for transfers between devices: 38.8 us -> 54 us  [swapped(): lax.ppermute(one, 'shot', [(s, (s + r + 1) % shots) for s in range(shots)])]
    all_to_all x3, waiting for transfers between devices: 43.1 us -> 32.3 us  [body(): lax.all_to_all(total, ('gx', 'gy'), split_axis=0, concat_axis=0, tiled=True)]
    unnamed x30 -> x24, local copies, waits for them, and re-layouts: 8.55 us -> 1.42 us
    ppermute x2, waiting for transfers between devices: 6.23 us -> 0.01 us  [body(): edges = [lax.ppermute(edges[n], 'gx', swaps_x[n]) for n in range(2)]]
    all_to_all x3, starting transfers between devices: 25.7 us -> 19.7 us  [body(): lax.all_to_all(total, ('gx', 'gy'), split_axis=0, concat_axis=0, tiled=True)]
    ppermute x3 -> x6, starting transfers between devices: 1.8 us -> 5.6 us  [swapped(): lax.ppermute(one, 'shot', [(s, (s + r + 1) % shots) for s in range(shots)])]
    dynamic_update_slice x8 -> x5, local copies, waits for them, and re-layouts: 8.79 us -> 6.25 us  [body(): lax.dynamic_update_slice(gathers, arrived[None, None, :, slot], (0, where...]
    pallas_call x5 -> x11, Pallas kernels: 27 us -> 29.5 us  [the longest x6 9.64 us: summed(): pl.pallas_call(functools.partial(sum_kernel, part, shots), out_shape=piec...]
  transfers between devices with their start and end apart: 14 -> 17, of which waited for: 11 -> 8; matrix products, arithmetic and copies ran while one was open for 5% -> 5% of each run, Pallas kernels for 12% -> 18%
where the time goes in v2:
time: 173 us; the launch traced here: 172 us
  waiting for transfers between devices  89.2 us (52%)
  starting transfers between devices  36.3 us (21%)
  Pallas kernels  35.1 us (20%)
  local copies, waits for them, and re-layouts  10.2 us (6%)
    ppermute x6, waiting for transfers between devices, swapped(): lax.ppermute(one, 'shot', [(s, (s + r + 1) % shots) for s in range(shots)])  54 us
    all_to_all x3, waiting for transfers between devices, body(): lax.all_to_all(total, ('gx', 'gy'), split_axis=0, concat_axis=0, tiled=True)  32.3 us
    all_to_all x3, starting transfers between devices, body(): lax.all_to_all(total, ('gx', 'gy'), split_axis=0, concat_axis=0, tiled=True)  19.7 us
    pallas_call x6, Pallas kernels, summed(): pl.pallas_call(functools.partial(sum_kernel, part, shots), out_shape=piec...  9.64 us
    pallas_call x2, Pallas kernels, others(): pl.pallas_call(functools.partial(rest_kernel, part, groups, shots), out_s...  8.09 us
    dynamic_update_slice x5, local copies, waits for them, and re-layouts, body(): lax.dynamic_update_slice(gathers, arrived[None, None, :, slot], (0, where...  6.25 us
    ppermute x6, starting transfers between devices, swapped(): lax.ppermute(one, 'shot', [(s, (s + r + 1) % shots) for s in range(shots)])  5.6 us
    pallas_call x1, Pallas kernels, body(): pl.pallas_call(functools.partial(outer_kernel, early, shots), out_shape=(...  5.49 us
  transfers between devices with their start and end apart: 17, of which 8 were waited for; matrix products, arithmetic and copies ran while one was open for 5% of the time, Pallas kernels for 18%

profile of v2, /device:TPU:11, one launch (start us, length us, event | category | flops | bytes accessed | tf_op | source)
XLA Modules:
  0.0 172.5 jit_solution(17453261517757731432)
XLA Ops:
  0.6 2.8 %pack_halos.1 = (f32[34,32,128]{2,1,0:T(8,128)}, f32[34,32,128]{2,1,0:T(8,128)}, f32[5,32,8,128]{3,2,1,0:T(8,128)}, f32[5,32,8,128]{3,2,1,0:T(8,128)}) custom-call(f32[32,32,128]{2,1,0:T(8,128)} %vel.5, f32[1,32,32,128]{3,2,1,0:T(8,128)} %src_prev.5, f32[1,32,32,128]{3,2,1,0:T(8,128)} %src_cur.5, f32[1,32,32,128]{3,2,1,0:T(8,128)} %rcv_prev.5, ...), custom_call_target="tpu_custom_call" | custom-call | tf_op jit(solution)/shard_map/pack_halos/pallas_call | solution.py:498
  5.2 4.3 %collective-permute-start.3 = (f32[34,32,128]{2,1,0:T(8,128)}, f32[34,32,128]{2,1,0:T(8,128)S(1)}, u32[]{:S(2)}, u32[]{:S(2)}) collective-permute-start(f32[34,32,128]{2,1,0:T(8,128)} %get-tuple-element.40), channel_id=1, source_target_pairs={{4,8},{8,4},{5,9},{9,5},{6,10},{10,6},{7,11},{11,7},{20,24},{24,20... | collective-permute-start | bytes 1671176 | tf_op jit(solution)/shard_map/ppermute | solution.py:508
  10.9 2.6 %spread_receivers.1 = f32[3,1760,128]{2,1,0:T(8,128)S(1)} custom-call(s32[1,512]{1,0:T(1,128)S(1)} %copy-done.11, f32[1,1536]{1,0:T(1,128)S(1)} %bitcast.35), custom_call_target="tpu_custom_call" | custom-call | flops 2076180480 | bytes 2703360 | tf_op jit(solution)/shard_map/spread_receivers/pallas_call | solution.py:512
  13.8 1.9 %collective-permute-start.5 = (f32[2,5,6,8,128]{4,3,2,1,0:T(8,128)S(1)}, f32[2,5,6,8,128]{4,3,2,1,0:T(8,128)S(1)}, u32[]{:S(2)}, u32[]{:S(2)}) collective-permute-start(f32[2,5,6,8,128]{4,3,2,1,0:T(8,128)S(1)} %get-tuple-element.42), channel_id=1, source_target_pairs={{4,8},{8,4},{5,9},{9,5},{6,10},{10,6},{7,11},{11,7},{20,24},{24,20... | collective-permute-start | bytes 737288 | tf_op jit(solution)/shard_map/ppermute | solution.py:535
  16.5 5.1 %inner_steps.1 = (f32[8,2,2,32,128]{4,3,2,1,0:T(8,128)S(1)}, f32[8,2,2,32,128]{4,3,2,1,0:T(8,128)S(1)}, f32[2,48,48,128]{3,2,1,0:T(8,128)S(1)}, f32[2,48,48,128]{3,2,1,0:T(8,128)S(1)}, f32[2,48,48,128]{3,2,1,0:T(8,128)S(1)}) custom-call(s32[16,16]{1,0:T(8,128)S(1)} %copy-done.6, s32[1,8]{1,0:T(1,128)S(1)} %copy-done.7, s32[1]{0:T(128)S(6)} %copy.39.src_pos, ...), custom_call_target="tpu_custom_call" | custom-call | flops 11796480 | bytes 12582912 | tf_op jit(solution)/shard_map/inner_steps/pallas_call | solution.py:549
  22.9 2.8 %collective-permute-done.5.c1 = f32[2,5,6,8,128]{4,3,2,1,0:T(8,128)S(1)} collective-permute-done((f32[2,5,6,8,128]{4,3,2,1,0:T(8,128)S(1)}, f32[2,5,6,8,128]{4,3,2,1,0:T(8,128)S(1)}, u32[]{:S(2)}, u32[]{:S(2)}) %collective-permute-start.5) | collective-permute-done | bytes 245792 | tf_op jit(solution)/shard_map/ppermute | solution.py:535
  25.7 5.5 %outer_steps.1 = (f32[8,2,2,32,128]{4,3,2,1,0:T(8,128)S(1)}, f32[8,2,2,32,128]{4,3,2,1,0:T(8,128)S(1)}, f32[2,48,48,128]{3,2,1,0:T(8,128)S(1)}, f32[2,48,48,128]...) custom-call(s32[16,16]{1,0:T(8,128)S(1)} %copy-done.6, ...), custom_call_target="tpu_custom_call" | custom-call | flops 11796480 | bytes 12582912 | tf_op jit(solution)/shard_map/outer_steps/pallas_call | solution.py:564
  32.6 3.1 %collective-permute-start.9 = (f32[24,32,128]{2,1,0:T(8,128)S(1)}, f32[24,32,128]{2,1,0:T(8,128)S(1)}, u32[]{:S(2)}, u32[]{:S(2)}) collective-permute-start(f32[24,32,128]{2,1,0:T(8,128)S(1)} %get-tuple-element.53), channel_id=1, source_target_pairs={{4,8},{8,4},{5,9},{9,5},{6,10},{10,6},{7,11},{11,7},{20,24},{24,20... | collective-permute-start | bytes 1179656 | tf_op jit(solution)/shard_map/ppermute | solution.py:580
  35.6 3.6 %far_strips.1 = (f32[8,3,2,32,128]{4,3,2,1,0:T(8,128)S(1)}, f32[8,3,2,32,128]{4,3,2,1,0:T(8,128)}, f32[8,3,2,32,128]{4,3,2,1,0:T(8,128)}, f32[8,3,2,32,128]{4,3,...) custom-call(s32[16,16]{1,0:T(8,128)S(1)} %copy-done.6, s32[1,8]{1,0:T(1,128)S(1)} %copy-done.7, ...), custom_call_target="tpu_custom_call" | custom-call | flops 10485760 | bytes 12582912 | tf_op jit(solution)/shard_map/far_strips/pallas_call | solution.py:586
  40.8 4.5 %collective-permute-done.6.refs_1_ = f32[8,2,2,32,128]{4,3,2,1,0:T(8,128)S(1)} collective-permute-done((f32[8,2,2,32,128]{4,3,2,1,0:T(8,128)S(1)}, f32[8,2,2,32,128]{4,3,2,1,0:T(8,128)S(1)}, u32[]{:S(2)}, u32[]{:S(2)}) %collective-permute-start.6) | collective-permute-done | bytes 524320 | tf_op jit(solution)/shard_map/ppermute | solution.py:608
  48.1 4.5 %near_strips.1 = (f32[8,3,2,32,128]{4,3,2,1,0:T(8,128)S(1)}, f32[8,3,2,32,128]{4,3,2,1,0:T(8,128)}, f32[8,3,2,32,128]{4,3,2,1,0:T(8,128)}, f32[8,3,2,32,128]{4,3,2,1,0:T(8,128)}) custom-call(s32[16,16]{1,0:T(8,128)S(1)} %copy-done.6, s32[1,8]{1,0:T(1,128)S(1)} %copy-done.7, f32[2,48,48,128]{3,2,1,0:T(8,128)S(1)} %get-tuple-element.36.i1, ...), custom_call_target="tpu_custom_call" | custom-call | flops 10485760 | bytes 12582912 | tf_op jit(solution)/shard_map/near_strips/pallas_call | solution.py:586
  52.9 7.5 %all-to-all-start = ((f32[16,2,2,32,128]{4,3,2,1,0:T(8,128)}), f32[16,2,2,32,128]{4,3,2,1,0:T(8,128)}, u32[]{:S(2)}, u32[]{:S(2)}) async-start(f32[16,2,2,32,128]{4,3,2,1,0:T(8,128)} %sum_near.3.rest_2_), calls=%async_computation | async-start | bytes 2097152 | tf_op jit(solution)/shard_map/all_to_all | solution.py:655
  63.5 15.3 %collective-permute-done.10.refs_1_ = f32[8,3,2,32,128]{4,3,2,1,0:T(8,128)S(1)} collective-permute-done((f32[8,3,2,32,128]{4,3,2,1,0:T(8,128)}, f32[8,3,2,32,128]{4,3,2,1,0:T(8,128)S(1)}, u32[]{:S(2)}, u32[]{:S(2)}) %collective-permute-start.10) | collective-permute-done | bytes 786464 | tf_op jit(solution)/shard_map/ppermute | solution.py:608
  80.5 4.9 %all-to-all-done = f32[16,2,2,32,128]{4,3,2,1,0:T(8,128)} async-done(((f32[16,2,2,32,128]{4,3,2,1,0:T(8,128)}), f32[16,2,2,32,128]{4,3,2,1,0:T(8,128)}, u32[]{:S(2)}, u32[]{:S(2)}) %all-to-all-start) | async-done | bytes 1048608 | tf_op jit(solution)/shard_map/all_to_all | solution.py:655
  85.4 5.4 %all-to-all-start.1 = ((f32[16,3,2,32,128]{4,3,2,1,0:T(8,128)}), f32[16,3,2,32,128]{4,3,2,1,0:T(8,128)S(1)}, u32[]{:S(2)}, u32[]{:S(2)}) async-start(f32[16,3,2,32,128]{4,3,2,1,0:T(8,128)} %sum_near.4), calls=%async_computation.1 | async-start | bytes 3145728 | tf_op jit(solution)/shard_map/all_to_all | solution.py:655
  92.2 17.5 %collective-permute-done.13.refs_1_ = f32[8,3,2,32,128]{4,3,2,1,0:T(8,128)S(1)} collective-permute-done((f32[8,3,2,32,128]{4,3,2,1,0:T(8,128)}, f32[8,3,2,32,128]{4,3,2,1,0:T(8,128)S(1)}, u32[]{:S(2)}, u32[]{:S(2)}) %collective-permute-start.13) | collective-permute-done | bytes 786464 | tf_op jit(solution)/shard_map/ppermute | solution.py:608
  109.7 1.7 sum_far.5.refs_2_
  111.4 15.2 %collective-permute-done.12.refs_1_ = f32[8,3,2,32,128]{4,3,2,1,0:T(8,128)S(1)} collective-permute-done((f32[8,3,2,32,128]{4,3,2,1,0:T(8,128)}, f32[8,3,2,32,128]{4,3,2,1,0:T(8,128)S(1)}, u32[]{:S(2)}, u32[]{:S(2)}) %collective-permute-start.12) | collective-permute-done | bytes 786464 | tf_op jit(solution)/shard_map/ppermute | solution.py:608
  126.6 1.7 sum_near.5
  128.3 6.8 %all-to-all-start.2 = ((f32[16,3,2,32,128]{4,3,2,1,0:T(8,128)}), f32[16,3,2,32,128]{4,3,2,1,0:T(8,128)S(1)}, u32[]{:S(2)}, u32[]{:S(2)}) async-start(f32[16,3,2,32,128]{4,3,2,1,0:T(8,128)} %sum_near.5), calls=%async_computation.2 | async-start | bytes 3145728 | tf_op jit(solution)/shard_map/all_to_all | solution.py:655
  135.1 2.5 %broadcast_in_dim.3 = f32[1,8,16,2,32,128]{5,4,3,2,1,0:T(8,128)} broadcast(f32[]{:T(128)} %constant.11.clone.1), dimensions={} | broadcast | bytes 4194308 | tf_op jit(solution)/shard_map/broadcast_in_dim | solution.py:652
  137.7 1.9 %fusion.4 = f32[1,8,16,2,32,128]{5,4,3,2,1,0:T(8,128)} fusion(f32[1,8,16,2,32,128]{5,4,3,2,1,0:T(8,128)} %broadcast_in_dim.3, s32[]{:T(128)S(6)} %select_n.21, f32[16,2,2,32,128]{4,3,2,1,0:T(8,128)} %all-to-all-done), kind=kLoop, calls=%fused_computation.9 | loop fusion | bytes 1048580 | tf_op jit(solution)/shard_map/dynamic_update_slice | solution.py:659
  139.5 1.9 %fusion.3 = f32[1,8,16,2,32,128]{5,4,3,2,1,0:T(8,128)} fusion(f32[1,8,16,2,32,128]{5,4,3,2,1,0:T(8,128)} %fusion.4, s32[]{:T(128)S(6)} %select_n.22, f32[16,2,2,32,128]{4,3,2,1,0:T(8,128)} %all-to-all-done), kind=kLoop, calls=%fused_computation.7 | loop fusion | bytes 1048580 | tf_op jit(solution)/shard_map/dynamic_update_slice | solution.py:659
  143.9 27.4 %all-to-all-done.2.piece = f32[16,3,2,32,128]{4,3,2,1,0:T(8,128)S(1)} async-done(((f32[16,3,2,32,128]{4,3,2,1,0:T(8,128)}), f32[16,3,2,32,128]{4,3,2,1,0:T(8,128)S(1)}, u32[]{:S(2)}, u32[]{:S(2)}) %all-to-all-start.2) | async-done | bytes 1572896 | tf_op jit(solution)/shard_map/all_to_all | solution.py:655
  (54 shorter events, 20.4 us)
Async XLA Ops:
  3.5 10.0 %collective-permute-start = (f32[5,32,8,128]{3,2,1,0:T(8,128)}, f32[5,32,8,128]{3,2,1,0:T(8,128)S(1)}, u32[]{:S(2)}, u32[]{:S(2)}) collective-permute-start(f32[5,32,8,128]{3,2,1,0:T(8,128)} %get-tuple-element.34), channel_id=1, source_target_pairs={{0,1},{1,0},{2,3},{3,2},{4,5},{5,4},{6,7},{7,6},{8,9},{9,8},{10,11... | collective-permute-start | bytes 1966088 | tf_op jit(solution)/shard_map/ppermute | solution.py:509
  4.2 9.3 %collective-permute-start.1 = (f32[5,32,8,128]{3,2,1,0:T(8,128)}, f32[5,32,8,128]{3,2,1,0:T(8,128)S(1)}, u32[]{:S(2)}, u32[]{:S(2)}) collective-permute-start(f32[5,32,8,128]{3,2,1,0:T(8,128)} %get-tuple-element.35), channel_id=1, source_target_pairs={{1,2},{2,1},{5,6},{6,5},{9,10},{10,9},{13,14},{14,13},{17,18},{18,... | collective-permute-start | bytes 1966088 | tf_op jit(solution)/shard_map/ppermute | solution.py:509
  4.9 18.0 %collective-permute-start.2 = (f32[34,32,128]{2,1,0:T(8,128)}, f32[34,32,128]{2,1,0:T(8,128)S(1)}, u32[]{:S(2)}, u32[]{:S(2)}) collective-permute-start(f32[34,32,128]{2,1,0:T(8,128)} %get-tuple-element.39), channel_id=1, source_target_pairs={{0,4},{4,0},{8,12},{12,8},{1,5},{5,1},{9,13},{13,9},{2,6},{6,2},{1... | collective-permute-start | bytes 1671176 | tf_op jit(solution)/shard_map/ppermute | solution.py:508
  5.2 17.7 %collective-permute-start.3 = (f32[34,32,128]{2,1,0:T(8,128)}, f32[34,32,128]{2,1,0:T(8,128)S(1)}, u32[]{:S(2)}, u32[]{:S(2)}) collective-permute-start(f32[34,32,128]{2,1,0:T(8,128)} %get-tuple-element.40), channel_id=1, source_target_pairs={{4,8},{8,4},{5,9},{9,5},{6,10},{10,6},{7,11},{11,7},{20,24},{24,20... | collective-permute-start | bytes 1671176 | tf_op jit(solution)/shard_map/ppermute | solution.py:508
  10.9 5.6 %copy-start.3 = (f32[1,32,32,128]{3,2,1,0:T(8,128)S(1)}, f32[1,32,32,128]{3,2,1,0:T(8,128)}, u32[]{:S(2)}) copy-start(f32[1,32,32,128]{3,2,1,0:T(8,128)} %rcv_prev.5) | copy-start | bytes 1572868
  10.9 5.6 %copy-start.4 = (f32[1,32,32,128]{3,2,1,0:T(8,128)S(1)}, f32[1,32,32,128]{3,2,1,0:T(8,128)}, u32[]{:S(2)}) copy-start(f32[1,32,32,128]{3,2,1,0:T(8,128)} %rcv_cur.5) | copy-start | bytes 1572868
  10.9 5.6 %copy-start.6 = (s32[16,16]{1,0:T(8,128)S(1)}, s32[16,16]{1,0:T(8,128)}, u32[]{:S(2)}) copy-start(s32[16,16]{1,0:T(8,128)} %owner.19) | copy-start | bytes 3076
  10.9 5.6 %copy-start.7 = (s32[1,8]{1,0:T(1,128)S(1)}, s32[1,8]{1,0:T(1,128)}, u32[]{:S(2)}) copy-start(s32[1,8]{1,0:T(1,128)} %aperture.7) | copy-start | bytes 100
  10.9 5.6 %copy-start.8 = (f32[1,3]{1,0:T(1,128)S(1)}, f32[1,3]{1,0:T(1,128)}, u32[]{:S(2)}) copy-start(f32[1,3]{1,0:T(1,128)} %amps.3) | copy-start | bytes 40
  13.7 9.2 %collective-permute-start.4 = (f32[2,5,6,8,128]{4,3,2,1,0:T(8,128)S(1)}, f32[2,5,6,8,128]{4,3,2,1,0:T(8,128)S(1)}, u32[]{:S(2)}, u32[]{:S(2)}) collective-permute-start(f32[2,5,6,8,128]{4,3,2,1,0:T(8,128)S(1)} %get-tuple-element.41), channel_id=1, source_target_pairs={{0,4},{4,0},{8,12},{12,8},{1,5},{5,1},{9,13},{13,9},{2,6},{6,2},{1... | collective-permute-start | bytes 737288 | tf_op jit(solution)/shard_map/ppermute | solution.py:535
  13.8 11.9 %collective-permute-start.5 = (f32[2,5,6,8,128]{4,3,2,1,0:T(8,128)S(1)}, f32[2,5,6,8,128]{4,3,2,1,0:T(8,128)S(1)}, u32[]{:S(2)}, u32[]{:S(2)}) collective-permute-start(f32[2,5,6,8,128]{4,3,2,1,0:T(8,128)S(1)} %get-tuple-element.42), channel_id=1, source_target_pairs={{4,8},{8,4},{5,9},{9,5},{6,10},{10,6},{7,11},{11,7},{20,24},{24,20... | collective-permute-start | bytes 737288 | tf_op jit(solution)/shard_map/ppermute | solution.py:535
  21.6 17.7 %collective-permute-start.7 = (f32[8,2,2,32,128]{4,3,2,1,0:T(8,128)S(1)}, f32[8,2,2,32,128]{4,3,2,1,0:T(8,128)S(1)}, u32[]{:S(2)}, u32[]{:S(2)}) collective-permute-start(f32[8,2,2,32,128]{4,3,2,1,0:T(8,128)S(1)} %get-tuple-element.51), channel_id=1, source_target_pairs={{0,16},{16,0},{1,17},{17,1},{2,18},{18,2},{3,19},{19,3},{4,20},{20... | collective-permute-start | bytes 1572872 | tf_op jit(solution)/shard_map/ppermute | solution.py:608
  31.2 14.1 %collective-permute-start.6 = (f32[8,2,2,32,128]{4,3,2,1,0:T(8,128)S(1)}, f32[8,2,2,32,128]{4,3,2,1,0:T(8,128)S(1)}, u32[]{:S(2)}, u32[]{:S(2)}) collective-permute-start(f32[8,2,2,32,128]{4,3,2,1,0:T(8,128)S(1)} %get-tuple-element.49), channel_id=1, source_target_pairs={{0,16},{16,0},{1,17},{17,1},{2,18},{18,2},{3,19},{19,3},{4,20},{20... | collective-permute-start | bytes 1572872 | tf_op jit(solution)/shard_map/ppermute | solution.py:608
  32.5 15.6 %collective-permute-start.8 = (f32[24,32,128]{2,1,0:T(8,128)S(1)}, f32[24,32,128]{2,1,0:T(8,128)S(1)}, u32[]{:S(2)}, u32[]{:S(2)}) collective-permute-start(f32[24,32,128]{2,1,0:T(8,128)S(1)} %get-tuple-element.52), channel_id=1, source_target_pairs={{0,4},{4,0},{8,12},{12,8},{1,5},{5,1},{9,13},{13,9},{2,6},{6,2},{1... | collective-permute-start | bytes 1179656 | tf_op jit(solution)/shard_map/ppermute | solution.py:580
  32.6 15.6 %collective-permute-start.9 = (f32[24,32,128]{2,1,0:T(8,128)S(1)}, f32[24,32,128]{2,1,0:T(8,128)S(1)}, u32[]{:S(2)}, u32[]{:S(2)}) collective-permute-start(f32[24,32,128]{2,1,0:T(8,128)S(1)} %get-tuple-element.53), channel_id=1, source_target_pairs={{4,8},{8,4},{5,9},{9,5},{6,10},{10,6},{7,11},{11,7},{20,24},{24,20... | collective-permute-start | bytes 1179656 | tf_op jit(solution)/shard_map/ppermute | solution.py:580
  45.3 16.6 %collective-permute-start.11 = (f32[8,3,2,32,128]{4,3,2,1,0:T(8,128)}, f32[8,3,2,32,128]{4,3,2,1,0:T(8,128)S(1)}, u32[]{:S(2)}, u32[]{:S(2)}) collective-permute-start(f32[8,3,2,32,128]{4,3,2,1,0:T(8,128)} %get-tuple-element.58), channel_id=1, source_target_pairs={{0,16},{16,0},{1,17},{17,1},{2,18},{18,2},{3,19},{19,3},{4,20},{20... | collective-permute-start | bytes 2359304 | tf_op jit(solution)/shard_map/ppermute | solution.py:608
  52.6 26.3 %collective-permute-start.10 = (f32[8,3,2,32,128]{4,3,2,1,0:T(8,128)}, f32[8,3,2,32,128]{4,3,2,1,0:T(8,128)S(1)}, u32[]{:S(2)}, u32[]{:S(2)}) collective-permute-start(f32[8,3,2,32,128]{4,3,2,1,0:T(8,128)} %get-tuple-element.55), channel_id=1, source_target_pairs={{0,16},{16,0},{1,17},{17,1},{2,18},{18,2},{3,19},{19,3},{4,20},{20... | collective-permute-start | bytes 2359304 | tf_op jit(solution)/shard_map/ppermute | solution.py:608
  52.9 32.5 %all-to-all-start = ((f32[16,2,2,32,128]{4,3,2,1,0:T(8,128)}), f32[16,2,2,32,128]{4,3,2,1,0:T(8,128)}, u32[]{:S(2)}, u32[]{:S(2)}) async-start(f32[16,2,2,32,128]{4,3,2,1,0:T(8,128)} %sum_near.3.rest_2_), calls=%async_computation | async-start | bytes 2097152 | tf_op jit(solution)/shard_map/all_to_all | solution.py:655
  78.9 30.9 %copy-start.5 = (f32[8,3,2,32,128]{4,3,2,1,0:T(8,128)S(1)}, f32[8,3,2,32,128]{4,3,2,1,0:T(8,128)}, u32[]{:S(2)}) copy-start(f32[8,3,2,32,128]{4,3,2,1,0:T(8,128)} %get-tuple-element.63.refs_0_) | copy-start | bytes 2359300
  80.5 46.1 %copy-start.9 = (f32[8,3,2,32,128]{4,3,2,1,0:T(8,128)S(1)}, f32[8,3,2,32,128]{4,3,2,1,0:T(8,128)}, u32[]{:S(2)}) copy-start(f32[8,3,2,32,128]{4,3,2,1,0:T(8,128)} %get-tuple-element.59.refs_0_) | copy-start | bytes 2359300
  85.4 42.9 %all-to-all-start.1 = ((f32[16,3,2,32,128]{4,3,2,1,0:T(8,128)}), f32[16,3,2,32,128]{4,3,2,1,0:T(8,128)S(1)}, u32[]{:S(2)}, u32[]{:S(2)}) async-start(f32[16,3,2,32,128]{4,3,2,1,0:T(8,128)} %sum_near.4), calls=%async_computation.1 | async-start | bytes 3145728 | tf_op jit(solution)/shard_map/all_to_all | solution.py:655
  90.8 19.0 %collective-permute-start.13 = (f32[8,3,2,32,128]{4,3,2,1,0:T(8,128)}, f32[8,3,2,32,128]{4,3,2,1,0:T(8,128)S(1)}, u32[]{:S(2)}, u32[]{:S(2)}) collective-permute-start(f32[8,3,2,32,128]{4,3,2,1,0:T(8,128)} %get-tuple-element.64), channel_id=1, source_target_pairs={{0,16},{16,0},{1,17},{17,1},{2,18},{18,2},{3,19},{19,3},{4,20},{20... | collective-permute-start | bytes 2359304 | tf_op jit(solution)/shard_map/ppermute | solution.py:608
  92.0 34.6 %collective-permute-start.12 = (f32[8,3,2,32,128]{4,3,2,1,0:T(8,128)}, f32[8,3,2,32,128]{4,3,2,1,0:T(8,128)S(1)}, u32[]{:S(2)}, u32[]{:S(2)}) collective-permute-start(f32[8,3,2,32,128]{4,3,2,1,0:T(8,128)} %get-tuple-element.62), channel_id=1, source_target_pairs={{0,16},{16,0},{1,17},{17,1},{2,18},{18,2},{3,19},{19,3},{4,20},{20... | collective-permute-start | bytes 2359304 | tf_op jit(solution)/shard_map/ppermute | solution.py:608
  128.3 43.0 %all-to-all-start.2 = ((f32[16,3,2,32,128]{4,3,2,1,0:T(8,128)}), f32[16,3,2,32,128]{4,3,2,1,0:T(8,128)S(1)}, u32[]{:S(2)}, u32[]{:S(2)}) async-start(f32[16,3,2,32,128]{4,3,2,1,0:T(8,128)} %sum_near.5), calls=%async_computation.2 | async-start | bytes 3145728 | tf_op jit(solution)/shard_map/all_to_all | solution.py:655
  (5 other events, 18.0 us)

commit v3 on v2

--- a/solution.py
+++ b/solution.py
@@ -50,18 +50,32 @@
     return pl.multiple_of(jnp.where(condition, upper, lower), multiple)
 
 
-def pack_kernel(vel, src_prev, src_cur, rcv_prev, rcv_cur, x0, x1, y0, y1, *scratch):
+Y_PLACES = ((PAD, 0, 0), (PAD, 1, 0), (PAD // 2, 2, 0), (PAD // 2, 2, PAD // 2), (PAD, 3, 0))
+Y_TILES = 4
+
+
+def pack_kernel(
+    positions_from, values_from, vel, src_prev, src_cur, rcv_prev, rcv_cur, x0, x1, y0, y1, positions, values, *scratch
+):
     *buffers, sems, out_sems = scratch
+    small = [
+        pltpu.make_async_copy(positions_from, positions, sems.at[20]),
+        pltpu.make_async_copy(values_from, values, sems.at[21]),
+    ]
     width_x, width_y, depth = vel.shape
     fields = (src_cur.at[0], rcv_cur.at[0], src_prev.at[0], rcv_prev.at[0], vel)
     jobs = []
     count = 0
     for swap in range(2):
-        start = pick(is_upper("gy", swap), width_y - PAD, 0, PAD)
         copies = []
         for n, field in enumerate(fields):
+            cols, tile, col = Y_PLACES[n]
+            start = pick(is_upper("gy", swap), width_y - cols, 0, cols)
             copies.append(
-                pltpu.make_async_copy(field.at[:, pl.ds(start, PAD)], buffers[2 + swap].at[n], sems.at[count])
+                pltpu.make_async_copy(
+                    field.at[:, pl.ds(start, cols)], buffers[2 + swap].at[tile, :, pl.ds(col, cols)],
+                    sems.at[count],
+                )
             )
             count += 1
         jobs.append((copies, buffers[2 + swap], (y0, y1)[swap]))
@@ -78,7 +92,7 @@
             row += rows
             count += 1
         jobs.append((copies, buffers[swap], (x0, x1)[swap]))
-    for copies, _, _ in jobs:
+    for copies in [copies for copies, _, _ in jobs] + [small]:
         for copy in copies:
             copy.start()
     sends = []
@@ -87,7 +101,7 @@
             copy.wait()
         sends.append(pltpu.make_async_copy(buffer, out, out_sems.at[n]))
         sends[-1].start()
-    for copy in sends:
+    for copy in small + sends:
         copy.wait()
 
 
@@ -112,7 +126,15 @@
     return x, y, lax.rem(position, depth), inside
 
 
-def spread_kernel(width_x, width_y, positions, values, out):
+def spread_kernel(positions, values, vel, src_prev, src_cur, rcv_prev, rcv_cur, out, ext, sems):
+    width_x, width_y, _ = vel.shape
+    fields = (src_cur.at[0], rcv_cur.at[0], src_prev.at[0], rcv_prev.at[0], vel)
+    others = [
+        pltpu.make_async_copy(field, ext.at[n, pl.ds(PAD, width_x), pl.ds(PAD, width_y)], sems.at[n])
+        for n, field in enumerate(fields)
+    ]
+    for copy in others:
+        copy.start()
     rows, depth = out.shape[1], out.shape[2]
     receivers = positions.shape[1]
     x, y, depths, inside = locate(positions[...], width_x, width_y, depth)
@@ -139,6 +161,8 @@
             total[:, (n * STEPS + t) * depth : (n * STEPS + t + 1) * depth] for n in range(3)
         )
         out[t] = high + (middle + low)
+    for copy in others:
+        copy.wait()
 
 
 def depth_matrix(depth):
@@ -226,10 +250,6 @@
     return (PAD - VALID[t], first + VALID[t] - PAD), (first + count, PAD + width_x + VALID[t] - first - count)
 
 
-def rims(width_x):
-    return (PAD + 2, PAD), (width_x - 2, PAD)
-
-
 class Sources:
     def __init__(self, src_pos, amps, shape):
         width_x, width_y, depth = shape
@@ -247,38 +267,37 @@
             out[self.row, pl.ds(self.col, 1), :] = cells + jnp.where(self.lane == self.depth, self.amps[0, t], 0.0)
 
 
+def tile_shape(ext):
+    return ext.shape[1] - 2 * PAD, ext.shape[2] - 2 * PAD, ext.shape[3]
+
+
 def column_window(t, width_y):
     return (PAD, width_y) if t == STEPS - 1 else (PAD // 2, width_y + PAD)
 
 
-def inner_kernel(
-    early, shots, owner, aperture, src_pos, amps,
-    vel, src_prev, src_cur, rcv_prev, rcv_cur, y0, y1, inject_from, *rest
-):
+def inner_kernel(early, shots, owner, aperture, src_pos, amps, y0, y1, inject, ext_in, *rest):
     count = shots if early else 0
-    outs, (s1, s2, s3, ext, inject, sems) = rest[:count], rest[count:]
-    width_x, width_y, depth = vel.shape
+    outs, (ext, s1, s2, s3, sems) = rest[:count], rest[count:]
+    width_x, width_y, depth = tile_shape(ext)
     inner_y = pl.ds(PAD, width_y)
     copies = []
-
-    def add(src, dst):
-        copies.append(pltpu.make_async_copy(src, dst, sems.at[len(copies)]))
-
     for swap, halo in enumerate((y0, y1)):
-        col = pick(is_upper("gy", swap), PAD + width_y, 0, PAD)
-        add(halo, ext.at[:, pl.ds(PAD, width_x), pl.ds(col, PAD)])
-    for n, field in ((0, src_cur.at[0]), (2, src_prev.at[0]), (4, vel), (1, rcv_cur.at[0]), (3, rcv_prev.at[0])):
-        add(field, ext.at[n, pl.ds(PAD, width_x), inner_y])
-    used = pl.ds(PAD, width_x - 4)
-    add(inject_from.at[:, used], inject.at[:, used])
+        for n, (cols, tile, col) in enumerate(Y_PLACES):
+            to = pick(is_upper("gy", swap), PAD + width_y, PAD - cols, cols)
+            copies.append(
+                pltpu.make_async_copy(
+                    halo.at[tile, :, pl.ds(col, cols)], ext.at[n, pl.ds(PAD, width_x), pl.ds(to, cols)],
+                    sems.at[len(copies)],
+                )
+            )
     for copy in copies:
         copy.start()
     keep = is_active(aperture)
     matrix = depth_matrix(depth)
-    source = Sources(src_pos, amps, vel.shape)
+    source = Sources(src_pos, amps, (width_x, width_y, depth))
+    for copy in copies:
+        copy.wait()
     for f in range(2):
-        for copy in copies[5:] if f else copies[:5]:
-            copy.wait()
         fields = [ext.at[f], s1.at[f], s2.at[f], s3.at[f]]
         for t in range(STEPS):
             prev = ext.at[2 + f] if t == 0 else fields[t - 1]
@@ -299,48 +318,35 @@
 
 
 def outer_kernel(
-    early, shots, owner, aperture, src_pos, amps,
-    vel, src_prev, src_cur, rcv_prev, rcv_cur, x0, x1, y0, y1, c0, c1, inject_from, i1, i2, i3, *rest
+    early, shots, owner, aperture, src_pos, amps, x0, x1, c0, c1, inject, ext_in, in1, in2, in3, *rest
 ):
     count = shots if early else 0
-    outs, (s1, s2, s3, edge0, edge1, ext, inject, sems, out_sems) = rest[:count], rest[count:]
-    width_x, width_y, depth = vel.shape
+    outs, (ext, s1, s2, s3, edge0, edge1, sems, out_sems) = rest[:count], rest[count:]
+    width_x, width_y, depth = tile_shape(ext)
     inner_y = pl.ds(PAD, width_y)
     copies = []
 
     def add(src, dst):
         copies.append(pltpu.make_async_copy(src, dst, sems.at[len(copies)]))
 
-    for swap, halo in enumerate((y0, y1)):
-        col = pick(is_upper("gy", swap), PAD + width_y, 0, PAD)
-        for first in (0, width_x - PAD):
-            add(halo.at[:, pl.ds(first, PAD)], ext.at[:, pl.ds(PAD + first, PAD), pl.ds(col, PAD)])
     for swap, corner in enumerate((c0, c1)):
         start = pick(is_upper("gx", swap), PAD + width_x, PAD - CORNER)
-        for n in range(2):
-            col = pick(is_upper("gy", n), PAD + width_y, 0, PAD)
-            add(corner.at[n], ext.at[:, pl.ds(start, CORNER), pl.ds(col, PAD)])
+        for side in range(2):
+            for n, (cols, tile, col) in enumerate(Y_PLACES):
+                to = pick(is_upper("gy", side), PAD + width_y, PAD - cols, cols)
+                add(corner.at[side, tile, :, pl.ds(col, cols)], ext.at[n, pl.ds(start, CORNER), pl.ds(to, cols)])
     row = 0
-    fields = (src_cur.at[0], rcv_cur.at[0], src_prev.at[0], rcv_prev.at[0], vel)
     for n in range(5):
         rows = HALF if n < 2 else VALID[0]
         for swap, halo in enumerate((x0, x1)):
             start = pick(is_upper("gx", swap), PAD + width_x, PAD - rows)
             add(halo.at[pl.ds(row, rows)], ext.at[n, pl.ds(start, rows), inner_y])
-        for first in (0, width_x - PAD):
-            add(fields[n].at[pl.ds(first, PAD)], ext.at[n, pl.ds(PAD + first, PAD), inner_y])
         row += rows
-    for first, rows in rims(width_x):
-        for inner, step in ((i1, s1), (i2, s2), (i3, s3)):
-            add(inner.at[:, pl.ds(first, rows)], step.at[:, pl.ds(first, rows)])
-    for first in (0, inject.shape[1] - 12):
-        used = pl.ds(first, 12)
-        add(inject_from.at[:, used], inject.at[:, used])
     for copy in copies:
         copy.start()
     keep = is_active(aperture)
     matrix = depth_matrix(depth)
-    source = Sources(src_pos, amps, vel.shape)
+    source = Sources(src_pos, amps, (width_x, width_y, depth))
     for copy in copies:
         copy.wait()
     chain = [[ext.at[f], s1.at[f], s2.at[f], s3.at[f]] for f in range(2)]
@@ -388,33 +394,31 @@
     return lambda n: n + jnp.where(n < side, 0, middle), 2 * side
 
 
-def rest_kernel(part, groups, shots, owner, aperture, i1, i2, i3, o1, o2, o3, *rest):
-    edges, rest = rest[: 3 * part], rest[3 * part :]
+def rest_kernel(part, groups, shots, owner, aperture, *rest):
     count = len(groups) * shots
-    results, rest = rest[:count], rest[count:]
-    last, rest = rest[: 2 - 2 * part], rest[2 - 2 * part :]
-    outs, (held, sems, out_sems) = (results[0], *rest[: count - 1]), rest[count - 1 :]
-    width_x = held.shape[2] - 2 * HALF
-    inner_y = pl.ds(PAD, held.shape[3])
+    if part == 0:
+        (s1, s2, s3), rest = rest[:3], rest[3:]
+        results, last, rest = rest[:count], rest[count : count + 2], rest[count + 2 :]
+    else:
+        edges, rest = rest[:2], rest[6:]
+        results, (s1, s2, s3), last, rest = rest[:count], rest[count : count + 3], (), rest[count + 3 :]
+    outs, (sems, out_sems) = (results[0], *rest[: count - 1]), rest[count - 1 :]
+    steps = (s1, s2, s3)
+    width_x, width_y, _ = tile_shape(s1)
+    inner_y = pl.ds(PAD, width_y)
     copies = []
-
-    def add(src, dst):
-        copies.append(pltpu.make_async_copy(src, dst, sems.at[len(copies)]))
-
-    (low, rim), (high, _) = rims(width_x)
     row = 0
-    for t, (inner, outer) in enumerate(((i1, o1), (i2, o2), (i3, o3))):
-        reach = VALID[t] if part else 0
+    for t in range(STEPS):
         rows = HALF - VALID[t]
-        middle = pl.ds(low + rim, high - low - rim)
-        spans = (pl.ds(PAD - reach, low + rim - PAD + reach), pl.ds(high, PAD + width_x + reach - high))
-        add(inner.at[:, middle, inner_y], held.at[t, :, middle])
-        for span in spans:
-            add(outer.at[:, span, inner_y], held.at[t, :, span])
         for f in range(2 * part):
-            for swap, edge in enumerate(edges[:2]):
-                start = pick(is_upper("gx", swap), HALF + width_x + reach, 0)
-                add(edge.at[pl.ds(row, rows)], held.at[t, f, pl.ds(start, rows)])
+            for swap, edge in enumerate(edges):
+                start = pick(is_upper("gx", swap), PAD + width_x + VALID[t], 0)
+                copies.append(
+                    pltpu.make_async_copy(
+                        edge.at[pl.ds(row, rows)], steps[t].at[f, pl.ds(start, rows), inner_y],
+                        sems.at[len(copies)],
+                    )
+                )
             row += rows
     keep = is_active(aperture)
     run_copies(copies)
@@ -429,14 +433,14 @@
         for slot, i in enumerate(group):
             places = slice(g * shots, (g + 1) * shots)
             correlate(
-                lambda t, x: held[t, 0, x], lambda t, x: held[t, 1, x],
+                lambda t, x: steps[t][0, x, inner_y, :], lambda t, x: steps[t][1, x, inner_y, :],
                 strip_map(part, width_x, strip_rows), keep, strip_rows, outs[places], slot, i,
             )
             for out, result in zip(outs[places], results[places]):
                 if out is not result:
                     send(out.at[:, slot], result.at[:, slot])
     for f, out in enumerate(last):
-        send(held.at[STEPS - 1, f, pl.ds(HALF, width_x)], out.at[0])
+        send(s3.at[f, pl.ds(PAD, width_x), inner_y], out.at[0])
     for copy in sends:
         copy.wait()
 
@@ -468,6 +472,10 @@
     run_copies(copies)
 
 
+PACK_LIMIT = 63_400_000
+SPREAD_LIMIT = 48 * 1024 * 1024
+
+
 def body(
     vel_coef, src_prev, src_cur, rcv_prev, rcv_cur, src_pos, src_amp, rcv_pos, rcv_data, aperture, owner
 ):
@@ -494,35 +502,40 @@
     args = (vel_coef, src_prev, src_cur, rcv_prev, rcv_cur)
 
     x_part = jax.ShapeDtypeStruct((x_rows, width_y, depth), f32)
-    y_part = jax.ShapeDtypeStruct((5, width_x, PAD, depth), f32)
-    sends = pl.pallas_call(
+    y_part = jax.ShapeDtypeStruct((Y_TILES, width_x, PAD, depth), f32)
+    receivers = rcv_pos.shape[1]
+    *sends, positions, values = pl.pallas_call(
         pack_kernel,
-        out_shape=(x_part, x_part, y_part, y_part),
-        in_specs=[ANY] * 5,
-        out_specs=(ANY,) * 4,
+        out_shape=(x_part, x_part, y_part, y_part)
+        + (pltpu.VMEM((1, receivers), jnp.int32), pltpu.VMEM((1, STEPS * receivers), f32)),
+        in_specs=[ANY] * 7,
+        out_specs=(ANY,) * 4 + (VMEM,) * 2,
         scratch_shapes=[pltpu.VMEM(part.shape, f32) for part in (x_part, x_part, y_part, y_part)]
-        + [pltpu.SemaphoreType.DMA((20,)), pltpu.SemaphoreType.DMA((4,))],
-        compiler_params=pltpu.CompilerParams(vmem_limit_bytes=60 * 1024 * 1024),
+        + [pltpu.SemaphoreType.DMA((22,)), pltpu.SemaphoreType.DMA((4,))],
+        compiler_params=pltpu.CompilerParams(vmem_limit_bytes=PACK_LIMIT),
         name="pack_halos",
-    )(*args)
+    )(rcv_pos, rcv_data.reshape(1, STEPS * receivers), *args)
     halos = [lax.ppermute(sends[n], "gx", swaps_x[n]) for n in range(2)]
     halos += [lax.ppermute(sends[2 + n], "gy", swaps_y[n]) for n in range(2)]
 
-    receivers = rcv_pos.shape[1]
-    inject = pl.pallas_call(
-        functools.partial(spread_kernel, width_x, width_y),
-        out_shape=jax.ShapeDtypeStruct((STEPS, ext_x * ext_y, depth), f32),
-        in_specs=[VMEM] * 2,
-        out_specs=VMEM,
-        compiler_params=big,
+    span = (width_x + 2 * PAD, width_y + 2 * PAD, depth)
+    padded = pltpu.VMEM((5,) + span, f32)
+    step = pltpu.VMEM((2,) + span, f32)
+    inject, ext = pl.pallas_call(
+        spread_kernel,
+        out_shape=(pltpu.VMEM((STEPS, ext_x * ext_y, depth), f32), padded),
+        in_specs=[VMEM] * 2 + [ANY] * 5,
+        out_specs=(VMEM, VMEM),
+        scratch_shapes=[pltpu.SemaphoreType.DMA((5,))],
+        compiler_params=pltpu.CompilerParams(vmem_limit_bytes=SPREAD_LIMIT),
         cost_estimate=pl.CostEstimate(
             flops=6 * ext_x * ext_y * receivers * depth * STEPS, bytes_accessed=4 * STEPS * ext_x * ext_y * depth,
             transcendentals=0),
         name="spread_receivers",
-    )(rcv_pos, rcv_data.reshape(1, STEPS * receivers))
-    inject = inject.reshape(STEPS, ext_x, ext_y, depth)
-
-    corner = jax.ShapeDtypeStruct((2, 5, CORNER, PAD, depth), f32)
+    )(positions, values, *args)
+    spread = inject.reshape(STEPS, ext_x, ext_y, depth)
+
+    corner = jax.ShapeDtypeStruct((2, Y_TILES, CORNER, PAD, depth), f32)
     corners = pl.pallas_call(
         corner_kernel,
         out_shape=(corner, corner),
@@ -541,61 +554,51 @@
     groups = [tuple(range(i, min(i + 3, held))) for i in range(early, held, 3)]
     edge_rows = 2 * sum(HALF - v for v in VALID)
     edge = jax.ShapeDtypeStruct((edge_rows, width_y, depth), f32)
-    span = (width_x + 2 * PAD, width_y + 2 * PAD, depth)
-    step = jax.ShapeDtypeStruct((2,) + span, f32)
     step_ops = 30 * width_x * width_y * depth * STEPS
     tables = (owner, aperture)
     middle = (width_x - 2 * HALF) // strip_rows
+    count = shots if early else 0
     inner = pl.pallas_call(
         functools.partial(inner_kernel, early, shots),
-        out_shape=(piece(middle, first),) * (shots if early else 0) + (step,) * 3,
-        in_specs=[SMEM] * 4 + [ANY] * 8,
-        out_specs=(VMEM,) * ((shots if early else 0) + 3),
-        scratch_shapes=[
-            pltpu.VMEM((5,) + span, f32),
-            pltpu.VMEM((STEPS, ext_x, ext_y, depth), f32),
-            pltpu.SemaphoreType.DMA((8,)),
-        ],
+        out_shape=(piece(middle, first),) * count + (padded,) + (step,) * 3,
+        in_specs=[SMEM] * 4 + [ANY] * 2 + [VMEM] * 2,
+        out_specs=(VMEM,) * (count + 4),
+        scratch_shapes=[pltpu.SemaphoreType.DMA((10,))],
+        input_output_aliases={7: count},
         compiler_params=big,
         cost_estimate=pl.CostEstimate(flops=step_ops, bytes_accessed=12 * 2**20, transcendentals=0),
         name="inner_steps",
-    )(*tables, src_pos, src_amp, *args, *halos[2:4], inject)
-    inner_pieces, inner = inner[:-3], inner[-3:]
+    )(*tables, src_pos, src_amp, *halos[2:4], spread, ext)
+    inner_pieces, inner = inner[:count], inner[count:]
     outer = pl.pallas_call(
         functools.partial(outer_kernel, early, shots),
-        out_shape=(piece(tiles - middle, first),) * (shots if early else 0) + (step,) * 3 + (edge, edge),
-        in_specs=[SMEM] * 4 + [ANY] * 15,
-        out_specs=(VMEM,) * ((shots if early else 0) + 3) + (VMEM,) * 2,
-        scratch_shapes=[
-            pltpu.VMEM((5,) + span, f32),
-            pltpu.VMEM((STEPS, ext_x, ext_y, depth), f32),
-            pltpu.SemaphoreType.DMA((40,)),
-            pltpu.SemaphoreType.DMA((12,)),
-        ],
+        out_shape=(piece(tiles - middle, first),) * count + (padded,) + (step,) * 3 + (edge, edge),
+        in_specs=[SMEM] * 4 + [ANY] * 4 + [VMEM] * 5,
+        out_specs=(VMEM,) * (count + 6),
+        scratch_shapes=[pltpu.SemaphoreType.DMA((30,)), pltpu.SemaphoreType.DMA((12,))],
+        input_output_aliases={9 + n: count + n for n in range(4)},
         compiler_params=big,
         cost_estimate=pl.CostEstimate(flops=step_ops, bytes_accessed=12 * 2**20, transcendentals=0),
         name="outer_steps",
-    )(*tables, src_pos, src_amp, *args, *halos, inject, *inner)
-    outer_pieces, outer, edges = outer[:-5], outer[-5:-2], outer[-2:]
+    )(*tables, src_pos, src_amp, *halos[:2], *halos[4:], spread, *inner)
+    outer_pieces, outer, edges = outer[:count], outer[count + 1 : count + 4], outer[count + 4 :]
     edges = [lax.ppermute(edges[n], "gx", swaps_x[n]) for n in range(2)]
     field = jax.ShapeDtypeStruct(src_cur.shape, f32)
 
     def others(part, *operands):
         strips = middle if part == 0 else tiles - middle
         shapes = [piece(strips, g).shape for g in groups for _ in range(shots)]
+        extra = (field, field) if part == 0 else (step,) * 3
         result = pl.pallas_call(
             functools.partial(rest_kernel, part, groups, shots),
             out_shape=(jax.ShapeDtypeStruct(shapes[0], f32),)
             + tuple(pltpu.HBM(shape, f32) for shape in shapes[1:])
-            + (field,) * (2 - 2 * part),
-            in_specs=[SMEM] * 2 + [ANY] * len(operands),
-            out_specs=(VMEM,) + (ANY,) * (len(shapes) + 1 - 2 * part),
+            + extra,
+            in_specs=[SMEM] * 2 + ([VMEM] * 3 if part == 0 else [ANY] * 2 + [VMEM] * 3 + [ANY]),
+            out_specs=(VMEM,) + (ANY,) * (len(shapes) - 1) + ((ANY,) * 2 if part == 0 else (VMEM,) * 3),
             scratch_shapes=[pltpu.VMEM(shape, f32) for shape in shapes[1:]]
-            + [
-                pltpu.VMEM((STEPS, 2, width_x + 2 * HALF, width_y, depth), f32),
-                pltpu.SemaphoreType.DMA((21,)),
-                pltpu.SemaphoreType.DMA((2 + held * shots,)),
-            ],
+            + [pltpu.SemaphoreType.DMA((12,)), pltpu.SemaphoreType.DMA((2 + held * shots,))],
+            input_output_aliases={4 + n: len(shapes) + n for n in range(3 * part)},
             compiler_params=big,
             cost_estimate=pl.CostEstimate(
                 flops=5 * OFFS * width_x * width_y * depth, bytes_accessed=12 * 2**20, transcendentals=0),
@@ -637,8 +640,8 @@
         both = (inner_pieces, outer_pieces)
         coming = [swapped(cells[1:]) for cells in both]
         totals.append(summed([cells[:1] for cells in both], coming, first))
-    far, (src_next, rcv_next) = others(0, *inner, *outer)
-    near, _ = others(1, *inner, *outer, *edges, totals[0] if early else edges[0])
+    far, (src_next, rcv_next) = others(0, *outer)
+    near, _ = others(1, *edges, *outer, totals[0] if early else edges[0])
     for g, group in enumerate(groups):
         both = [cells[g * shots : (g + 1) * shots] for cells in (far, near)]
         going = [cells[1:] for cells in both]

time: 173 us -> 172 us (level)
  starting transfers between devices: 36.3 us -> 38.2 us
    all_to_all x3, starting transfers between devices: 19.7 us -> 21.5 us  [body(): lax.all_to_all(total, ('gx', 'gy'), split_axis=0, concat_axis=0, tiled=True)]
  transfers between devices with their start and end apart: 17 -> 17, of which waited for: 8 -> 8; matrix products, arithmetic and copies ran while one was open for 5% -> 5% of each run, Pallas kernels for 18% -> 17%
where the time goes in v3:
time: 172 us; the launch traced here: 171 us
  waiting for transfers between devices  89 us (52%)
  starting transfers between devices  38.2 us (22%)
  Pallas kernels  33.5 us (19%)
  local copies, waits for them, and re-layouts  8.83 us (5%)
    ppermute x6, waiting for transfers between devices, swapped(): lax.ppermute(one, 'shot', [(s, (s + r + 1) % shots) for s in range(shots)])  53 us
    all_to_all x3, waiting for transfers between devices, body(): lax.all_to_all(total, ('gx', 'gy'), split_axis=0, concat_axis=0, tiled=True)  33.3 us
    all_to_all x3, starting transfers between devices, body(): lax.all_to_all(total, ('gx', 'gy'), split_axis=0, concat_axis=0, tiled=True)  21.5 us
    pallas_call x6, Pallas kernels, summed(): pl.pallas_call(functools.partial(sum_kernel, part, shots), out_shape=piec...  9.64 us
    pallas_call x2, Pallas kernels, others(): pl.pallas_call(functools.partial(rest_kernel, part, groups, shots), out_s...  7.19 us
    dynamic_update_slice x5, local copies, waits for them, and re-layouts, body(): lax.dynamic_update_slice(gathers, arrived[None, None, :, slot], (0, where...  6.25 us
    ppermute x6, starting transfers between devices, swapped(): lax.ppermute(one, 'shot', [(s, (s + r + 1) % shots) for s in range(shots)])  5.62 us
    pallas_call x1, Pallas kernels, body(): pl.pallas_call(functools.partial(inner_kernel, early, shots), out_shape=(...  4.89 us
  transfers between devices with their start and end apart: 17, of which 8 were waited for; matrix products, arithmetic and copies ran while one was open for 5% of the time, Pallas kernels for 17%

profile of v3, /device:TPU:11, one launch (start us, length us, event | category | flops | bytes accessed | tf_op | source)
XLA Modules:
  0.0 171.0 jit_solution(15835525648096776788)
XLA Ops:
  0.6 2.7 %pack_halos.1 = (f32[34,32,128]{2,1,0:T(8,128)}, f32[34,32,128]{2,1,0:T(8,128)}, f32[4,32,8,128]{3,2,1,0:T(8,128)}, f32[4,32,8,128]{3,2,1,0:T(8,128)}, s32[1,512]{1,0:T(1,128)S(1)}, /*index=5*/f32[1,1536]{1,0:T(1,128)S(1)}) custom-call(s32[1,512]{1,0:T(1,128)} %positions_from.1, f32[1,1536]{1,0:T(1,128)} %bitcast.34, f32[32,32,128]{2,1,0:T(8,128)} %vel.3, ...), custom_call_target="tpu_custom_call" | custom-call | tf_op jit(solution)/shard_map/pack_halos/pallas_call | solution.py:507
  5.0 4.3 %collective-permute-start.1 = (f32[34,32,128]{2,1,0:T(8,128)}, f32[34,32,128]{2,1,0:T(8,128)S(1)}, u32[]{:S(2)}, u32[]{:S(2)}) collective-permute-start(f32[34,32,128]{2,1,0:T(8,128)} %get-tuple-element.40), channel_id=1, source_target_pairs={{4,8},{8,4},{5,9},{9,5},{6,10},{10,6},{7,11},{11,7},{20,24},{24,20... | collective-permute-start | bytes 1671176 | tf_op jit(solution)/shard_map/ppermute | solution.py:518
  9.4 3.3 %spread_receivers.1 = (f32[3,1760,128]{2,1,0:T(8,128)S(1)}, f32[5,48,48,128]{3,2,1,0:T(8,128)S(1)}) custom-call(s32[1,512]{1,0:T(1,128)} %copy-done.6, f32[1,1536]{1,0:T(1,128)} %copy-done.5, f32[32,32,128]{2,1,0:T(8,128)} %vel.3, f32[1,32,32,128]{3,2,1,0:T(8,128)} %src_prev.3, f32[1,32,32,128]{3,2,1,0:T(8,128)} %src_cur.3, f32[1,32,32,128]{3,2,1,0:T(8,128)} %rcv_prev.3, ...), custom_call_target="tpu_custom_call" | custom-call | flops 2076180480 | bytes 2703360 | tf_op jit(solution)/shard_map/spread_receivers/pallas_call | solution.py:524
  13.1 1.9 %collective-permute-start.5 = (f32[2,4,6,8,128]{4,3,2,1,0:T(8,128)S(1)}, f32[2,4,6,8,128]{4,3,2,1,0:T(8,128)S(1)}, u32[]{:S(2)}, u32[]{:S(2)}) collective-permute-start(f32[2,4,6,8,128]{4,3,2,1,0:T(8,128)S(1)} %get-tuple-element.47), channel_id=1, source_target_pairs={{4,8},{8,4},{5,9},{9,5},{6,10},{10,6},{7,11},{11,7},{20,24},{24,20... | collective-permute-start | bytes 589832 | tf_op jit(solution)/shard_map/ppermute | solution.py:548
  15.7 4.9 %inner_steps.1 = (f32[8,2,2,32,128]{4,3,2,1,0:T(8,128)S(1)}, f32[8,2,2,32,128]{4,3,2,1,0:T(8,128)S(1)}, f32[5,48,48,128]{3,2,1,0:T(8,128)S(1)}, f32[2,48,48,128]...) custom-call(s32[16,16]{1,0:T(8,128)S(1)} %copy-done.1, ...), custom_call_target="tpu_custom_call", output_to_operand_aliasing={{2}: (7, {})} | custom-call | flops 11796480 | bytes 12582912 | tf_op jit(solution)/shard_map/inner_steps/pallas_call | solution.py:561
  21.9 2.7 %collective-permute-done.5.c1 = f32[2,4,6,8,128]{4,3,2,1,0:T(8,128)S(1)} collective-permute-done((f32[2,4,6,8,128]{4,3,2,1,0:T(8,128)S(1)}, f32[2,4,6,8,128]{4,3,2,1,0:T(8,128)S(1)}, u32[]{:S(2)}, u32[]{:S(2)}) %collective-permute-start.5) | collective-permute-done | bytes 196640 | tf_op jit(solution)/shard_map/ppermute | solution.py:548
  24.6 4.4 %outer_steps.1 = (f32[8,2,2,32,128]{4,3,2,1,0:T(8,128)S(1)}, f32[8,2,2,32,128]{4,3,2,1,0:T(8,128)S(1)}, f32[5,48,48,128]{3,2,1,0:T(8,128)S(1)}, f32[2,48,48,128]...) custom-call(s32[16,16]{1,0:T(8,128)S(1)} %copy-done.1, ...), custom_call_target="tpu_custom_call", output_to_operand_aliasing={{2}: (9, {}), {3}: (10, {}), {4}: (11, {}), {5}: (12, {})} | custom-call | flops 11796480 | bytes 12582912 | tf_op jit(solution)/shard_map/outer_steps/pallas_call | solution.py:573
  30.2 3.1 %collective-permute-start.9 = (f32[24,32,128]{2,1,0:T(8,128)S(1)}, f32[24,32,128]{2,1,0:T(8,128)S(1)}, u32[]{:S(2)}, u32[]{:S(2)}) collective-permute-start(f32[24,32,128]{2,1,0:T(8,128)S(1)} %get-tuple-element.63), channel_id=1, source_target_pairs={{4,8},{8,4},{5,9},{9,5},{6,10},{10,6},{7,11},{11,7},{20,24},{24,20... | collective-permute-start | bytes 1179656 | tf_op jit(solution)/shard_map/ppermute | solution.py:585
  33.3 3.6 %far_strips.1 = (f32[8,3,2,32,128]{4,3,2,1,0:T(8,128)S(1)}, f32[8,3,2,32,128]{4,3,2,1,0:T(8,128)}, f32[8,3,2,32,128]{4,3,2,1,0:T(8,128)}, f32[8,3,2,32,128]{4,3,...) custom-call(s32[16,16]{1,0:T(8,128)S(1)} %copy-done.1, s32[1,8]{1,0:T(1,128)S(1)} %copy-done.2, ...), custom_call_target="tpu_custom_call" | custom-call | flops 10485760 | bytes 12582912 | tf_op jit(solution)/shard_map/far_strips/pallas_call | solution.py:592
  38.5 4.5 %collective-permute-done.6.refs_1_ = f32[8,2,2,32,128]{4,3,2,1,0:T(8,128)S(1)} collective-permute-done((f32[8,2,2,32,128]{4,3,2,1,0:T(8,128)S(1)}, f32[8,2,2,32,128]{4,3,2,1,0:T(8,128)S(1)}, u32[]{:S(2)}, u32[]{:S(2)}) %collective-permute-start.6) | collective-permute-done | bytes 524320 | tf_op jit(solution)/shard_map/ppermute | solution.py:611
  45.8 3.6 %near_strips.1 = (f32[8,3,2,32,128]{4,3,2,1,0:T(8,128)S(1)}, f32[8,3,2,32,128]{4,3,2,1,0:T(8,128)}, f32[8,3,2,32,128]{4,3,2,1,0:T(8,128)}, f32[8,3,2,32,128]{4,3...) custom-call(s32[16,16]{1,0:T(8,128)S(1)} %copy-done.1, ...), custom_call_target="tpu_custom_call", output_to_operand_aliasing={{4}: (4, {}), {5}: (5, {}), {6}: (6, {})} | custom-call | flops 10485760 | bytes 12582912 | tf_op jit(solution)/shard_map/near_strips/pallas_call | solution.py:592
  49.7 8.9 %all-to-all-start = ((f32[16,2,2,32,128]{4,3,2,1,0:T(8,128)}), f32[16,2,2,32,128]{4,3,2,1,0:T(8,128)}, u32[]{:S(2)}, u32[]{:S(2)}) async-start(f32[16,2,2,32,128]{4,3,2,1,0:T(8,128)} %sum_near.3.rest_5_), calls=%async_computation | async-start | bytes 2097152 | tf_op jit(solution)/shard_map/all_to_all | solution.py:658
  60.6 15.3 %collective-permute-done.10.refs_1_ = f32[8,3,2,32,128]{4,3,2,1,0:T(8,128)S(1)} collective-permute-done((f32[8,3,2,32,128]{4,3,2,1,0:T(8,128)}, f32[8,3,2,32,128]{4,3,2,1,0:T(8,128)S(1)}, u32[]{:S(2)}, u32[]{:S(2)}) %collective-permute-start.10) | collective-permute-done | bytes 786464 | tf_op jit(solution)/shard_map/ppermute | solution.py:611
  77.6 5.9 %all-to-all-done = f32[16,2,2,32,128]{4,3,2,1,0:T(8,128)} async-done(((f32[16,2,2,32,128]{4,3,2,1,0:T(8,128)}), f32[16,2,2,32,128]{4,3,2,1,0:T(8,128)}, u32[]{:S(2)}, u32[]{:S(2)}) %all-to-all-start) | async-done | bytes 1048608 | tf_op jit(solution)/shard_map/all_to_all | solution.py:658
  83.6 5.7 %all-to-all-start.1 = ((f32[16,3,2,32,128]{4,3,2,1,0:T(8,128)}), f32[16,3,2,32,128]{4,3,2,1,0:T(8,128)S(1)}, u32[]{:S(2)}, u32[]{:S(2)}) async-start(f32[16,3,2,32,128]{4,3,2,1,0:T(8,128)} %sum_near.4), calls=%async_computation.1 | async-start | bytes 3145728 | tf_op jit(solution)/shard_map/all_to_all | solution.py:658
  90.7 17.5 %collective-permute-done.13.refs_1_ = f32[8,3,2,32,128]{4,3,2,1,0:T(8,128)S(1)} collective-permute-done((f32[8,3,2,32,128]{4,3,2,1,0:T(8,128)}, f32[8,3,2,32,128]{4,3,2,1,0:T(8,128)S(1)}, u32[]{:S(2)}, u32[]{:S(2)}) %collective-permute-start.13) | collective-permute-done | bytes 786464 | tf_op jit(solution)/shard_map/ppermute | solution.py:611
  108.2 1.7 sum_far.5.refs_2_
  109.9 15.2 %collective-permute-done.12.refs_1_ = f32[8,3,2,32,128]{4,3,2,1,0:T(8,128)S(1)} collective-permute-done((f32[8,3,2,32,128]{4,3,2,1,0:T(8,128)}, f32[8,3,2,32,128]{4,3,2,1,0:T(8,128)S(1)}, u32[]{:S(2)}, u32[]{:S(2)}) %collective-permute-start.12) | collective-permute-done | bytes 786464 | tf_op jit(solution)/shard_map/ppermute | solution.py:611
  125.1 1.6 sum_near.5
  126.7 6.9 %all-to-all-start.2 = ((f32[16,3,2,32,128]{4,3,2,1,0:T(8,128)}), f32[16,3,2,32,128]{4,3,2,1,0:T(8,128)S(1)}, u32[]{:S(2)}, u32[]{:S(2)}) async-start(f32[16,3,2,32,128]{4,3,2,1,0:T(8,128)} %sum_near.5), calls=%async_computation.2 | async-start | bytes 3145728 | tf_op jit(solution)/shard_map/all_to_all | solution.py:658
  133.7 2.5 %broadcast_in_dim.3 = f32[1,8,16,2,32,128]{5,4,3,2,1,0:T(8,128)} broadcast(f32[]{:T(128)} %constant.11.clone.1), dimensions={} | broadcast | bytes 4194308 | tf_op jit(solution)/shard_map/broadcast_in_dim | solution.py:655
  136.2 1.9 %fusion.4 = f32[1,8,16,2,32,128]{5,4,3,2,1,0:T(8,128)} fusion(f32[1,8,16,2,32,128]{5,4,3,2,1,0:T(8,128)} %broadcast_in_dim.3, s32[]{:T(128)S(6)} %select_n.21, f32[16,2,2,32,128]{4,3,2,1,0:T(8,128)} %all-to-all-done), kind=kLoop, calls=%fused_computation.9 | loop fusion | bytes 1048580 | tf_op jit(solution)/shard_map/dynamic_update_slice | solution.py:662
  138.1 1.9 %fusion.3 = f32[1,8,16,2,32,128]{5,4,3,2,1,0:T(8,128)} fusion(f32[1,8,16,2,32,128]{5,4,3,2,1,0:T(8,128)} %fusion.4, s32[]{:T(128)S(6)} %select_n.22, f32[16,2,2,32,128]{4,3,2,1,0:T(8,128)} %all-to-all-done), kind=kLoop, calls=%fused_computation.7 | loop fusion | bytes 1048580 | tf_op jit(solution)/shard_map/dynamic_update_slice | solution.py:662
  142.5 27.4 %all-to-all-done.2.piece = f32[16,3,2,32,128]{4,3,2,1,0:T(8,128)S(1)} async-done(((f32[16,3,2,32,128]{4,3,2,1,0:T(8,128)}), f32[16,3,2,32,128]{4,3,2,1,0:T(8,128)S(1)}, u32[]{:S(2)}, u32[]{:S(2)}) %all-to-all-start.2) | async-done | bytes 1572896 | tf_op jit(solution)/shard_map/all_to_all | solution.py:658
  (44 shorter events, 18.0 us)
Async XLA Ops:
  3.3 6.0 %copy-start.5 = (f32[1,1536]{1,0:T(1,128)}, f32[1,1536]{1,0:T(1,128)S(1)}, u32[]{:S(2)}) copy-start(f32[1,1536]{1,0:T(1,128)S(1)} %get-tuple-element.44.values) | copy-start | bytes 18436
  3.3 6.0 %copy-start.6 = (s32[1,512]{1,0:T(1,128)}, s32[1,512]{1,0:T(1,128)S(1)}, u32[]{:S(2)}) copy-start(s32[1,512]{1,0:T(1,128)S(1)} %get-tuple-element.43.positions) | copy-start | bytes 6148
  3.4 9.4 %collective-permute-start.2 = (f32[4,32,8,128]{3,2,1,0:T(8,128)}, f32[4,32,8,128]{3,2,1,0:T(8,128)S(1)}, u32[]{:S(2)}, u32[]{:S(2)}) collective-permute-start(f32[4,32,8,128]{3,2,1,0:T(8,128)} %get-tuple-element.41), channel_id=1, source_target_pairs={{0,1},{1,0},{2,3},{3,2},{4,5},{5,4},{6,7},{7,6},{8,9},{9,8},{10,11... | collective-permute-start | bytes 1572872 | tf_op jit(solution)/shard_map/ppermute | solution.py:519
  4.1 8.7 %collective-permute-start.3 = (f32[4,32,8,128]{3,2,1,0:T(8,128)}, f32[4,32,8,128]{3,2,1,0:T(8,128)S(1)}, u32[]{:S(2)}, u32[]{:S(2)}) collective-permute-start(f32[4,32,8,128]{3,2,1,0:T(8,128)} %get-tuple-element.42), channel_id=1, source_target_pairs={{1,2},{2,1},{5,6},{6,5},{9,10},{10,9},{13,14},{14,13},{17,18},{18,... | collective-permute-start | bytes 1572872 | tf_op jit(solution)/shard_map/ppermute | solution.py:519
  4.8 17.1 %collective-permute-start = (f32[34,32,128]{2,1,0:T(8,128)}, f32[34,32,128]{2,1,0:T(8,128)S(1)}, u32[]{:S(2)}, u32[]{:S(2)}) collective-permute-start(f32[34,32,128]{2,1,0:T(8,128)} %get-tuple-element.39), channel_id=1, source_target_pairs={{0,4},{4,0},{8,12},{12,8},{1,5},{5,1},{9,13},{13,9},{2,6},{6,2},{1... | collective-permute-start | bytes 1671176 | tf_op jit(solution)/shard_map/ppermute | solution.py:518
  5.0 16.9 %collective-permute-start.1 = (f32[34,32,128]{2,1,0:T(8,128)}, f32[34,32,128]{2,1,0:T(8,128)S(1)}, u32[]{:S(2)}, u32[]{:S(2)}) collective-permute-start(f32[34,32,128]{2,1,0:T(8,128)} %get-tuple-element.40), channel_id=1, source_target_pairs={{4,8},{8,4},{5,9},{9,5},{6,10},{10,6},{7,11},{11,7},{20,24},{24,20... | collective-permute-start | bytes 1671176 | tf_op jit(solution)/shard_map/ppermute | solution.py:518
  9.4 6.3 %copy-start.1 = (s32[16,16]{1,0:T(8,128)S(1)}, s32[16,16]{1,0:T(8,128)}, u32[]{:S(2)}) copy-start(s32[16,16]{1,0:T(8,128)} %owner.19) | copy-start | bytes 3076
  9.4 6.3 %copy-start.2 = (s32[1,8]{1,0:T(1,128)S(1)}, s32[1,8]{1,0:T(1,128)}, u32[]{:S(2)}) copy-start(s32[1,8]{1,0:T(1,128)} %aperture.7) | copy-start | bytes 100
  9.4 6.3 %copy-start.3 = (f32[1,3]{1,0:T(1,128)S(1)}, f32[1,3]{1,0:T(1,128)}, u32[]{:S(2)}) copy-start(f32[1,3]{1,0:T(1,128)} %amps.3) | copy-start | bytes 40
  13.0 8.9 %collective-permute-start.4 = (f32[2,4,6,8,128]{4,3,2,1,0:T(8,128)S(1)}, f32[2,4,6,8,128]{4,3,2,1,0:T(8,128)S(1)}, u32[]{:S(2)}, u32[]{:S(2)}) collective-permute-start(f32[2,4,6,8,128]{4,3,2,1,0:T(8,128)S(1)} %get-tuple-element.46), channel_id=1, source_target_pairs={{0,4},{4,0},{8,12},{12,8},{1,5},{5,1},{9,13},{13,9},{2,6},{6,2},{1... | collective-permute-start | bytes 589832 | tf_op jit(solution)/shard_map/ppermute | solution.py:548
  13.1 11.5 %collective-permute-start.5 = (f32[2,4,6,8,128]{4,3,2,1,0:T(8,128)S(1)}, f32[2,4,6,8,128]{4,3,2,1,0:T(8,128)S(1)}, u32[]{:S(2)}, u32[]{:S(2)}) collective-permute-start(f32[2,4,6,8,128]{4,3,2,1,0:T(8,128)S(1)} %get-tuple-element.47), channel_id=1, source_target_pairs={{4,8},{8,4},{5,9},{9,5},{6,10},{10,6},{7,11},{11,7},{20,24},{24,20... | collective-permute-start | bytes 589832 | tf_op jit(solution)/shard_map/ppermute | solution.py:548
  20.6 16.4 %collective-permute-start.7 = (f32[8,2,2,32,128]{4,3,2,1,0:T(8,128)S(1)}, f32[8,2,2,32,128]{4,3,2,1,0:T(8,128)S(1)}, u32[]{:S(2)}, u32[]{:S(2)}) collective-permute-start(f32[8,2,2,32,128]{4,3,2,1,0:T(8,128)S(1)} %get-tuple-element.61), channel_id=1, source_target_pairs={{0,16},{16,0},{1,17},{17,1},{2,18},{18,2},{3,19},{19,3},{4,20},{20... | collective-permute-start | bytes 1572872 | tf_op jit(solution)/shard_map/ppermute | solution.py:611
  28.9 14.1 %collective-permute-start.6 = (f32[8,2,2,32,128]{4,3,2,1,0:T(8,128)S(1)}, f32[8,2,2,32,128]{4,3,2,1,0:T(8,128)S(1)}, u32[]{:S(2)}, u32[]{:S(2)}) collective-permute-start(f32[8,2,2,32,128]{4,3,2,1,0:T(8,128)S(1)} %get-tuple-element.59), channel_id=1, source_target_pairs={{0,16},{16,0},{1,17},{17,1},{2,18},{18,2},{3,19},{19,3},{4,20},{20... | collective-permute-start | bytes 1572872 | tf_op jit(solution)/shard_map/ppermute | solution.py:611
  30.2 15.6 %collective-permute-start.8 = (f32[24,32,128]{2,1,0:T(8,128)S(1)}, f32[24,32,128]{2,1,0:T(8,128)S(1)}, u32[]{:S(2)}, u32[]{:S(2)}) collective-permute-start(f32[24,32,128]{2,1,0:T(8,128)S(1)} %get-tuple-element.62), channel_id=1, source_target_pairs={{0,4},{4,0},{8,12},{12,8},{1,5},{5,1},{9,13},{13,9},{2,6},{6,2},{1... | collective-permute-start | bytes 1179656 | tf_op jit(solution)/shard_map/ppermute | solution.py:585
  30.2 15.6 %collective-permute-start.9 = (f32[24,32,128]{2,1,0:T(8,128)S(1)}, f32[24,32,128]{2,1,0:T(8,128)S(1)}, u32[]{:S(2)}, u32[]{:S(2)}) collective-permute-start(f32[24,32,128]{2,1,0:T(8,128)S(1)} %get-tuple-element.63), channel_id=1, source_target_pairs={{4,8},{8,4},{5,9},{9,5},{6,10},{10,6},{7,11},{11,7},{20,24},{24,20... | collective-permute-start | bytes 1179656 | tf_op jit(solution)/shard_map/ppermute | solution.py:585
  43.0 16.0 %collective-permute-start.11 = (f32[8,3,2,32,128]{4,3,2,1,0:T(8,128)}, f32[8,3,2,32,128]{4,3,2,1,0:T(8,128)S(1)}, u32[]{:S(2)}, u32[]{:S(2)}) collective-permute-start(f32[8,3,2,32,128]{4,3,2,1,0:T(8,128)} %get-tuple-element.68), channel_id=1, source_target_pairs={{0,16},{16,0},{1,17},{17,1},{2,18},{18,2},{3,19},{19,3},{4,20},{20... | collective-permute-start | bytes 2359304 | tf_op jit(solution)/shard_map/ppermute | solution.py:611
  49.4 26.6 %collective-permute-start.10 = (f32[8,3,2,32,128]{4,3,2,1,0:T(8,128)}, f32[8,3,2,32,128]{4,3,2,1,0:T(8,128)S(1)}, u32[]{:S(2)}, u32[]{:S(2)}) collective-permute-start(f32[8,3,2,32,128]{4,3,2,1,0:T(8,128)} %get-tuple-element.65), channel_id=1, source_target_pairs={{0,16},{16,0},{1,17},{17,1},{2,18},{18,2},{3,19},{19,3},{4,20},{20... | collective-permute-start | bytes 2359304 | tf_op jit(solution)/shard_map/ppermute | solution.py:611
  49.7 33.9 %all-to-all-start = ((f32[16,2,2,32,128]{4,3,2,1,0:T(8,128)}), f32[16,2,2,32,128]{4,3,2,1,0:T(8,128)}, u32[]{:S(2)}, u32[]{:S(2)}) async-start(f32[16,2,2,32,128]{4,3,2,1,0:T(8,128)} %sum_near.3.rest_5_), calls=%async_computation | async-start | bytes 2097152 | tf_op jit(solution)/shard_map/all_to_all | solution.py:658
  76.0 32.3 %copy-start = (f32[8,3,2,32,128]{4,3,2,1,0:T(8,128)S(1)}, f32[8,3,2,32,128]{4,3,2,1,0:T(8,128)}, u32[]{:S(2)}) copy-start(f32[8,3,2,32,128]{4,3,2,1,0:T(8,128)} %get-tuple-element.73.refs_0_) | copy-start | bytes 2359300
  77.6 47.5 %copy-start.4 = (f32[8,3,2,32,128]{4,3,2,1,0:T(8,128)S(1)}, f32[8,3,2,32,128]{4,3,2,1,0:T(8,128)}, u32[]{:S(2)}) copy-start(f32[8,3,2,32,128]{4,3,2,1,0:T(8,128)} %get-tuple-element.69.refs_0_) | copy-start | bytes 2359300
  83.6 43.2 %all-to-all-start.1 = ((f32[16,3,2,32,128]{4,3,2,1,0:T(8,128)}), f32[16,3,2,32,128]{4,3,2,1,0:T(8,128)S(1)}, u32[]{:S(2)}, u32[]{:S(2)}) async-start(f32[16,3,2,32,128]{4,3,2,1,0:T(8,128)} %sum_near.4), calls=%async_computation.1 | async-start | bytes 3145728 | tf_op jit(solution)/shard_map/all_to_all | solution.py:658
  89.3 19.0 %collective-permute-start.13 = (f32[8,3,2,32,128]{4,3,2,1,0:T(8,128)}, f32[8,3,2,32,128]{4,3,2,1,0:T(8,128)S(1)}, u32[]{:S(2)}, u32[]{:S(2)}) collective-permute-start(f32[8,3,2,32,128]{4,3,2,1,0:T(8,128)} %get-tuple-element.74), channel_id=1, source_target_pairs={{0,16},{16,0},{1,17},{17,1},{2,18},{18,2},{3,19},{19,3},{4,20},{20... | collective-permute-start | bytes 2359304 | tf_op jit(solution)/shard_map/ppermute | solution.py:611
  90.5 34.6 %collective-permute-start.12 = (f32[8,3,2,32,128]{4,3,2,1,0:T(8,128)}, f32[8,3,2,32,128]{4,3,2,1,0:T(8,128)S(1)}, u32[]{:S(2)}, u32[]{:S(2)}) collective-permute-start(f32[8,3,2,32,128]{4,3,2,1,0:T(8,128)} %get-tuple-element.72), channel_id=1, source_target_pairs={{0,16},{16,0},{1,17},{17,1},{2,18},{18,2},{3,19},{19,3},{4,20},{20... | collective-permute-start | bytes 2359304 | tf_op jit(solution)/shard_map/ppermute | solution.py:611
  126.7 43.1 %all-to-all-start.2 = ((f32[16,3,2,32,128]{4,3,2,1,0:T(8,128)}), f32[16,3,2,32,128]{4,3,2,1,0:T(8,128)S(1)}, u32[]{:S(2)}, u32[]{:S(2)}) async-start(f32[16,3,2,32,128]{4,3,2,1,0:T(8,128)} %sum_near.5), calls=%async_computation.2 | async-start | bytes 3145728 | tf_op jit(solution)/shard_map/all_to_all | solution.py:658

commit v4 on v3

--- a/solution.py
+++ b/solution.py
@@ -476,6 +476,9 @@
 SPREAD_LIMIT = 48 * 1024 * 1024
 
 
+SUM_COSTS = ((2**20, 2**34), (2**20, 2**35), (3 * 2**33, 2**20))
+
+
 def body(
     vel_coef, src_prev, src_cur, rcv_prev, rcv_cur, src_pos, src_amp, rcv_pos, rcv_data, aperture, owner
 ):
@@ -612,46 +615,44 @@
             for r, one in enumerate(cells)
         ]
 
-    long_cost = pl.CostEstimate(flops=2**37, bytes_accessed=2**28, transcendentals=0)
-
-    def summed(kept, coming, group):
-        total = []
-        for part in range(2):
-            cells = list(kept[part]) + list(coming[part])
-            total = [
-                pl.pallas_call(
-                    functools.partial(sum_kernel, part, shots),
-                    out_shape=piece(tiles, group),
-                    in_specs=[SMEM] + [VMEM] * shots + [ANY] * part,
-                    out_specs=ANY,
-                    scratch_shapes=[
-                        pltpu.VMEM(cells[0].shape, f32), pltpu.SemaphoreType.DMA((cells[0].shape[0],))],
-                    input_output_aliases={1 + shots: 0} if part else {},
-                    compiler_params=small,
-                    cost_estimate=pl.CostEstimate(flops=(2**20, 2**34)[part], bytes_accessed=2**20, transcendentals=0),
-                    name=("sum_far", "sum_near")[part],
-                )(owner, *cells, *total)
-            ]
-        return total[0]
+    def summed(part, kept, coming, group, old, cost):
+        cells = list(kept[part]) + list(coming[part])
+        return pl.pallas_call(
+            functools.partial(sum_kernel, part, shots),
+            out_shape=piece(tiles, group),
+            in_specs=[SMEM] + [VMEM] * shots + [ANY] * part,
+            out_specs=ANY,
+            scratch_shapes=[
+                pltpu.VMEM(cells[0].shape, f32), pltpu.SemaphoreType.DMA((cells[0].shape[0],))],
+            input_output_aliases={1 + shots: 0} if part else {},
+            compiler_params=small,
+            cost_estimate=pl.CostEstimate(flops=cost[part], bytes_accessed=2**20, transcendentals=0),
+            name=("sum_far", "sum_near")[part],
+        )(owner, *cells, *old)
 
     totals = []
     coming = []
     if early:
         both = (inner_pieces, outer_pieces)
         coming = [swapped(cells[1:]) for cells in both]
-        totals.append(summed([cells[:1] for cells in both], coming, first))
+        kept = [cells[:1] for cells in both]
+        half = summed(0, kept, coming, first, [], SUM_COSTS[0])
+        totals.append(summed(1, kept, coming, first, [half], SUM_COSTS[0]))
     far, (src_next, rcv_next) = others(0, *outer)
     near, _ = others(1, *edges, *outer, totals[0] if early else edges[0])
+    half = None
     for g, group in enumerate(groups):
         both = [cells[g * shots : (g + 1) * shots] for cells in (far, near)]
         going = [cells[1:] for cells in both]
-        if coming:
-            if g == 0 and early:
-                (going[0], coming) = lax.optimization_barrier((going[0], coming))
-            else:
-                (going, coming) = lax.optimization_barrier((going, coming))
+        if half is not None:
+            (going, coming, half) = lax.optimization_barrier((going, coming, half))
+            totals.append(summed(1, kept, coming, groups[g - 1], [half], SUM_COSTS[min(g, 2)]))
+        elif coming:
+            (going[0], coming) = lax.optimization_barrier((going[0], coming))
         coming = [swapped(cells) for cells in going]
-        totals.append(summed([cells[:1] for cells in both], coming, group))
+        kept = [cells[:1] for cells in both]
+        half = summed(0, kept, coming, group, [], SUM_COSTS[min(g + 1, 2)])
+    totals.append(summed(1, kept, coming, groups[-1], [half], SUM_COSTS[min(len(groups), 2)]))
     gathers = jnp.zeros((1, held, tiles, strip_rows, width_y, depth), f32)
     chunks = ([first] if early else []) + groups
     for n, (group, total) in enumerate(zip(chunks, totals)):

time: 172 us -> 170 us (0.988)
    ppermute x6, waiting for transfers between devices: 53 us -> 38.2 us  [swapped(): lax.ppermute(one, 'shot', [(s, (s + r + 1) % shots) for s in range(shots)])]
    all_to_all x3, waiting for transfers between devices: 33.3 us -> 46.8 us  [body(): lax.all_to_all(total, ('gx', 'gy'), split_axis=0, concat_axis=0, tiled=True)]
  transfers between devices with their start and end apart: 17 -> 17, of which waited for: 8 -> 9; matrix products, arithmetic and copies ran while one was open for 5% -> 5% of each run, Pallas kernels for 17% -> 18%
where the time goes in v4:
time: 170 us; the launch traced here: 169 us
  waiting for transfers between devices  87.7 us (52%)
  starting transfers between devices  37.5 us (22%)
  Pallas kernels  33.5 us (20%)
  local copies, waits for them, and re-layouts  8.83 us (5%)
    all_to_all x3, waiting for transfers between devices, body(): lax.all_to_all(total, ('gx', 'gy'), split_axis=0, concat_axis=0, tiled=True)  46.8 us
    ppermute x6, waiting for transfers between devices, swapped(): lax.ppermute(one, 'shot', [(s, (s + r + 1) % shots) for s in range(shots)])  38.2 us
    all_to_all x3, starting transfers between devices, body(): lax.all_to_all(total, ('gx', 'gy'), split_axis=0, concat_axis=0, tiled=True)  20.9 us
    pallas_call x6, Pallas kernels, summed(): pl.pallas_call(functools.partial(sum_kernel, part, shots), out_shape=piec...  9.69 us
    pallas_call x2, Pallas kernels, others(): pl.pallas_call(functools.partial(rest_kernel, part, groups, shots), out_s...  7.19 us
    dynamic_update_slice x5, local copies, waits for them, and re-layouts, body(): lax.dynamic_update_slice(gathers, arrived[None, None, :, slot], (0, where...  6.25 us
    ppermute x6, starting transfers between devices, swapped(): lax.ppermute(one, 'shot', [(s, (s + r + 1) % shots) for s in range(shots)])  5.59 us
    pallas_call x1, Pallas kernels, body(): pl.pallas_call(functools.partial(inner_kernel, early, shots), out_shape=(...  4.89 us
  transfers between devices with their start and end apart: 17, of which 9 were waited for; matrix products, arithmetic and copies ran while one was open for 5% of the time, Pallas kernels for 18%

profile of v4, /device:TPU:11, one launch (start us, length us, event | category | flops | bytes accessed | tf_op | source)
XLA Modules:
  0.0 169.1 jit_solution(13859637221696476797)
XLA Ops:
  0.6 2.7 %pack_halos.1 = (f32[34,32,128]{2,1,0:T(8,128)}, f32[34,32,128]{2,1,0:T(8,128)}, f32[4,32,8,128]{3,2,1,0:T(8,128)}, f32[4,32,8,128]{3,2,1,0:T(8,128)}, s32[1,512]{1,0:T(1,128)S(1)}, /*index=5*/f32[1,1536]{1,0:T(1,128)S(1)}) custom-call(s32[1,512]{1,0:T(1,128)} %positions_from.1, f32[1,1536]{1,0:T(1,128)} %bitcast.34, f32[32,32,128]{2,1,0:T(8,128)} %vel.3, ...), custom_call_target="tpu_custom_call" | custom-call | tf_op jit(solution)/shard_map/pack_halos/pallas_call | solution.py:510
  5.0 4.3 %collective-permute-start.1 = (f32[34,32,128]{2,1,0:T(8,128)}, f32[34,32,128]{2,1,0:T(8,128)S(1)}, u32[]{:S(2)}, u32[]{:S(2)}) collective-permute-start(f32[34,32,128]{2,1,0:T(8,128)} %get-tuple-element.42), channel_id=1, source_target_pairs={{4,8},{8,4},{5,9},{9,5},{6,10},{10,6},{7,11},{11,7},{20,24},{24,20... | collective-permute-start | bytes 1671176 | tf_op jit(solution)/shard_map/ppermute | solution.py:521
  9.4 3.3 %spread_receivers.1 = (f32[3,1760,128]{2,1,0:T(8,128)S(1)}, f32[5,48,48,128]{3,2,1,0:T(8,128)S(1)}) custom-call(s32[1,512]{1,0:T(1,128)} %copy-done.6, f32[1,1536]{1,0:T(1,128)} %copy-done.5, f32[32,32,128]{2,1,0:T(8,128)} %vel.3, f32[1,32,32,128]{3,2,1,0:T(8,128)} %src_prev.3, f32[1,32,32,128]{3,2,1,0:T(8,128)} %src_cur.3, f32[1,32,32,128]{3,2,1,0:T(8,128)} %rcv_prev.3, ...), custom_call_target="tpu_custom_call" | custom-call | flops 2076180480 | bytes 2703360 | tf_op jit(solution)/shard_map/spread_receivers/pallas_call | solution.py:527
  13.1 1.9 %collective-permute-start.5 = (f32[2,4,6,8,128]{4,3,2,1,0:T(8,128)S(1)}, f32[2,4,6,8,128]{4,3,2,1,0:T(8,128)S(1)}, u32[]{:S(2)}, u32[]{:S(2)}) collective-permute-start(f32[2,4,6,8,128]{4,3,2,1,0:T(8,128)S(1)} %get-tuple-element.49), channel_id=1, source_target_pairs={{4,8},{8,4},{5,9},{9,5},{6,10},{10,6},{7,11},{11,7},{20,24},{24,20... | collective-permute-start | bytes 589832 | tf_op jit(solution)/shard_map/ppermute | solution.py:551
  15.7 4.9 %inner_steps.1 = (f32[8,2,2,32,128]{4,3,2,1,0:T(8,128)S(1)}, f32[8,2,2,32,128]{4,3,2,1,0:T(8,128)S(1)}, f32[5,48,48,128]{3,2,1,0:T(8,128)S(1)}, f32[2,48,48,128]...) custom-call(s32[16,16]{1,0:T(8,128)S(1)} %copy-done.1, ...), custom_call_target="tpu_custom_call", output_to_operand_aliasing={{2}: (7, {})} | custom-call | flops 11796480 | bytes 12582912 | tf_op jit(solution)/shard_map/inner_steps/pallas_call | solution.py:564
  21.9 2.7 %collective-permute-done.5.c1 = f32[2,4,6,8,128]{4,3,2,1,0:T(8,128)S(1)} collective-permute-done((f32[2,4,6,8,128]{4,3,2,1,0:T(8,128)S(1)}, f32[2,4,6,8,128]{4,3,2,1,0:T(8,128)S(1)}, u32[]{:S(2)}, u32[]{:S(2)}) %collective-permute-start.5) | collective-permute-done | bytes 196640 | tf_op jit(solution)/shard_map/ppermute | solution.py:551
  24.6 4.4 %outer_steps.1 = (f32[8,2,2,32,128]{4,3,2,1,0:T(8,128)S(1)}, f32[8,2,2,32,128]{4,3,2,1,0:T(8,128)S(1)}, f32[5,48,48,128]{3,2,1,0:T(8,128)S(1)}, f32[2,48,48,128]...) custom-call(s32[16,16]{1,0:T(8,128)S(1)} %copy-done.1, ...), custom_call_target="tpu_custom_call", output_to_operand_aliasing={{2}: (9, {}), {3}: (10, {}), {4}: (11, {}), {5}: (12, {})} | custom-call | flops 11796480 | bytes 12582912 | tf_op jit(solution)/shard_map/outer_steps/pallas_call | solution.py:576
  30.2 3.1 %collective-permute-start.9 = (f32[24,32,128]{2,1,0:T(8,128)S(1)}, f32[24,32,128]{2,1,0:T(8,128)S(1)}, u32[]{:S(2)}, u32[]{:S(2)}) collective-permute-start(f32[24,32,128]{2,1,0:T(8,128)S(1)} %get-tuple-element.65), channel_id=1, source_target_pairs={{4,8},{8,4},{5,9},{9,5},{6,10},{10,6},{7,11},{11,7},{20,24},{24,20... | collective-permute-start | bytes 1179656 | tf_op jit(solution)/shard_map/ppermute | solution.py:588
  33.3 3.6 %far_strips.1 = (f32[8,3,2,32,128]{4,3,2,1,0:T(8,128)S(1)}, f32[8,3,2,32,128]{4,3,2,1,0:T(8,128)}, f32[8,3,2,32,128]{4,3,2,1,0:T(8,128)}, f32[8,3,2,32,128]{4,3,...) custom-call(s32[16,16]{1,0:T(8,128)S(1)} %copy-done.1, s32[1,8]{1,0:T(1,128)S(1)} %copy-done.2, ...), custom_call_target="tpu_custom_call" | custom-call | flops 10485760 | bytes 12582912 | tf_op jit(solution)/shard_map/far_strips/pallas_call | solution.py:595
  38.5 4.5 %collective-permute-done.6.refs_1_ = f32[8,2,2,32,128]{4,3,2,1,0:T(8,128)S(1)} collective-permute-done((f32[8,2,2,32,128]{4,3,2,1,0:T(8,128)S(1)}, f32[8,2,2,32,128]{4,3,2,1,0:T(8,128)S(1)}, u32[]{:S(2)}, u32[]{:S(2)}) %collective-permute-start.6) | collective-permute-done | bytes 524320 | tf_op jit(solution)/shard_map/ppermute | solution.py:614
  45.8 3.6 %near_strips.1 = (f32[8,3,2,32,128]{4,3,2,1,0:T(8,128)S(1)}, f32[8,3,2,32,128]{4,3,2,1,0:T(8,128)}, f32[8,3,2,32,128]{4,3,2,1,0:T(8,128)}, f32[8,3,2,32,128]{4,3...) custom-call(s32[16,16]{1,0:T(8,128)S(1)} %copy-done.1, ...), custom_call_target="tpu_custom_call", output_to_operand_aliasing={{4}: (4, {}), {5}: (5, {}), {6}: (6, {})} | custom-call | flops 10485760 | bytes 12582912 | tf_op jit(solution)/shard_map/near_strips/pallas_call | solution.py:595
  49.7 8.9 %all-to-all-start = ((f32[16,2,2,32,128]{4,3,2,1,0:T(8,128)}), f32[16,2,2,32,128]{4,3,2,1,0:T(8,128)}, u32[]{:S(2)}, u32[]{:S(2)}) async-start(f32[16,2,2,32,128]{4,3,2,1,0:T(8,128)} %sum_near.3.rest_5_), calls=%async_computation | async-start | bytes 2097152 | tf_op jit(solution)/shard_map/all_to_all | solution.py:659
  60.6 15.3 %collective-permute-done.11.refs_1_ = f32[8,3,2,32,128]{4,3,2,1,0:T(8,128)S(1)} collective-permute-done((f32[8,3,2,32,128]{4,3,2,1,0:T(8,128)}, f32[8,3,2,32,128]{4,3,2,1,0:T(8,128)S(1)}, u32[]{:S(2)}, u32[]{:S(2)}) %collective-permute-start.11) | collective-permute-done | bytes 786464 | tf_op jit(solution)/shard_map/ppermute | solution.py:614
  78.8 4.7 %all-to-all-done = f32[16,2,2,32,128]{4,3,2,1,0:T(8,128)} async-done(((f32[16,2,2,32,128]{4,3,2,1,0:T(8,128)}), f32[16,2,2,32,128]{4,3,2,1,0:T(8,128)}, u32[]{:S(2)}, u32[]{:S(2)}) %all-to-all-start) | async-done | bytes 1048608 | tf_op jit(solution)/shard_map/all_to_all | solution.py:659
  83.5 7.1 %all-to-all-start.1 = ((f32[16,3,2,32,128]{4,3,2,1,0:T(8,128)}), f32[16,3,2,32,128]{4,3,2,1,0:T(8,128)S(1)}, u32[]{:S(2)}, u32[]{:S(2)}) async-start(f32[16,3,2,32,128]{4,3,2,1,0:T(8,128)} %sum_near.4), calls=%async_computation.1 | async-start | bytes 3145728 | tf_op jit(solution)/shard_map/all_to_all | solution.py:659
  92.0 1.6 sum_far.5.refs_2_
  93.6 16.8 %collective-permute-done.12.refs_1_ = f32[8,3,2,32,128]{4,3,2,1,0:T(8,128)S(1)} collective-permute-done((f32[8,3,2,32,128]{4,3,2,1,0:T(8,128)}, f32[8,3,2,32,128]{4,3,2,1,0:T(8,128)S(1)}, u32[]{:S(2)}, u32[]{:S(2)}) %collective-permute-start.12) | collective-permute-done | bytes 786464 | tf_op jit(solution)/shard_map/ppermute | solution.py:614
  110.5 1.7 sum_near.5
  112.2 14.7 %all-to-all-done.1 = f32[16,3,2,32,128]{4,3,2,1,0:T(8,128)S(1)} async-done(((f32[16,3,2,32,128]{4,3,2,1,0:T(8,128)}), f32[16,3,2,32,128]{4,3,2,1,0:T(8,128)S(1)}, u32[]{:S(2)}, u32[]{:S(2)}) %all-to-all-start.1) | async-done | bytes 1572896 | tf_op jit(solution)/shard_map/all_to_all | solution.py:659
  126.8 4.9 %all-to-all-start.2 = ((f32[16,3,2,32,128]{4,3,2,1,0:T(8,128)}), f32[16,3,2,32,128]{4,3,2,1,0:T(8,128)S(1)}, u32[]{:S(2)}, u32[]{:S(2)}) async-start(f32[16,3,2,32,128]{4,3,2,1,0:T(8,128)} %sum_near.5), calls=%async_computation.2 | async-start | bytes 3145728 | tf_op jit(solution)/shard_map/all_to_all | solution.py:659
  131.7 2.5 %broadcast_in_dim.3 = f32[1,8,16,2,32,128]{5,4,3,2,1,0:T(8,128)} broadcast(f32[]{:T(128)} %constant.11.clone.1), dimensions={} | broadcast | bytes 4194308 | tf_op jit(solution)/shard_map/broadcast_in_dim | solution.py:656
  134.3 1.9 %fusion.4 = f32[1,8,16,2,32,128]{5,4,3,2,1,0:T(8,128)} fusion(f32[1,8,16,2,32,128]{5,4,3,2,1,0:T(8,128)} %broadcast_in_dim.3, s32[]{:T(128)S(6)} %select_n.21, f32[16,2,2,32,128]{4,3,2,1,0:T(8,128)} %all-to-all-done), kind=kLoop, calls=%fused_computation.9 | loop fusion | bytes 1048580 | tf_op jit(solution)/shard_map/dynamic_update_slice | solution.py:663
  136.2 1.9 %fusion.3 = f32[1,8,16,2,32,128]{5,4,3,2,1,0:T(8,128)} fusion(f32[1,8,16,2,32,128]{5,4,3,2,1,0:T(8,128)} %fusion.4, s32[]{:T(128)S(6)} %select_n.22, f32[16,2,2,32,128]{4,3,2,1,0:T(8,128)} %all-to-all-done), kind=kLoop, calls=%fused_computation.7 | loop fusion | bytes 1048580 | tf_op jit(solution)/shard_map/dynamic_update_slice | solution.py:663
  140.5 27.4 %all-to-all-done.2.piece = f32[16,3,2,32,128]{4,3,2,1,0:T(8,128)S(1)} async-done(((f32[16,3,2,32,128]{4,3,2,1,0:T(8,128)}), f32[16,3,2,32,128]{4,3,2,1,0:T(8,128)S(1)}, u32[]{:S(2)}, u32[]{:S(2)}) %all-to-all-start.2) | async-done | bytes 1572896 | tf_op jit(solution)/shard_map/all_to_all | solution.py:659
  (44 shorter events, 19.2 us)
Async XLA Ops:
  3.3 6.0 %copy-start.5 = (f32[1,1536]{1,0:T(1,128)}, f32[1,1536]{1,0:T(1,128)S(1)}, u32[]{:S(2)}) copy-start(f32[1,1536]{1,0:T(1,128)S(1)} %get-tuple-element.46.values) | copy-start | bytes 18436
  3.3 6.0 %copy-start.6 = (s32[1,512]{1,0:T(1,128)}, s32[1,512]{1,0:T(1,128)S(1)}, u32[]{:S(2)}) copy-start(s32[1,512]{1,0:T(1,128)S(1)} %get-tuple-element.45.positions) | copy-start | bytes 6148
  3.4 9.4 %collective-permute-start.2 = (f32[4,32,8,128]{3,2,1,0:T(8,128)}, f32[4,32,8,128]{3,2,1,0:T(8,128)S(1)}, u32[]{:S(2)}, u32[]{:S(2)}) collective-permute-start(f32[4,32,8,128]{3,2,1,0:T(8,128)} %get-tuple-element.43), channel_id=1, source_target_pairs={{0,1},{1,0},{2,3},{3,2},{4,5},{5,4},{6,7},{7,6},{8,9},{9,8},{10,11... | collective-permute-start | bytes 1572872 | tf_op jit(solution)/shard_map/ppermute | solution.py:522
  4.1 8.7 %collective-permute-start.3 = (f32[4,32,8,128]{3,2,1,0:T(8,128)}, f32[4,32,8,128]{3,2,1,0:T(8,128)S(1)}, u32[]{:S(2)}, u32[]{:S(2)}) collective-permute-start(f32[4,32,8,128]{3,2,1,0:T(8,128)} %get-tuple-element.44), channel_id=1, source_target_pairs={{1,2},{2,1},{5,6},{6,5},{9,10},{10,9},{13,14},{14,13},{17,18},{18,... | collective-permute-start | bytes 1572872 | tf_op jit(solution)/shard_map/ppermute | solution.py:522
  4.8 17.1 %collective-permute-start = (f32[34,32,128]{2,1,0:T(8,128)}, f32[34,32,128]{2,1,0:T(8,128)S(1)}, u32[]{:S(2)}, u32[]{:S(2)}) collective-permute-start(f32[34,32,128]{2,1,0:T(8,128)} %get-tuple-element.41), channel_id=1, source_target_pairs={{0,4},{4,0},{8,12},{12,8},{1,5},{5,1},{9,13},{13,9},{2,6},{6,2},{1... | collective-permute-start | bytes 1671176 | tf_op jit(solution)/shard_map/ppermute | solution.py:521
  5.0 16.9 %collective-permute-start.1 = (f32[34,32,128]{2,1,0:T(8,128)}, f32[34,32,128]{2,1,0:T(8,128)S(1)}, u32[]{:S(2)}, u32[]{:S(2)}) collective-permute-start(f32[34,32,128]{2,1,0:T(8,128)} %get-tuple-element.42), channel_id=1, source_target_pairs={{4,8},{8,4},{5,9},{9,5},{6,10},{10,6},{7,11},{11,7},{20,24},{24,20... | collective-permute-start | bytes 1671176 | tf_op jit(solution)/shard_map/ppermute | solution.py:521
  9.4 6.3 %copy-start.1 = (s32[16,16]{1,0:T(8,128)S(1)}, s32[16,16]{1,0:T(8,128)}, u32[]{:S(2)}) copy-start(s32[16,16]{1,0:T(8,128)} %owner.19) | copy-start | bytes 3076
  9.4 6.3 %copy-start.2 = (s32[1,8]{1,0:T(1,128)S(1)}, s32[1,8]{1,0:T(1,128)}, u32[]{:S(2)}) copy-start(s32[1,8]{1,0:T(1,128)} %aperture.7) | copy-start | bytes 100
  9.4 6.3 %copy-start.3 = (f32[1,3]{1,0:T(1,128)S(1)}, f32[1,3]{1,0:T(1,128)}, u32[]{:S(2)}) copy-start(f32[1,3]{1,0:T(1,128)} %amps.3) | copy-start | bytes 40
  13.0 8.9 %collective-permute-start.4 = (f32[2,4,6,8,128]{4,3,2,1,0:T(8,128)S(1)}, f32[2,4,6,8,128]{4,3,2,1,0:T(8,128)S(1)}, u32[]{:S(2)}, u32[]{:S(2)}) collective-permute-start(f32[2,4,6,8,128]{4,3,2,1,0:T(8,128)S(1)} %get-tuple-element.48), channel_id=1, source_target_pairs={{0,4},{4,0},{8,12},{12,8},{1,5},{5,1},{9,13},{13,9},{2,6},{6,2},{1... | collective-permute-start | bytes 589832 | tf_op jit(solution)/shard_map/ppermute | solution.py:551
  13.1 11.5 %collective-permute-start.5 = (f32[2,4,6,8,128]{4,3,2,1,0:T(8,128)S(1)}, f32[2,4,6,8,128]{4,3,2,1,0:T(8,128)S(1)}, u32[]{:S(2)}, u32[]{:S(2)}) collective-permute-start(f32[2,4,6,8,128]{4,3,2,1,0:T(8,128)S(1)} %get-tuple-element.49), channel_id=1, source_target_pairs={{4,8},{8,4},{5,9},{9,5},{6,10},{10,6},{7,11},{11,7},{20,24},{24,20... | collective-permute-start | bytes 589832 | tf_op jit(solution)/shard_map/ppermute | solution.py:551
  20.6 16.4 %collective-permute-start.7 = (f32[8,2,2,32,128]{4,3,2,1,0:T(8,128)S(1)}, f32[8,2,2,32,128]{4,3,2,1,0:T(8,128)S(1)}, u32[]{:S(2)}, u32[]{:S(2)}) collective-permute-start(f32[8,2,2,32,128]{4,3,2,1,0:T(8,128)S(1)} %get-tuple-element.63), channel_id=1, source_target_pairs={{0,16},{16,0},{1,17},{17,1},{2,18},{18,2},{3,19},{19,3},{4,20},{20... | collective-permute-start | bytes 1572872 | tf_op jit(solution)/shard_map/ppermute | solution.py:614
  28.9 14.1 %collective-permute-start.6 = (f32[8,2,2,32,128]{4,3,2,1,0:T(8,128)S(1)}, f32[8,2,2,32,128]{4,3,2,1,0:T(8,128)S(1)}, u32[]{:S(2)}, u32[]{:S(2)}) collective-permute-start(f32[8,2,2,32,128]{4,3,2,1,0:T(8,128)S(1)} %get-tuple-element.61), channel_id=1, source_target_pairs={{0,16},{16,0},{1,17},{17,1},{2,18},{18,2},{3,19},{19,3},{4,20},{20... | collective-permute-start | bytes 1572872 | tf_op jit(solution)/shard_map/ppermute | solution.py:614
  30.2 15.6 %collective-permute-start.8 = (f32[24,32,128]{2,1,0:T(8,128)S(1)}, f32[24,32,128]{2,1,0:T(8,128)S(1)}, u32[]{:S(2)}, u32[]{:S(2)}) collective-permute-start(f32[24,32,128]{2,1,0:T(8,128)S(1)} %get-tuple-element.64), channel_id=1, source_target_pairs={{0,4},{4,0},{8,12},{12,8},{1,5},{5,1},{9,13},{13,9},{2,6},{6,2},{1... | collective-permute-start | bytes 1179656 | tf_op jit(solution)/shard_map/ppermute | solution.py:588
  30.2 15.6 %collective-permute-start.9 = (f32[24,32,128]{2,1,0:T(8,128)S(1)}, f32[24,32,128]{2,1,0:T(8,128)S(1)}, u32[]{:S(2)}, u32[]{:S(2)}) collective-permute-start(f32[24,32,128]{2,1,0:T(8,128)S(1)} %get-tuple-element.65), channel_id=1, source_target_pairs={{4,8},{8,4},{5,9},{9,5},{6,10},{10,6},{7,11},{11,7},{20,24},{24,20... | collective-permute-start | bytes 1179656 | tf_op jit(solution)/shard_map/ppermute | solution.py:588
  43.0 16.0 %collective-permute-start.10 = (f32[8,3,2,32,128]{4,3,2,1,0:T(8,128)}, f32[8,3,2,32,128]{4,3,2,1,0:T(8,128)S(1)}, u32[]{:S(2)}, u32[]{:S(2)}) collective-permute-start(f32[8,3,2,32,128]{4,3,2,1,0:T(8,128)} %get-tuple-element.70), channel_id=1, source_target_pairs={{0,16},{16,0},{1,17},{17,1},{2,18},{18,2},{3,19},{19,3},{4,20},{20... | collective-permute-start | bytes 2359304 | tf_op jit(solution)/shard_map/ppermute | solution.py:614
  49.4 26.6 %collective-permute-start.11 = (f32[8,3,2,32,128]{4,3,2,1,0:T(8,128)}, f32[8,3,2,32,128]{4,3,2,1,0:T(8,128)S(1)}, u32[]{:S(2)}, u32[]{:S(2)}) collective-permute-start(f32[8,3,2,32,128]{4,3,2,1,0:T(8,128)} %get-tuple-element.71), channel_id=1, source_target_pairs={{0,16},{16,0},{1,17},{17,1},{2,18},{18,2},{3,19},{19,3},{4,20},{20... | collective-permute-start | bytes 2359304 | tf_op jit(solution)/shard_map/ppermute | solution.py:614
  49.7 33.9 %all-to-all-start = ((f32[16,2,2,32,128]{4,3,2,1,0:T(8,128)}), f32[16,2,2,32,128]{4,3,2,1,0:T(8,128)}, u32[]{:S(2)}, u32[]{:S(2)}) async-start(f32[16,2,2,32,128]{4,3,2,1,0:T(8,128)} %sum_near.3.rest_5_), calls=%async_computation | async-start | bytes 2097152 | tf_op jit(solution)/shard_map/all_to_all | solution.py:659
  76.0 16.0 %collective-permute-start.13 = (f32[8,3,2,32,128]{4,3,2,1,0:T(8,128)}, f32[8,3,2,32,128]{4,3,2,1,0:T(8,128)S(1)}, u32[]{:S(2)}, u32[]{:S(2)}) collective-permute-start(f32[8,3,2,32,128]{4,3,2,1,0:T(8,128)} %get-tuple-element.78), channel_id=1, source_target_pairs={{0,16},{16,0},{1,17},{17,1},{2,18},{18,2},{3,19},{19,3},{4,20},{20... | collective-permute-start | bytes 2359304 | tf_op jit(solution)/shard_map/ppermute | solution.py:614
  77.2 14.8 %copy-start.4 = (f32[8,3,2,32,128]{4,3,2,1,0:T(8,128)S(1)}, f32[8,3,2,32,128]{4,3,2,1,0:T(8,128)}, u32[]{:S(2)}) copy-start(f32[8,3,2,32,128]{4,3,2,1,0:T(8,128)} %get-tuple-element.77.refs_0_) | copy-start | bytes 2359300
  83.5 43.3 %all-to-all-start.1 = ((f32[16,3,2,32,128]{4,3,2,1,0:T(8,128)}), f32[16,3,2,32,128]{4,3,2,1,0:T(8,128)S(1)}, u32[]{:S(2)}, u32[]{:S(2)}) async-start(f32[16,3,2,32,128]{4,3,2,1,0:T(8,128)} %sum_near.4), calls=%async_computation.1 | async-start | bytes 3145728 | tf_op jit(solution)/shard_map/all_to_all | solution.py:659
  90.6 19.8 %collective-permute-start.12 = (f32[8,3,2,32,128]{4,3,2,1,0:T(8,128)}, f32[8,3,2,32,128]{4,3,2,1,0:T(8,128)S(1)}, u32[]{:S(2)}, u32[]{:S(2)}) collective-permute-start(f32[8,3,2,32,128]{4,3,2,1,0:T(8,128)} %get-tuple-element.76), channel_id=1, source_target_pairs={{0,16},{16,0},{1,17},{17,1},{2,18},{18,2},{3,19},{19,3},{4,20},{20... | collective-permute-start | bytes 2359304 | tf_op jit(solution)/shard_map/ppermute | solution.py:614
  92.0 18.5 %copy-start = (f32[8,3,2,32,128]{4,3,2,1,0:T(8,128)S(1)}, f32[8,3,2,32,128]{4,3,2,1,0:T(8,128)}, u32[]{:S(2)}) copy-start(f32[8,3,2,32,128]{4,3,2,1,0:T(8,128)} %get-tuple-element.75.refs_0_) | copy-start | bytes 2359300
  126.8 41.1 %all-to-all-start.2 = ((f32[16,3,2,32,128]{4,3,2,1,0:T(8,128)}), f32[16,3,2,32,128]{4,3,2,1,0:T(8,128)S(1)}, u32[]{:S(2)}, u32[]{:S(2)}) async-start(f32[16,3,2,32,128]{4,3,2,1,0:T(8,128)} %sum_near.5), calls=%async_computation.2 | async-start | bytes 3145728 | tf_op jit(solution)/shard_map/all_to_all | solution.py:659
